TPU v7x, 32 devices: a whole 2x2x4 slice. The times are simulated.
32 devices in a mesh: lon: 8 (over y, x, core), lat: 4 (over z).
Axes of the slice: x: 2, y: 2, z: 4, core: 2. Of those that a mesh axis runs over, the one named last changes fastest.
Arguments:
- vel_base: bfloat16 [8, 4, 8, 16, 2, 128], P('lon', 'lat'), may hold values from -1.25 to 1.25
- vel_grad: bfloat16 [8, 4, 8, 16, 4, 128], P('lon', 'lat'), may hold values from -0.29882812 to 0.29882812
- route_dev: int32 [8, 4, 8, 128, 1], P('lon', 'lat'), may hold values from 0 to 31; in each aligned block of 128 rows (0 to 127, 128 to 255, ..., all dimensions but the last counted through in order) at most 8 rows name the same one
- route_block: int32 [8, 4, 8, 128], P('lon', 'lat'), may hold values from 0 to 15
- seed_cells: int32 [8, 2048, 1024], P(None, 'lat', 'lon'), may hold values from 0 to 127
Outputs:
- flow_map: float32 [2, 2048, 1024], P(None, 'lat', 'lon')
- ftle_field: float32 [2048, 1024], P('lat', 'lon')
Inputs may be any that keep to these rules, and one draw needn't show every extreme that they name: `route_dev`: in each step, at most 8 of the 128 seed groups of one device name the same owner; in some steps of some devices an owner is named by exactly 8 groups.
All inputs are finite; a program needn't handle non-finite values.
Results may differ from a plain program's by a relative error of at most 0.0003.
Values may be sent and summed in bfloat16 or wider, within the bound.
No kernel may reach another device: no remote copies, remote signals or barrier semaphores. Data moves between devices by JAX's collectives and lax.ppermute only.
A program may use at most 64 MiB of HBM per device.

v0:
```python
import math

import jax
import jax.numpy as jnp
from jax import lax
from jax.sharding import PartitionSpec as P

GROUP_ROWS = 4


def extended(block, sides, width):
    for axis, dim in sides:
        count = lax.axis_size(axis)
        forward = [(i, i + 1) for i in range(count - 1)]
        forward.append((count - 1, 0))
        backward = [(target, source) for source, target in forward]
        low = lax.ppermute(
            lax.slice_in_dim(block, block.shape[dim] - width, None, axis=dim), axis, forward
        )
        high = lax.ppermute(lax.slice_in_dim(block, 0, width, axis=dim), axis, backward)
        block = jnp.concatenate([low, block, high], axis=dim)
    return block


def velocity_rate(eastward_component, along_y, coeffs):
    vel_x, vel_y, grad_xx, grad_xy, grad_yx, grad_yy = coeffs
    return (
        -(vel_x + grad_xx * eastward_component + grad_xy * along_y),
        -(vel_y + grad_yx * eastward_component + grad_yy * along_y),
    )


def runge_kutta(eastward_component, along_y, coeffs, dt_step):
    half_step = 0.5 * dt_step
    rate_one = velocity_rate(eastward_component, along_y, coeffs)
    rate_two = velocity_rate(
        eastward_component + half_step * rate_one[0], along_y + half_step * rate_one[1], coeffs
    )
    rate_three = velocity_rate(
        eastward_component + half_step * rate_two[0], along_y + half_step * rate_two[1], coeffs
    )
    rate_four = velocity_rate(
        eastward_component + dt_step * rate_three[0], along_y + dt_step * rate_three[1], coeffs
    )
    sixth = dt_step / 6.0
    new_x = eastward_component + sixth * (
        rate_one[0] + 2.0 * rate_two[0] + 2.0 * rate_three[0] + rate_four[0]
    )
    new_y = along_y + sixth * (rate_one[1] + 2.0 * rate_two[1] + 2.0 * rate_three[1] + rate_four[1])
    return (new_x, new_y)


def stretch_rate(diff_lon, diff_lat):
    map_xx = 1.0 + diff_lon[0]
    map_xy = diff_lat[0]
    map_yx = diff_lon[1]
    map_yy = 1.0 + diff_lat[1]
    green_xx = map_xx * map_xx + map_yx * map_yx
    green_yy = map_xy * map_xy + map_yy * map_yy
    green_xy = map_xx * map_xy + map_yx * map_yy
    half_diff = 0.5 * (green_xx - green_yy)
    largest = 0.5 * (green_xx + green_yy) + jnp.sqrt(half_diff * half_diff + green_xy * green_xy)
    return 0.5 * jnp.log(largest)


def route_requests(pending_requests):
    return lax.all_to_all(pending_requests, ("lon", "lat"), split_axis=0, concat_axis=0, tiled=True)


def route_replies(replies):
    return lax.all_to_all(replies, ("lon", "lat"), split_axis=0, concat_axis=0, tiled=True)


def fetch_blocks(vel_table, owners, needed_blocks, first_step, step_count, devices, capacity):
    owner_ids = owners[first_step : first_step + step_count]
    block_ids = needed_blocks[first_step : first_step + step_count]
    num_groups = owner_ids.shape[1]
    position = jnp.arange(num_groups, dtype=jnp.int32)
    matches = (owner_ids[:, :, None] == owner_ids[:, None, :]) & (
        position[None, None, :] < position[None, :, None]
    )
    slot_rank = jnp.sum(matches.astype(jnp.int32), axis=2)
    step_of = jnp.broadcast_to(jnp.arange(step_count, dtype=jnp.int32)[:, None], owner_ids.shape)
    pending_requests = (
        jnp.zeros((devices, step_count, capacity), jnp.int32)
        .at[owner_ids, step_of, slot_rank]
        .set(block_ids)
    )
    received = route_requests(pending_requests)
    step_pick = jnp.arange(step_count, dtype=jnp.int32)[None, :, None] + first_step
    chosen = vel_table[step_pick, received]
    replies = route_replies(chosen)
    return replies[owner_ids, step_of, slot_rank]


def select_cells(blocks, cell_numbers):
    num_groups, components, block_cells = blocks.shape
    group_size = cell_numbers.shape[1]
    batch_size = math.gcd(num_groups, 32)
    batched_blocks = blocks.reshape(num_groups // batch_size, batch_size, components, block_cells)
    batched_cells = cell_numbers.reshape(num_groups // batch_size, batch_size, group_size)

    def single_batch(operands):
        block_portion, cell_part = operands
        indicator_matrix = (
            cell_part[:, :, None] == lax.iota(jnp.int32, block_cells)[None, None, :]
        ).astype(jnp.bfloat16)
        return jnp.einsum(
            "dox,dlx->dol", block_portion, indicator_matrix, preferred_element_type=jnp.float32
        )

    picked = lax.map(single_batch, (batched_blocks, batched_cells))
    return picked.reshape(num_groups, components, group_size)


def body(vel_base, vel_grad, route_dev, route_block, seed_cells):
    n_lon = lax.axis_size("lon")
    n_lat = lax.axis_size("lat")
    devices = n_lon * n_lat
    num_steps, seed_lat, seed_lon = seed_cells.shape
    lat_groups = seed_lat // GROUP_ROWS
    lon_groups = seed_lon // 128
    num_groups = lat_groups * lon_groups
    capacity = max(2, 2 * num_groups // devices)
    group_size = GROUP_ROWS * 128
    vel_table = jnp.concatenate([vel_base[0, 0], vel_grad[0, 0]], axis=2)
    group_cells = seed_cells.reshape(num_steps, lat_groups, GROUP_ROWS, lon_groups, 128)
    group_cells = jnp.transpose(group_cells, (0, 1, 3, 2, 4)).reshape(
        num_steps, num_groups, group_size
    )
    owners = route_dev[0, 0, :, :, 0]
    needed_blocks = route_block[0, 0]
    dt_step = 1.0 / num_steps
    eastward_component = jnp.zeros((num_groups, group_size), jnp.float32)
    along_y = jnp.zeros((num_groups, group_size), jnp.float32)
    for step_index in range(num_steps):
        blocks = fetch_blocks(vel_table, owners, needed_blocks, step_index, 1, devices, capacity)[0]
        values = select_cells(blocks, group_cells[step_index])
        coeffs = tuple((values[:, component] for component in range(6)))
        eastward_component, along_y = runge_kutta(eastward_component, along_y, coeffs, dt_step)
    stacked = jnp.stack([eastward_component, along_y], axis=1)
    field_grid = stacked.reshape(lat_groups, lon_groups, 2, GROUP_ROWS, 128)
    field_grid = jnp.transpose(field_grid, (2, 0, 3, 1, 4)).reshape(2, seed_lat, seed_lon)
    padded = extended(field_grid, (("lon", 2), ("lat", 1)), 1)
    lat_index = lax.axis_index("lat")
    south_row = jnp.where(lat_index == 0, padded[:, 1:2, 1:-1], padded[:, 0:1, 1:-1])
    north_row = jnp.where(lat_index == n_lat - 1, padded[:, -2:-1, 1:-1], padded[:, -1:, 1:-1])
    diff_lon = (padded[:, 1:-1, 2:] - padded[:, 1:-1, :-2]) * 0.5
    lat_rows = jnp.concatenate([south_row, field_grid, north_row], axis=1)
    diff_lat = (lat_rows[:, 2:] - lat_rows[:, :-2]) * 0.5
    return (field_grid, stretch_rate(diff_lon, diff_lat))


def solution(mesh):
    in_specs = (
        P("lon", "lat", None, None, None, None),
        P("lon", "lat", None, None, None, None),
        P("lon", "lat", None, None, None),
        P("lon", "lat", None, None),
        P(None, "lat", "lon"),
    )
    out_specs = (P(None, "lat", "lon"), P("lat", "lon"))
    return jax.shard_map(body, mesh=mesh, in_specs=in_specs, out_specs=out_specs, check_vma=False)
```

profile of v0, /device:TPU:0, one launch (start us, length us, event | category | flops | bytes accessed | tf_op | source)
XLA Modules:
  0.0 471.4 jit_solution(10315182436324278291)
XLA Ops:
  4.0 6.4 %scatter_fusion = s32[32,8]{0,1:T(8,128)S(1)} fusion(s32[32,8]{0,1:T(8,128)S(1)} %broadcast.1317.clone.4, s32[128]{0:T(128)S(1)} %get-tuple-element.341, s32[128]{0:T(128)S(1)} %get-tuple-element.316), kind=kCustom, calls=%fused_computation.16 | custom fusion | bytes 2560 | tf_op jit(solution)/shard_map/scatter | solution.py:87
  11.1 7.3 %all-to-all-start = ((s32[32,1,8]{2,1,0:T(1,128)}), s32[32,1,8]{2,1,0:T(1,128)S(1)}, u32[]{:S(2)}, u32[]{:S(2)}) async-start(s32[32,1,8]{2,1,0:T(1,128)} %copy.219), calls=%async_computation | async-start | bytes 32768 | tf_op jit(solution)/shard_map/all_to_all | solution.py:67
  20.2 6.4 %scatter_fusion.1 = s32[32,8]{0,1:T(8,128)S(1)} fusion(s32[32,8]{0,1:T(8,128)S(1)} %broadcast.1317.clone.3, s32[128]{0:T(128)S(1)} %get-tuple-element.343, s32[128]{0:T(128)S(1)} %get-tuple-element.315), kind=kCustom, calls=%fused_computation.17 | custom fusion | bytes 2560 | tf_op jit(solution)/shard_map/scatter | solution.py:87
  27.4 6.4 %scatter_fusion.3 = s32[32,8]{0,1:T(8,128)S(1)} fusion(s32[32,8]{0,1:T(8,128)S(1)} %broadcast.1317.clone.2, s32[128]{0:T(128)S(1)} %get-tuple-element.345, s32[128]{0:T(128)S(1)} %get-tuple-element.313), kind=kCustom, calls=%fused_computation.19 | custom fusion | bytes 2560 | tf_op jit(solution)/shard_map/scatter | solution.py:87
  35.5 6.4 %scatter_fusion.2 = s32[32,8]{0,1:T(8,128)S(1)} fusion(s32[32,8]{0,1:T(8,128)S(1)} %broadcast.1317.clone.5, s32[128]{0:T(128)S(1)} %get-tuple-element.339, s32[128]{0:T(128)S(1)} %get-tuple-element.314), kind=kCustom, calls=%fused_computation.18 | custom fusion | bytes 2560 | tf_op jit(solution)/shard_map/scatter | solution.py:87
  43.4 6.4 %scatter_fusion.5 = s32[32,8]{0,1:T(8,128)S(1)} fusion(s32[32,8]{0,1:T(8,128)S(1)} %broadcast.1317.clone.1, s32[128]{0:T(128)S(1)} %get-tuple-element.347, s32[128]{0:T(128)S(1)} %get-tuple-element.311), kind=kCustom, calls=%fused_computation.21 | custom fusion | bytes 2560 | tf_op jit(solution)/shard_map/scatter | solution.py:87
  51.2 6.4 %scatter_fusion.4 = s32[32,8]{0,1:T(8,128)S(1)} fusion(s32[32,8]{0,1:T(8,128)S(1)} %broadcast.1317.clone.6, s32[128]{0:T(128)S(1)} %get-tuple-element.337, s32[128]{0:T(128)S(1)} %get-tuple-element.312), kind=kCustom, calls=%fused_computation.20 | custom fusion | bytes 2560 | tf_op jit(solution)/shard_map/scatter | solution.py:87
  59.1 6.4 %scatter_fusion.7 = s32[32,8]{0,1:T(8,128)S(1)} fusion(s32[32,8]{0,1:T(8,128)S(1)} %broadcast.1317.clone, s32[128]{0:T(128)S(1)} %get-tuple-element.349, s32[128]{0:T(128)S(1)} %get-tuple-element.317), kind=kCustom, calls=%fused_computation.23 | custom fusion | bytes 2560 | tf_op jit(solution)/shard_map/scatter | solution.py:87
  67.0 6.4 %scatter_fusion.6 = s32[32,8]{0,1:T(8,128)S(1)} fusion(s32[32,8]{0,1:T(8,128)S(1)} %broadcast.1317.clone.7, s32[128]{0:T(128)S(1)} %get-tuple-element.335, s32[128]{0:T(128)S(1)} %get-tuple-element.310), kind=kCustom, calls=%fused_computation.22 | custom fusion | bytes 2560 | tf_op jit(solution)/shard_map/scatter | solution.py:87
  74.1 5.8 %all-to-all-start.2 = ((s32[32,1,8]{2,1,0:T(1,128)}), s32[32,1,8]{2,1,0:T(1,128)S(1)}, u32[]{:S(2)}, u32[]{:S(2)}) async-start(s32[32,1,8]{2,1,0:T(1,128)} %copy.228), calls=%async_computation.2 | async-start | bytes 32768 | tf_op jit(solution)/shard_map/all_to_all | solution.py:67
  80.1 7.1 %all-to-all-done.2 = s32[32,1,8]{2,1,0:T(1,128)S(1)} async-done(((s32[32,1,8]{2,1,0:T(1,128)}), s32[32,1,8]{2,1,0:T(1,128)S(1)}, u32[]{:S(2)}, u32[]{:S(2)}) %all-to-all-start.2) | async-done | bytes 1056 | tf_op jit(solution)/shard_map/all_to_all | solution.py:67
  89.7 7.1 %all-to-all-done.6 = s32[32,1,8]{2,1,0:T(1,128)S(1)} async-done(((s32[32,1,8]{2,1,0:T(1,128)}), s32[32,1,8]{2,1,0:T(1,128)S(1)}, u32[]{:S(2)}, u32[]{:S(2)}) %all-to-all-start.6) | async-done | bytes 1056 | tf_op jit(solution)/shard_map/all_to_all | solution.py:67
  99.4 7.1 %all-to-all-done.4 = s32[32,1,8]{2,1,0:T(1,128)S(1)} async-done(((s32[32,1,8]{2,1,0:T(1,128)}), s32[32,1,8]{2,1,0:T(1,128)S(1)}, u32[]{:S(2)}, u32[]{:S(2)}) %all-to-all-start.4) | async-done | bytes 1056 | tf_op jit(solution)/shard_map/all_to_all | solution.py:67
  109.1 7.1 %all-to-all-done.10 = s32[32,1,8]{2,1,0:T(1,128)S(1)} async-done(((s32[32,1,8]{2,1,0:T(1,128)}), s32[32,1,8]{2,1,0:T(1,128)S(1)}, u32[]{:S(2)}, u32[]{:S(2)}) %all-to-all-start.10) | async-done | bytes 1056 | tf_op jit(solution)/shard_map/all_to_all | solution.py:67
  118.7 7.1 %all-to-all-done.8 = s32[32,1,8]{2,1,0:T(1,128)S(1)} async-done(((s32[32,1,8]{2,1,0:T(1,128)}), s32[32,1,8]{2,1,0:T(1,128)S(1)}, u32[]{:S(2)}, u32[]{:S(2)}) %all-to-all-start.8) | async-done | bytes 1056 | tf_op jit(solution)/shard_map/all_to_all | solution.py:67
  128.5 7.1 %all-to-all-done.14 = s32[32,1,8]{2,1,0:T(1,128)S(1)} async-done(((s32[32,1,8]{2,1,0:T(1,128)}), s32[32,1,8]{2,1,0:T(1,128)S(1)}, u32[]{:S(2)}, u32[]{:S(2)}) %all-to-all-start.14) | async-done | bytes 1056 | tf_op jit(solution)/shard_map/all_to_all | solution.py:67
  160.3 7.7 %all-to-all-done.1 = bf16[32,1,8,6,128]{4,2,3,1,0:T(8,128)(2,1)S(1)} async-done(((bf16[32,1,8,6,128]{4,2,3,1,0:T(8,128)(2,1)}), bf16[32,1,8,6,128]{4,2,3,1,0:T(8,128)(2,1)S(1)}, u32[]{:S(2)}, u32[]{:S(2)}) %all-to-all-start.1) | async-done | bytes 393248 | tf_op jit(solution)/shard_map/all_to_all | solution.py:71
  173.0 22.2 %while.80 = (s32[]{:T(128)}, f32[4,32,6,512]{3,1,0,2:T(8,128)S(1)}, bf16[4,32,6,128]{3,2,1,0:T(8,128)(2,1)S(1)}, s32[4,32,512]{2,1,0:T(8,128)S(1)}, s32[]{:T(128)}) while((s32[]{:T(128)}, f32[4,32,6,512]{3,1,0,2:T(8,128)S(1)}, bf16[4,32,6,128]{3,2,1,0:T(8,128)(2,1)S(1)}, s32[4,32,512]{2,1,0:T(8,128)S(1)}, s32[]{:T(128)}) %tuple.204), condition=%wide.region_3.4_spmd, body=%wide.region_2.3_spmd.sunk | while | flops 27262976 | bytes 1572937 | solution.py:112
  195.2 5.8 %all-to-all-start.7 = ((bf16[32,1,8,6,128]{4,2,3,1,0:T(8,128)(2,1)}), bf16[32,1,8,6,128]{4,2,3,1,0:T(8,128)(2,1)S(1)}, u32[]{:S(2)}, u32[]{:S(2)}) async-start(bf16[32,1,8,6,128]{4,2,3,1,0:T(8,128)(2,1)} %copy.249), calls=%async_computation.7 | async-start | bytes 786432 | tf_op jit(solution)/shard_map/all_to_all | solution.py:71
  204.1 22.2 %while.81 = (s32[]{:T(128)}, f32[4,32,6,512]{3,1,0,2:T(8,128)S(1)}, bf16[4,32,6,128]{3,2,1,0:T(8,128)(2,1)S(1)}, s32[4,32,512]{2,1,0:T(8,128)S(1)}, s32[]{:T(128)}) while((s32[]{:T(128)}, f32[4,32,6,512]{3,1,0,2:T(8,128)S(1)}, bf16[4,32,6,128]{3,2,1,0:T(8,128)(2,1)S(1)}, s32[4,32,512]{2,1,0:T(8,128)S(1)}, s32[]{:T(128)}) %tuple.205), condition=%wide.region_7.8_spmd, body=%wide.region_6.7_spmd.sunk | while | flops 27262976 | bytes 1572937 | solution.py:112
  226.3 6.0 %all-to-all-start.5 = ((bf16[32,1,8,6,128]{4,2,3,1,0:T(8,128)(2,1)}), bf16[32,1,8,6,128]{4,2,3,1,0:T(8,128)(2,1)}, u32[]{:S(2)}, u32[]{:S(2)}) async-start(bf16[32,1,8,6,128]{4,2,3,1,0:T(8,128)(2,1)} %copy.241), calls=%async_computation.5 | async-start | bytes 786432 | tf_op jit(solution)/shard_map/all_to_all | solution.py:71
  234.1 24.8 %while.83 = (s32[]{:T(128)}, f32[4,32,6,512]{3,1,0,2:T(8,128)S(1)}, bf16[4,32,6,128]{3,2,1,0:T(8,128)(2,1)}, s32[4,32,512]{2,1,0:T(8,128)}, s32[]{:T(128)}) while((s32[]{:T(128)}, f32[4,32,6,512]{3,1,0,2:T(8,128)S(1)}, bf16[4,32,6,128]{3,2,1,0:T(8,128)(2,1)}, s32[4,32,512]{2,1,0:T(8,128)}, s32[]{:T(128)}) %tuple.206), condition=%wide.region_15.16_spmd, body=%wide.region_14.15_spmd.sunk | while | flops 27262976 | bytes 1573445 | solution.py:112
  259.0 5.9 %all-to-all-start.11 = ((bf16[32,1,8,6,128]{4,2,3,1,0:T(8,128)(2,1)}), bf16[32,1,8,6,128]{4,2,3,1,0:T(8,128)(2,1)}, u32[]{:S(2)}, u32[]{:S(2)}) async-start(bf16[32,1,8,6,128]{4,2,3,1,0:T(8,128)(2,1)} %copy.265), calls=%async_computation.11 | async-start | bytes 786432 | tf_op jit(solution)/shard_map/all_to_all | solution.py:71
  270.8 27.7 %while.82 = (s32[]{:T(128)}, f32[4,32,6,512]{3,1,0,2:T(8,128)}, bf16[4,32,6,128]{3,2,1,0:T(8,128)(2,1)}, s32[4,32,512]{2,1,0:T(8,128)}, s32[]{:T(128)}) while((s32[]{:T(128)}, f32[4,32,6,512]{3,1,0,2:T(8,128)}, bf16[4,32,6,128]{3,2,1,0:T(8,128)(2,1)}, s32[4,32,512]{2,1,0:T(8,128)}, s32[]{:T(128)}) %tuple.207), condition=%wide.region_11.12_spmd, body=%wide.region_10.11_spmd.sunk | while | flops 27262976 | bytes 1442881 | solution.py:112
  298.5 6.1 %all-to-all-start.9 = ((bf16[32,1,8,6,128]{4,2,3,1,0:T(8,128)(2,1)}), bf16[32,1,8,6,128]{4,2,3,1,0:T(8,128)(2,1)}, u32[]{:S(2)}, u32[]{:S(2)}) async-start(bf16[32,1,8,6,128]{4,2,3,1,0:T(8,128)(2,1)} %copy.257), calls=%async_computation.9 | async-start | bytes 786432 | tf_op jit(solution)/shard_map/all_to_all | solution.py:71
  307.5 24.8 %while.85 = (s32[]{:T(128)}, f32[4,32,6,512]{3,1,0,2:T(8,128)S(1)}, bf16[4,32,6,128]{3,2,1,0:T(8,128)(2,1)}, s32[4,32,512]{2,1,0:T(8,128)}, s32[]{:T(128)}) while((s32[]{:T(128)}, f32[4,32,6,512]{3,1,0,2:T(8,128)S(1)}, bf16[4,32,6,128]{3,2,1,0:T(8,128)(2,1)}, s32[4,32,512]{2,1,0:T(8,128)}, s32[]{:T(128)}) %tuple.208), condition=%wide.region_23.24_spmd, body=%wide.region_22.23_spmd.sunk | while | flops 27262976 | bytes 1573445 | solution.py:112
  332.3 5.7 %all-to-all-start.15 = ((bf16[32,1,8,6,128]{4,2,3,1,0:T(8,128)(2,1)}), bf16[32,1,8,6,128]{4,2,3,1,0:T(8,128)(2,1)}, u32[]{:S(2)}, u32[]{:S(2)}) async-start(bf16[32,1,8,6,128]{4,2,3,1,0:T(8,128)(2,1)} %copy.281), calls=%async_computation.15 | async-start | bytes 786432 | tf_op jit(solution)/shard_map/all_to_all | solution.py:71
  343.9 27.7 %while.84 = (s32[]{:T(128)}, f32[4,32,6,512]{3,1,0,2:T(8,128)}, bf16[4,32,6,128]{3,2,1,0:T(8,128)(2,1)}, s32[4,32,512]{2,1,0:T(8,128)}, s32[]{:T(128)}) while((s32[]{:T(128)}, f32[4,32,6,512]{3,1,0,2:T(8,128)}, bf16[4,32,6,128]{3,2,1,0:T(8,128)(2,1)}, s32[4,32,512]{2,1,0:T(8,128)}, s32[]{:T(128)}) %tuple.209), condition=%wide.region_19.20_spmd, body=%wide.region_18.19_spmd.sunk | while | flops 27262976 | bytes 1442881 | solution.py:112
  371.6 5.9 %all-to-all-start.13 = ((bf16[32,1,8,6,128]{4,2,3,1,0:T(8,128)(2,1)}), bf16[32,1,8,6,128]{4,2,3,1,0:T(8,128)(2,1)}, u32[]{:S(2)}, u32[]{:S(2)}) async-start(bf16[32,1,8,6,128]{4,2,3,1,0:T(8,128)(2,1)} %copy.273), calls=%async_computation.13 | async-start | bytes 786432 | tf_op jit(solution)/shard_map/all_to_all | solution.py:71
  380.4 24.8 %while.87 = (s32[]{:T(128)}, f32[4,32,6,512]{3,1,0,2:T(8,128)S(1)}, bf16[4,32,6,128]{3,2,1,0:T(8,128)(2,1)}, s32[4,32,512]{2,1,0:T(8,128)}, s32[]{:T(128)}) while((s32[]{:T(128)}, f32[4,32,6,512]{3,1,0,2:T(8,128)S(1)}, bf16[4,32,6,128]{3,2,1,0:T(8,128)(2,1)}, s32[4,32,512]{2,1,0:T(8,128)}, s32[]{:T(128)}) %tuple.210), condition=%wide.region_31.32_spmd, body=%wide.region_30.31_spmd.sunk | while | flops 27262976 | bytes 1573445 | solution.py:112
  411.1 24.5 %while.86 = (s32[]{:T(128)}, f32[4,32,6,512]{3,1,0,2:T(8,128)}, bf16[4,32,6,128]{3,2,1,0:T(8,128)(2,1)}, s32[4,32,512]{2,1,0:T(8,128)S(1)}, s32[]{:T(128)}) while((s32[]{:T(128)}, f32[4,32,6,512]{3,1,0,2:T(8,128)}, bf16[4,32,6,128]{3,2,1,0:T(8,128)(2,1)}, s32[4,32,512]{2,1,0:T(8,128)S(1)}, s32[]{:T(128)}) %tuple.203), condition=%wide.region_27.28_spmd, body=%wide.region_26.27_spmd.sunk | while | flops 27262976 | bytes 1442881 | solution.py:112
  447.6 11.2 %collective-permute-done = f32[2,512,1]{2,1,0:T(8,128)S(1)} collective-permute-done((f32[2,512,1]{2,1,0:T(8,128)S(1)}, f32[2,512,1]{2,1,0:T(8,128)S(1)}, u32[]{:S(2)}, u32[]{:S(2)}) %collective-permute-start) | collective-permute-done | bytes 4128 | tf_op jit(solution)/shard_map/ppermute | solution.py:20
  (279 shorter events, 308.0 us)
Async XLA Ops:
  11.1 63.0 %all-to-all-start = ((s32[32,1,8]{2,1,0:T(1,128)}), s32[32,1,8]{2,1,0:T(1,128)S(1)}, u32[]{:S(2)}, u32[]{:S(2)}) async-start(s32[32,1,8]{2,1,0:T(1,128)} %copy.219), calls=%async_computation | async-start | bytes 32768 | tf_op jit(solution)/shard_map/all_to_all | solution.py:67
  20.2 15.2 %copy-start.8 = (bf16[1,1,8,16,4,128]{5,4,3,2,1,0:T(4,128)(2,1)S(1)}, bf16[1,1,8,16,4,128]{5,4,3,2,1,0:T(4,128)(2,1)}, u32[]{:S(2)}) copy-start(bf16[1,1,8,16,4,128]{5,4,3,2,1,0:T(4,128)(2,1)} %param.22) | copy-start | bytes 393220
  20.2 15.2 %copy-start.9 = (bf16[1,1,8,16,2,128]{5,4,3,2,1,0:T(2,128)(2,1)S(1)}, bf16[1,1,8,16,2,128]{5,4,3,2,1,0:T(2,128)(2,1)}, u32[]{:S(2)}) copy-start(bf16[1,1,8,16,2,128]{5,4,3,2,1,0:T(2,128)(2,1)} %param.21) | copy-start | bytes 196612
  74.1 13.0 %all-to-all-start.2 = ((s32[32,1,8]{2,1,0:T(1,128)}), s32[32,1,8]{2,1,0:T(1,128)S(1)}, u32[]{:S(2)}, u32[]{:S(2)}) async-start(s32[32,1,8]{2,1,0:T(1,128)} %copy.228), calls=%async_computation.2 | async-start | bytes 32768 | tf_op jit(solution)/shard_map/all_to_all | solution.py:67
  87.2 9.7 %all-to-all-start.6 = ((s32[32,1,8]{2,1,0:T(1,128)}), s32[32,1,8]{2,1,0:T(1,128)S(1)}, u32[]{:S(2)}, u32[]{:S(2)}) async-start(s32[32,1,8]{2,1,0:T(1,128)} %copy.244), calls=%async_computation.6 | async-start | bytes 32768 | tf_op jit(solution)/shard_map/all_to_all | solution.py:67
  96.8 9.7 %all-to-all-start.4 = ((s32[32,1,8]{2,1,0:T(1,128)}), s32[32,1,8]{2,1,0:T(1,128)S(1)}, u32[]{:S(2)}, u32[]{:S(2)}) async-start(s32[32,1,8]{2,1,0:T(1,128)} %copy.236), calls=%async_computation.4 | async-start | bytes 32768 | tf_op jit(solution)/shard_map/all_to_all | solution.py:67
  106.5 9.6 %all-to-all-start.10 = ((s32[32,1,8]{2,1,0:T(1,128)}), s32[32,1,8]{2,1,0:T(1,128)S(1)}, u32[]{:S(2)}, u32[]{:S(2)}) async-start(s32[32,1,8]{2,1,0:T(1,128)} %copy.260), calls=%async_computation.10 | async-start | bytes 32768 | tf_op jit(solution)/shard_map/all_to_all | solution.py:67
  116.2 9.7 %all-to-all-start.8 = ((s32[32,1,8]{2,1,0:T(1,128)}), s32[32,1,8]{2,1,0:T(1,128)S(1)}, u32[]{:S(2)}, u32[]{:S(2)}) async-start(s32[32,1,8]{2,1,0:T(1,128)} %copy.252), calls=%async_computation.8 | async-start | bytes 32768 | tf_op jit(solution)/shard_map/all_to_all | solution.py:67
  125.9 9.6 %all-to-all-start.14 = ((s32[32,1,8]{2,1,0:T(1,128)}), s32[32,1,8]{2,1,0:T(1,128)S(1)}, u32[]{:S(2)}, u32[]{:S(2)}) async-start(s32[32,1,8]{2,1,0:T(1,128)} %copy.276), calls=%async_computation.14 | async-start | bytes 32768 | tf_op jit(solution)/shard_map/all_to_all | solution.py:67
  135.5 14.9 %all-to-all-start.12 = ((s32[32,1,8]{2,1,0:T(1,128)}), s32[32,1,8]{2,1,0:T(1,128)S(1)}, u32[]{:S(2)}, u32[]{:S(2)}) async-start(s32[32,1,8]{2,1,0:T(1,128)} %copy.268), calls=%async_computation.12 | async-start | bytes 32768 | tf_op jit(solution)/shard_map/all_to_all | solution.py:67
  150.4 17.5 %all-to-all-start.1 = ((bf16[32,1,8,6,128]{4,2,3,1,0:T(8,128)(2,1)}), bf16[32,1,8,6,128]{4,2,3,1,0:T(8,128)(2,1)S(1)}, u32[]{:S(2)}, u32[]{:S(2)}) async-start(bf16[32,1,8,6,128]{4,2,3,1,0:T(8,128)(2,1)} %copy.225), calls=%async_computation.1 | async-start | bytes 786432 | tf_op jit(solution)/shard_map/all_to_all | solution.py:71
  167.9 27.3 %all-to-all-start.3 = ((bf16[32,1,8,6,128]{4,2,3,1,0:T(8,128)(2,1)}), bf16[32,1,8,6,128]{4,2,3,1,0:T(8,128)(2,1)S(1)}, u32[]{:S(2)}, u32[]{:S(2)}) async-start(bf16[32,1,8,6,128]{4,2,3,1,0:T(8,128)(2,1)} %copy.233), calls=%async_computation.3 | async-start | bytes 786432 | tf_op jit(solution)/shard_map/all_to_all | solution.py:71
  195.2 8.7 %copy-start.5 = (f32[4,32,6,512]{3,1,0,2:T(8,128)}, f32[4,32,6,512]{3,1,0,2:T(8,128)S(1)}, u32[]{:S(2)}) copy-start(f32[4,32,6,512]{3,1,0,2:T(8,128)S(1)} %get-tuple-element.178) | copy-start | bytes 4718596
  195.2 31.1 %all-to-all-start.7 = ((bf16[32,1,8,6,128]{4,2,3,1,0:T(8,128)(2,1)}), bf16[32,1,8,6,128]{4,2,3,1,0:T(8,128)(2,1)S(1)}, u32[]{:S(2)}, u32[]{:S(2)}) async-start(bf16[32,1,8,6,128]{4,2,3,1,0:T(8,128)(2,1)} %copy.249), calls=%async_computation.7 | async-start | bytes 786432 | tf_op jit(solution)/shard_map/all_to_all | solution.py:71
  226.3 32.7 %all-to-all-start.5 = ((bf16[32,1,8,6,128]{4,2,3,1,0:T(8,128)(2,1)}), bf16[32,1,8,6,128]{4,2,3,1,0:T(8,128)(2,1)}, u32[]{:S(2)}, u32[]{:S(2)}) async-start(bf16[32,1,8,6,128]{4,2,3,1,0:T(8,128)(2,1)} %copy.241), calls=%async_computation.5 | async-start | bytes 786432 | tf_op jit(solution)/shard_map/all_to_all | solution.py:71
  258.9 11.9 %copy-start = (f32[4,32,6,512]{3,1,0,2:T(8,128)}, f32[4,32,6,512]{3,1,0,2:T(8,128)S(1)}, u32[]{:S(2)}) copy-start(f32[4,32,6,512]{3,1,0,2:T(8,128)S(1)} %get-tuple-element.181) | copy-start | bytes 4718596
  259.0 39.5 %all-to-all-start.11 = ((bf16[32,1,8,6,128]{4,2,3,1,0:T(8,128)(2,1)}), bf16[32,1,8,6,128]{4,2,3,1,0:T(8,128)(2,1)}, u32[]{:S(2)}, u32[]{:S(2)}) async-start(bf16[32,1,8,6,128]{4,2,3,1,0:T(8,128)(2,1)} %copy.265), calls=%async_computation.11 | async-start | bytes 786432 | tf_op jit(solution)/shard_map/all_to_all | solution.py:71
  298.5 33.8 %all-to-all-start.9 = ((bf16[32,1,8,6,128]{4,2,3,1,0:T(8,128)(2,1)}), bf16[32,1,8,6,128]{4,2,3,1,0:T(8,128)(2,1)}, u32[]{:S(2)}, u32[]{:S(2)}) async-start(bf16[32,1,8,6,128]{4,2,3,1,0:T(8,128)(2,1)} %copy.257), calls=%async_computation.9 | async-start | bytes 786432 | tf_op jit(solution)/shard_map/all_to_all | solution.py:71
  332.3 11.6 %copy-start.2 = (f32[4,32,6,512]{3,1,0,2:T(8,128)}, f32[4,32,6,512]{3,1,0,2:T(8,128)S(1)}, u32[]{:S(2)}) copy-start(f32[4,32,6,512]{3,1,0,2:T(8,128)S(1)} %get-tuple-element.183) | copy-start | bytes 4718596
  332.3 39.3 %all-to-all-start.15 = ((bf16[32,1,8,6,128]{4,2,3,1,0:T(8,128)(2,1)}), bf16[32,1,8,6,128]{4,2,3,1,0:T(8,128)(2,1)}, u32[]{:S(2)}, u32[]{:S(2)}) async-start(bf16[32,1,8,6,128]{4,2,3,1,0:T(8,128)(2,1)} %copy.281), calls=%async_computation.15 | async-start | bytes 786432 | tf_op jit(solution)/shard_map/all_to_all | solution.py:71
  371.6 33.6 %all-to-all-start.13 = ((bf16[32,1,8,6,128]{4,2,3,1,0:T(8,128)(2,1)}), bf16[32,1,8,6,128]{4,2,3,1,0:T(8,128)(2,1)}, u32[]{:S(2)}, u32[]{:S(2)}) async-start(bf16[32,1,8,6,128]{4,2,3,1,0:T(8,128)(2,1)} %copy.273), calls=%async_computation.13 | async-start | bytes 786432 | tf_op jit(solution)/shard_map/all_to_all | solution.py:71
  435.6 2.4 copy-start.1
  435.6 2.5 copy-start.6
  438.1 1.5 copy-start.3
  438.1 1.9 copy-start.7
  445.0 24.9 %copy-start.4 = (f32[128,1,2,4,128]{4,3,0,2,1:T(4,128)}, f32[128,1,2,4,128]{4,3,0,2,1:T(4,128)S(1)}, u32[]{:S(2)}) copy-start(f32[128,1,2,4,128]{4,3,0,2,1:T(4,128)S(1)} %pad_maximum_fusion.4) | copy-start | bytes 1572868
  445.2 13.6 %collective-permute-start = (f32[2,512,1]{2,1,0:T(8,128)S(1)}, f32[2,512,1]{2,1,0:T(8,128)S(1)}, u32[]{:S(2)}, u32[]{:S(2)}) collective-permute-start(f32[2,512,1]{2,1,0:T(8,128)S(1)} %get-tuple-element.309), channel_id=1, source_target_pairs={{4,0},{8,4},{12,8},{16,12},{20,16},{24,20},{28,24},{0,28},{5,1},{9... | collective-permute-start | bytes 12296 | tf_op jit(solution)/shard_map/ppermute | solution.py:20
  447.6 13.3 %collective-permute-start.1 = (f32[2,512,1]{2,1,0:T(8,128)S(1)}, f32[2,512,1]{2,1,0:T(8,128)S(1)}, u32[]{:S(2)}, u32[]{:S(2)}) collective-permute-start(f32[2,512,1]{2,1,0:T(8,128)S(1)} %get-tuple-element.308), channel_id=1, source_target_pairs={{0,4},{4,8},{8,12},{12,16},{16,20},{20,24},{24,28},{28,0},{1,5},{5... | collective-permute-start | bytes 12296 | tf_op jit(solution)/shard_map/ppermute | solution.py:17
  461.0 4.7 collective-permute-start.2
  464.4 5.4 %collective-permute-start.3 = (f32[2,1,130]{2,1,0:T(1,128)S(1)}, f32[2,1,130]{2,1,0:T(1,128)S(1)}, u32[]{:S(2)}, u32[]{:S(2)}) collective-permute-start(f32[2,1,130]{2,1,0:T(1,128)S(1)} %get-tuple-element.303), channel_id=1, source_target_pairs={{0,1},{1,2},{2,3},{3,0},{4,5},{5,6},{6,7},{7,4},{8,9},{9,10},{10,1... | collective-permute-start | bytes 3128 | tf_op jit(solution)/shard_map/ppermute | solution.py:17
where the time goes:
time: 480 us; the launch traced here: 471 us
  matrix products  164 us (34%)
  local copies, waits for them, and re-layouts  145 us (30%)
  starting transfers between devices  79.2 us (16%)
  waiting for transfers between devices  68.9 us (14%)
  other arithmetic  12.3 us (3%)
    dot_general x32, matrix products, single_batch(): jnp.einsum('dox,dlx->dol', block_portion, indicator_matrix, preferred_ele...  164 us
    scatter x16, local copies, waits for them, and re-layouts, fetch_blocks(): pending_requests = jnp.zeros((devices, step_count, capacity), jnp.int32)....  56.8 us
    all_to_all x8, starting transfers between devices, route_replies(): lax.all_to_all(replies, ('lon', 'lat'), split_axis=0, concat_axis=0, tile...  44.9 us
    all_to_all x8, waiting for transfers between devices, route_requests(): lax.all_to_all(pending_requests, ('lon', 'lat'), split_axis=0, concat_axi...  42.5 us
    all_to_all x8, starting transfers between devices, route_requests(): lax.all_to_all(pending_requests, ('lon', 'lat'), split_axis=0, concat_axi...  28.5 us
    dynamic_update_slice x32, local copies, waits for them, and re-layouts, select_cells(): picked = lax.map(single_batch, (batched_blocks, batched_cells))  17.3 us
    eq x32, local copies, waits for them, and re-layouts, single_batch(): cell_part[:, :, None] == lax.iota(jnp.int32, block_cells)[None, None, :]  17.1 us
    gather x16, local copies, waits for them, and re-layouts, fetch_blocks(): chosen = vel_table[step_pick, received]  15.5 us
  transfers between devices with their start and end apart: 20, of which 11 were waited for; matrix products, arithmetic and copies ran while one was open for 57% of the time, Pallas kernels for 0%

commit v1 on v0

v1 whole, which is shorter than its diff:
```python
import functools

import jax
import jax.numpy as jnp
from jax import lax
from jax.experimental import pallas as pl
from jax.experimental.pallas import tpu as pltpu
from jax.sharding import PartitionSpec as P

GROUP_ROWS = 4
LANES = 128
SPLIT = 4


def swap(value, axis, masks):
    count = lax.axis_size(axis)
    pairs = [(i, i ^ masks[i % len(masks)]) for i in range(count)]
    return lax.ppermute(value, axis, pairs)


def plane_masks(n_lon):
    bits = []
    mask = 2
    while mask < n_lon:
        bits.append(mask)
        mask *= 2
    return bits, bits[::-1]


def plane_gather(shard):
    even, odd = plane_masks(lax.axis_size("lon"))
    held = shard[None]
    for even_mask, odd_mask in zip(even, odd):
        held = jnp.concatenate([held, swap(held, "lon", (even_mask, odd_mask))], axis=0)
    return held


def slot_of(owners, n_lat):
    lon, lat = lax.axis_index("lon"), lax.axis_index("lat")
    even, odd = plane_masks(lax.axis_size("lon"))
    owner_lon, owner_lat = owners // n_lat, owners % n_lat
    family = (owner_lon ^ lon) & 1
    base = lon ^ family
    parity = base & 1
    apart = owner_lon ^ base
    place = jnp.zeros_like(owners)
    for position, (even_mask, odd_mask) in enumerate(zip(even, odd)):
        mask = jnp.where(parity == 0, even_mask, odd_mask)
        place = place + jnp.where((apart & mask) != 0, 1 << position, 0)
    return (family * n_lat + (owner_lat ^ lat)) * (1 << len(even)) + place


def advance(along_x, along_y, coeffs):
    vel_x, vel_y, xx, xy, yx, yy = coeffs
    half_x = vel_x + xx * along_x + xy * along_y
    half_y = vel_y + yx * along_x + yy * along_y
    full_x = half_x + half_x
    full_y = half_y + half_y
    third_x = full_x + (xx * half_x + xy * half_y)
    third_y = full_y + (yx * half_x + yy * half_y)
    ratio = 2.0 / 3.0
    second_x = full_x + ratio * (xx * third_x + xy * third_y)
    second_y = full_y + ratio * (yx * third_x + yy * third_y)
    new_x = along_x + (full_x + (xx * second_x + xy * second_y))
    new_y = along_y + (full_y + (yx * second_x + yy * second_y))
    return new_x, new_y


def steps_kernel(first, scale, piece_steps, n_pieces, has_start, unroll, *refs):
    base_ref, grad_ref, cells_ref = refs[:3]
    pieces = refs[3 : 3 + n_pieces]
    start_ref = refs[3 + n_pieces] if has_start else None
    out_ref, table = refs[-2:]
    steps, rows, lanes = cells_ref.shape
    places, _, step_rows, _ = pieces[0].shape
    for number, piece in enumerate(pieces):

        def widen(place, carry, number=number, piece=piece):
            for step in range(steps):
                row = ((number * places + place) * steps + step) * step_rows
                row = pl.multiple_of(row, step_rows)
                source = piece[place, piece_steps[number] + step]
                table[pl.ds(row, step_rows), :] = source.astype(jnp.float32) * scale
            return carry

        lax.fori_loop(0, places, widen, 0)
    upper = lax.broadcasted_iota(jnp.int32, (8, lanes), 0) < GROUP_ROWS

    def tile(number):
        row = pl.multiple_of(number * 8, 8)
        if has_start:
            along_x = start_ref[0, pl.ds(row, 8), :]
            along_y = start_ref[1, pl.ds(row, 8), :]
        else:
            along_x = jnp.zeros((8, lanes), jnp.float32)
            along_y = jnp.zeros((8, lanes), jnp.float32)
        for step in range(steps):
            index = cells_ref[step, pl.ds(row, 8), :]
            one, two = 2 * number, 2 * number + 1
            sources = [
                (base_ref[first + step, one] + k, base_ref[first + step, two] + k) for k in range(2)
            ]
            sources += [
                (grad_ref[first + step, one] + k, grad_ref[first + step, two] + k) for k in range(4)
            ]
            coeffs = []
            for above, below in sources:
                values = jnp.where(
                    upper,
                    jnp.broadcast_to(table[pl.ds(above, 1), :], (8, lanes)),
                    jnp.broadcast_to(table[pl.ds(below, 1), :], (8, lanes)),
                )
                coeffs.append(
                    jnp.take_along_axis(values, index, axis=1, mode="promise_in_bounds")
                )
            along_x, along_y = advance(along_x, along_y, coeffs)
        out_ref[0, pl.ds(row, 8), :] = along_x
        out_ref[1, pl.ds(row, 8), :] = along_y

    def tiles(number, carry):
        for inner in range(unroll):
            tile(number * unroll + inner)
        return carry

    lax.fori_loop(0, rows // 8 // unroll, tiles, 0)


def run_steps(first, last, scale, base, grad, cells, pieces, piece_steps, start):
    steps = last - first
    _, rows, lanes = cells.shape
    places, _, step_rows, _ = pieces[0].shape
    table_rows = len(pieces) * places * steps * step_rows
    vmem = pl.BlockSpec(memory_space=pltpu.VMEM)
    smem = pl.BlockSpec(memory_space=pltpu.SMEM)
    operands = [base, grad, cells[first:last], *pieces] + ([start] if start is not None else [])
    need = table_rows * lanes * 4 + sum(value.size * value.dtype.itemsize for value in operands)
    need += 2 * rows * lanes * 4
    return pl.pallas_call(
        functools.partial(
            steps_kernel, first, scale, piece_steps, len(pieces), start is not None, 8
        ),
        out_shape=jax.ShapeDtypeStruct((2, rows, lanes), jnp.float32),
        in_specs=[smem, smem] + [vmem] * (len(operands) - 2),
        out_specs=vmem,
        scratch_shapes=[pltpu.VMEM((table_rows, lanes), jnp.float32)],
        compiler_params=pltpu.CompilerParams(vmem_limit_bytes=need + (4 << 20)),
        name=f"rk_steps_{first}",
    )(*operands)


def stretch_rate(diff_lon, diff_lat):
    map_xx = 1.0 + diff_lon[0]
    map_xy = diff_lat[0]
    map_yx = diff_lon[1]
    map_yy = 1.0 + diff_lat[1]
    green_xx = map_xx * map_xx + map_yx * map_yx
    green_yy = map_xy * map_xy + map_yy * map_yy
    green_xy = map_xx * map_xy + map_yx * map_yy
    half_diff = 0.5 * (green_xx - green_yy)
    largest = 0.5 * (green_xx + green_yy) + jnp.sqrt(half_diff * half_diff + green_xy * green_xy)
    return 0.5 * jnp.log(largest)


def shifted(value, axis, by):
    count = lax.axis_size(axis)
    return lax.ppermute(value, axis, [(i, (i + by) % count) for i in range(count)])


def body(vel_base, vel_grad, route_dev, route_block, seed_cells):
    n_lon, n_lat = lax.axis_size("lon"), lax.axis_size("lat")
    num_steps, rows, lanes = seed_cells.shape
    blocks = vel_base.shape[3]
    shard = jnp.concatenate(
        [
            vel_base.reshape(num_steps, 2 * blocks, lanes),
            vel_grad.reshape(num_steps, 4 * blocks, lanes),
        ],
        axis=1,
    )
    step_rows = shard.shape[1]
    spans = [(0, SPLIT), (SPLIT, num_steps)]
    rounds = []
    for apart in range(n_lat):
        if apart < n_lat - 1:
            parts = [(0, num_steps)]
        else:
            parts = spans
        for begin, end in parts:
            piece = shard[begin:end]
            if apart:
                piece = swap(piece, "lat", (apart,))
            mine = plane_gather(piece)
            other = swap(mine, "lon", (1,))
            rounds.append((apart, begin, end, mine, other))
    owners = route_dev[0, 0, :, :, 0]
    slots = slot_of(owners, n_lat)
    scale = -0.5 / num_steps
    flow = None
    for first, last in spans:
        chosen = [item for item in rounds if item[1] <= first and last <= item[2]]
        pieces = [item[3] for item in chosen] + [item[4] for item in chosen]
        piece_steps = tuple([first - item[1] for item in chosen] * 2)
        local = jnp.arange(num_steps, dtype=jnp.int32)[:, None] - first
        row = (slots * (last - first) + local) * step_rows
        base = row + 2 * route_block[0, 0]
        grad = row + 2 * blocks + 4 * route_block[0, 0]
        flow = run_steps(
            first, last, scale, base, grad, seed_cells, pieces, piece_steps, flow
        )
    west = shifted(flow[:, :, -1], "lon", 1)
    east = shifted(flow[:, :, 0], "lon", -1)
    south = shifted(flow[:, -1:, :], "lat", 1)
    north = shifted(flow[:, :1, :], "lat", -1)
    lat_index = lax.axis_index("lat")
    south = jnp.where(lat_index == 0, flow[:, :1, :], south)
    north = jnp.where(lat_index == n_lat - 1, flow[:, -1:, :], north)
    right = jnp.concatenate([flow[:, :, 1:], east[:, :, None]], axis=2)
    left = jnp.concatenate([west[:, :, None], flow[:, :, :-1]], axis=2)
    diff_lon = (right - left) * 0.5
    lat_rows = jnp.concatenate([south, flow, north], axis=1)
    diff_lat = (lat_rows[:, 2:] - lat_rows[:, :-2]) * 0.5
    return (flow, stretch_rate(diff_lon, diff_lat))


def solution(mesh):
    in_specs = (
        P("lon", "lat", None, None, None, None),
        P("lon", "lat", None, None, None, None),
        P("lon", "lat", None, None, None),
        P("lon", "lat", None, None),
        P(None, "lat", "lon"),
    )
    out_specs = (P(None, "lat", "lon"), P("lat", "lon"))
    return jax.shard_map(body, mesh=mesh, in_specs=in_specs, out_specs=out_specs, check_vma=False)
```

time: 480 us -> 71.8 us (0.15); the launches traced: 471 us -> 71.4 us
  matrix products: 164 us -> 0 us
  local copies, waits for them, and re-layouts: 145 us -> 4.12 us
  waiting for transfers between devices: 68.9 us -> 18.7 us
  starting transfers between devices: 79.2 us -> 31 us
  Pallas kernels: 0 us -> 11.4 us
  other arithmetic: 12.3 us -> 5.33 us
    dot_general x32 -> x0, matrix products: 164 us -> none  [single_batch(): jnp.einsum('dox,dlx->dol', block_portion, indicator_matrix, preferred_ele...]
    all_to_all x16 -> x0, starting transfers between devices: 73.4 us -> none  [the longest x8 44.9 us: route_replies(): lax.all_to_all(replies, ('lon', 'lat'), split_axis=0, concat_axis=0, tile...]
    scatter x16 -> x0, local copies, waits for them, and re-layouts: 56.8 us -> none  [fetch_blocks(): pending_requests = jnp.zeros((devices, step_count, capacity), jnp.int32)....]
    all_to_all x16 -> x0, waiting for transfers between devices: 50.2 us -> none  [the longest x8 42.5 us: route_requests(): lax.all_to_all(pending_requests, ('lon', 'lat'), split_axis=0, concat_axi...]
    gather x24 -> x0, local copies, waits for them, and re-layouts: 30.8 us -> none  [the longest x16 15.5 us: fetch_blocks(): chosen = vel_table[step_pick, received]]
    ppermute x4 -> x23, starting transfers between devices: 5.81 us -> 31 us  [the longest x19 24.2 us: swap(): return lax.ppermute(value, axis, pairs)]
    eq x33 -> x0, local copies, waits for them, and re-layouts: 17.8 us -> none  [the longest x32 17.1 us: single_batch(): cell_part[:, :, None] == lax.iota(jnp.int32, block_cells)[None, None, :]]
    dynamic_update_slice x32 -> x0, local copies, waits for them, and re-layouts: 17.3 us -> none  [select_cells(): picked = lax.map(single_batch, (batched_blocks, batched_cells))]
  transfers between devices with their start and end apart: 20 -> 23, of which waited for: 11 -> 8; matrix products, arithmetic and copies ran while one was open for 57% -> 8% of each run, Pallas kernels for 0% -> 8%
where the time goes in v1:
time: 71.8 us; the launch traced here: 71.4 us
  starting transfers between devices  31 us (43%)
  waiting for transfers between devices  18.7 us (26%)
  Pallas kernels  11.4 us (16%)
  other arithmetic  5.33 us (7%)
  local copies, waits for them, and re-layouts  4.12 us (6%)
  between operations  0.83 us (1%)
    ppermute x19, starting transfers between devices, swap(): return lax.ppermute(value, axis, pairs)  24.2 us
    ppermute x19, waiting for transfers between devices, swap(): return lax.ppermute(value, axis, pairs)  15.1 us
    pallas_call x2, Pallas kernels, run_steps(): pl.pallas_call(functools.partial(steps_kernel, first, scale, piece_steps,...  11.4 us
    ppermute x4, starting transfers between devices, shifted(): lax.ppermute(value, axis, [(i, (i + by) % count) for i in range(count)])  6.86 us
    ppermute x4, waiting for transfers between devices, shifted(): lax.ppermute(value, axis, [(i, (i + by) % count) for i in range(count)])  3.57 us
    concatenate x2, other arithmetic, body(): jnp.concatenate([vel_base.reshape(num_steps, 2 * blocks, lanes), vel_grad...  1.89 us
    slice x1, local copies, waits for them, and re-layouts, run_steps(): cells[first:last]  1.69 us
    slice x1, local copies, waits for them, and re-layouts, body(): left = jnp.concatenate([west[:, :, None], flow[:, :, :-1]], axis=2)  1.46 us
  transfers between devices with their start and end apart: 23, of which 8 were waited for; matrix products, arithmetic and copies ran while one was open for 8% of the time, Pallas kernels for 8%

profile of v1, /device:TPU:0, one launch (start us, length us, event | category | flops | bytes accessed | tf_op | source)
XLA Modules:
  0.0 71.4 jit_solution(3536390268350392923)
XLA Ops:
  0.6 1.0 %pad_maximum_fusion.10 = (bf16[8,96,128]{2,1,0:T(8,128)(2,1)S(1)}, bf16[1,8,96,128]{3,2,1,0:T(8,128)(2,1)S(1)}) fusion(bf16[8,32,128]{2,1,0:T(8,128)(2,1)} %bitcast.33, bf16[8,64,128]{2,1,0:T(8,128)(2,1)} %bitcast.25), kind=kLoop, calls=%fused_computation.18 | loop fusion | flops 393216 | bytes 589824 | tf_op jit(solution)/shard_map/concatenate | solution.py:173
  1.6 3.1 %collective-permute-start.2 = (bf16[8,96,128]{2,1,0:T(8,128)(2,1)S(1)}, bf16[8,96,128]{2,1,0:T(8,128)(2,1)S(1)}, u32[]{:S(2)}, u32[]{:S(2)}) collective-permute-start(bf16[8,96,128]{2,1,0:T(8,128)(2,1)S(1)} %get-tuple-element.16), channel_id=1, source_target_pairs={{0,1},{1,0},{2,3},{3,2},{4,5},{5,4},{6,7},{7,6},{8,9},{9,8},{10,11... | collective-permute-start | bytes 589832 | tf_op jit(solution)/shard_map/ppermute | solution.py:18
  4.7 2.6 %collective-permute-start.5 = (bf16[8,96,128]{2,1,0:T(8,128)(2,1)S(1)}, bf16[8,96,128]{2,1,0:T(8,128)(2,1)S(1)}, u32[]{:S(2)}, u32[]{:S(2)}) collective-permute-start(bf16[8,96,128]{2,1,0:T(8,128)(2,1)S(1)} %get-tuple-element.16), channel_id=1, source_target_pairs={{0,2},{1,3},{2,0},{3,1},{4,6},{5,7},{6,4},{7,5},{8,10},{9,11},{10,... | collective-permute-start | bytes 589832 | tf_op jit(solution)/shard_map/ppermute | solution.py:18
  7.3 1.5 %collective-permute-start = (bf16[1,8,96,128]{3,2,1,0:T(8,128)(2,1)S(1)}, bf16[1,8,96,128]{3,2,1,0:T(8,128)(2,1)S(1)}, u32[]{:S(2)}, u32[]{:S(2)}) collective-permute-start(bf16[1,8,96,128]{3,2,1,0:T(8,128)(2,1)S(1)} %get-tuple-element.17), channel_id=1, source_target_pairs={{0,8},{4,20},{8,0},{12,28},{16,24},{20,4},{24,16},{28,12},{1,9},{5... | collective-permute-start | bytes 589832 | tf_op jit(solution)/shard_map/ppermute | solution.py:18
  8.8 0.9 %fusion.4 = (bf16[4,96,128]{2,1,0:T(8,128)(2,1)S(1)}, bf16[4,96,128]{2,1,0:T(8,128)(2,1)S(1)}) fusion(bf16[8,64,128]{2,1,0:T(8,128)(2,1)} %bitcast.26, bf16[8,32,128]{2,1,0:T(8,128)(2,1)} %bitcast.34), kind=kLoop, calls=%fused_computation.27 | loop fusion | flops 393216 | bytes 393216 | tf_op jit(solution)/shard_map/concatenate | solution.py:173
  10.0 3.6 %collective-permute-start.8 = (bf16[4,96,128]{2,1,0:T(8,128)(2,1)S(1)}, bf16[4,96,128]{2,1,0:T(8,128)(2,1)S(1)}, u32[]{:S(2)}, u32[]{:S(2)}) collective-permute-start(bf16[4,96,128]{2,1,0:T(8,128)(2,1)S(1)} %get-tuple-element.15), channel_id=1, source_target_pairs={{0,3},{1,2},{2,1},{3,0},{4,7},{5,6},{6,5},{7,4},{8,11},{9,10},{10,... | collective-permute-start | bytes 294920 | tf_op jit(solution)/shard_map/ppermute | solution.py:18
  13.6 1.3 %collective-permute-start.3 = (bf16[1,8,96,128]{3,2,1,0:T(8,128)(2,1)S(1)}, bf16[1,8,96,128]{3,2,1,0:T(8,128)(2,1)S(1)}, u32[]{:S(2)}, u32[]{:S(2)}) collective-permute-start(bf16[1,8,96,128]{3,2,1,0:T(8,128)(2,1)S(1)} %bitcast.22), channel_id=1, source_target_pairs={{0,8},{4,20},{8,0},{12,28},{16,24},{20,4},{24,16},{28,12},{1,9},{5... | collective-permute-start | bytes 589832 | tf_op jit(solution)/shard_map/ppermute | solution.py:18
  14.9 0.7 %bitcast_add_fusion = (s32[8,128]{1,0:T(8,128)S(1)}, s32[8,128]{1,0:T(8,128)S(1)}) fusion(s32[1,1,8,128]{3,2,1,0:T(8,128)} %param.8, s32[]{:T(128)S(6)} %axis_index.29, s32[]{:T(128)S(6)} %axis_index.27, s32[8,128]{1,0:T(8,128)} %bitcast.37), kind=kLoop, calls=%fused_computation.38 | loop fusion | flops 46080 | bytes 16392 | tf_op jit(solution)/shard_map/add | solution.py:206
  15.7 3.6 %collective-permute-done.15 = bf16[4,96,128]{2,1,0:T(8,128)(2,1)S(1)} collective-permute-done((bf16[4,96,128]{2,1,0:T(8,128)(2,1)S(1)}, bf16[4,96,128]{2,1,0:T(8,128)(2,1)S(1)}, u32[]{:S(2)}, u32[]{:S(2)}) %collective-permute-start.15) | collective-permute-done | bytes 98336 | tf_op jit(solution)/shard_map/ppermute | solution.py:18
  19.3 1.5 %collective-permute-start.16 = (bf16[1,4,96,128]{3,2,1,0:T(8,128)(2,1)S(1)}, bf16[1,4,96,128]{3,2,1,0:T(8,128)(2,1)S(1)}, u32[]{:S(2)}, u32[]{:S(2)}) collective-permute-start(bf16[1,4,96,128]{3,2,1,0:T(8,128)(2,1)S(1)} %bitcast.30), channel_id=1, source_target_pairs={{0,8},{4,20},{8,0},{12,28},{16,24},{20,4},{24,16},{28,12},{1,9},{5... | collective-permute-start | bytes 294920 | tf_op jit(solution)/shard_map/ppermute | solution.py:18
  20.8 1.0 %collective-permute-start.9 = (bf16[1,4,96,128]{3,2,1,0:T(8,128)(2,1)S(1)}, bf16[1,4,96,128]{3,2,1,0:T(8,128)(2,1)S(1)}, u32[]{:S(2)}, u32[]{:S(2)}) collective-permute-start(bf16[1,4,96,128]{3,2,1,0:T(8,128)(2,1)S(1)} %bitcast.27), channel_id=1, source_target_pairs={{0,8},{4,20},{8,0},{12,28},{16,24},{20,4},{24,16},{28,12},{1,9},{5... | collective-permute-start | bytes 294920 | tf_op jit(solution)/shard_map/ppermute | solution.py:18
  21.8 1.1 %collective-permute-start.6 = (bf16[1,8,96,128]{3,2,1,0:T(8,128)(2,1)S(1)}, bf16[1,8,96,128]{3,2,1,0:T(8,128)(2,1)S(1)}, u32[]{:S(2)}, u32[]{:S(2)}) collective-permute-start(bf16[1,8,96,128]{3,2,1,0:T(8,128)(2,1)S(1)} %bitcast.19), channel_id=1, source_target_pairs={{0,8},{4,20},{8,0},{12,28},{16,24},{20,4},{24,16},{28,12},{1,9},{5... | collective-permute-start | bytes 589832 | tf_op jit(solution)/shard_map/ppermute | solution.py:18
  23.0 2.0 %collective-permute-start.1 = (bf16[2,8,96,128]{3,2,1,0:T(8,128)(2,1)S(1)}, bf16[2,8,96,128]{3,2,1,0:T(8,128)(2,1)S(1)}, u32[]{:S(2)}, u32[]{:S(2)}) collective-permute-start(bf16[2,8,96,128]{3,2,1,0:T(8,128)(2,1)S(1)} %pad_maximum_fusion.5), channel_id=1, source_target_pairs={{0,16},{4,12},{8,24},{12,4},{16,0},{20,28},{24,8},{28,20},{1,17},{... | collective-permute-start | bytes 1179656 | tf_op jit(solution)/shard_map/ppermute | solution.py:18
  25.2 5.6 %collective-permute-done.6 = bf16[1,8,96,128]{3,2,1,0:T(8,128)(2,1)S(1)} collective-permute-done((bf16[1,8,96,128]{3,2,1,0:T(8,128)(2,1)S(1)}, bf16[1,8,96,128]{3,2,1,0:T(8,128)(2,1)S(1)}, u32[]{:S(2)}, u32[]{:S(2)}) %collective-permute-start.6) | collective-permute-done | bytes 196640 | tf_op jit(solution)/shard_map/ppermute | solution.py:18
  30.8 1.6 %collective-permute-start.7 = (bf16[2,8,96,128]{3,2,1,0:T(8,128)(2,1)S(1)}, bf16[2,8,96,128]{3,2,1,0:T(8,128)(2,1)S(1)}, u32[]{:S(2)}, u32[]{:S(2)}) collective-permute-start(bf16[2,8,96,128]{3,2,1,0:T(8,128)(2,1)S(1)} %pad_maximum_fusion.7), channel_id=1, source_target_pairs={{0,16},{4,12},{8,24},{12,4},{16,0},{20,28},{24,8},{28,20},{1,17},{... | collective-permute-start | bytes 1179656 | tf_op jit(solution)/shard_map/ppermute | solution.py:18
  33.0 1.6 %collective-permute-start.10 = (bf16[2,4,96,128]{3,2,1,0:T(8,128)(2,1)S(1)}, bf16[2,4,96,128]{3,2,1,0:T(8,128)(2,1)S(1)}, u32[]{:S(2)}, u32[]{:S(2)}) collective-permute-start(bf16[2,4,96,128]{3,2,1,0:T(8,128)(2,1)S(1)} %pad_maximum_fusion.11), channel_id=1, source_target_pairs={{0,16},{4,12},{8,24},{12,4},{16,0},{20,28},{24,8},{28,20},{1,17},{... | collective-permute-start | bytes 589832 | tf_op jit(solution)/shard_map/ppermute | solution.py:18
  35.1 0.6 collective-permute-start.12
  35.8 3.5 %collective-permute-done.7 = bf16[2,8,96,128]{3,2,1,0:T(8,128)(2,1)S(1)} collective-permute-done((bf16[2,8,96,128]{3,2,1,0:T(8,128)(2,1)S(1)}, bf16[2,8,96,128]{3,2,1,0:T(8,128)(2,1)S(1)}, u32[]{:S(2)}, u32[]{:S(2)}) %collective-permute-start.7) | collective-permute-done | bytes 393248 | tf_op jit(solution)/shard_map/ppermute | solution.py:18
  39.3 0.6 collective-permute-start.13
  40.0 1.4 %collective-permute-done.17 = bf16[2,4,96,128]{3,2,1,0:T(8,128)(2,1)S(1)} collective-permute-done((bf16[2,4,96,128]{3,2,1,0:T(8,128)(2,1)S(1)}, bf16[2,4,96,128]{3,2,1,0:T(8,128)(2,1)S(1)}, u32[]{:S(2)}, u32[]{:S(2)}) %collective-permute-start.17) | collective-permute-done | bytes 196640 | tf_op jit(solution)/shard_map/ppermute | solution.py:18
  41.4 0.8 %pad_maximum_fusion.9.refs_6_ = bf16[4,4,96,128]{3,2,1,0:T(8,128)(2,1)} fusion(bf16[2,4,96,128]{3,2,1,0:T(8,128)(2,1)S(1)} %collective-permute-done.17, bf16[1,4,96,128]{3,2,1,0:T(8,128)(2,1)S(1)} %collective-permute-done.16, bf16[1,4,96,128]{3,2,1,0:T(8,128)(2,1)S(1)} %bitcast.32), kind=kLoop, calls=%fused_computation.15 | loop fusion | flops 393216 | bytes 786432 | tf_op jit(solution)/shard_map/concatenate | solution.py:34
  42.7 0.8 %collective-permute-done.10 = bf16[2,4,96,128]{3,2,1,0:T(8,128)(2,1)S(1)} collective-permute-done((bf16[2,4,96,128]{3,2,1,0:T(8,128)(2,1)S(1)}, bf16[2,4,96,128]{3,2,1,0:T(8,128)(2,1)S(1)}, u32[]{:S(2)}, u32[]{:S(2)}) %collective-permute-start.10) | collective-permute-done | bytes 196640 | tf_op jit(solution)/shard_map/ppermute | solution.py:18
  43.9 1.7 %fusion.14 = (s32[4,512,128]{2,1,0:T(8,128)S(1)}, s32[4,512,128]{2,1,0:T(8,128)S(1)}) fusion(s32[8,512,128]{2,1,0:T(8,128)} %param.9), kind=kLoop, calls=%fused_computation.55 | loop fusion | bytes 4194304 | tf_op jit(solution)/shard_map/slice | solution.py:135
  45.7 5.4 %rk_steps_0.1.refs_11_ = f32[2,512,128]{2,1,0:T(8,128)S(1)} custom-call(s32[8,128]{1,0:T(8,128)S(1)} %get-tuple-element.20.refs_0_, s32[8,128]{1,0:T(8,128)S(1)} %get-tuple-element.4.refs_1_, s32[4,512,128]{2,1,0:T(8,128)S(1)} %get-tuple-element.6.refs_2_, bf16[4,8,96,128]{3,2,1,0:T(8,128)(2,1)S(1)} %pad_maximum_fusion.refs_3_, ...), custom_call_target="tpu_custom_call" | custom-call | tf_op jit(solution)/shard_map/rk_steps_0/pallas_call | solution.py:138
  51.1 6.1 %rk_steps_4.1 = f32[2,512,128]{2,1,0:T(8,128)} custom-call(s32[8,128]{1,0:T(8,128)S(1)} %get-tuple-element.19.refs_0_, s32[8,128]{1,0:T(8,128)S(1)} %get-tuple-element.18.refs_1_, s32[4,512,128]{2,1,0:T(8,128)S(1)} %get-tuple-element.7.refs_2_, bf16[4,8,96,128]{3,2,1,0:T(8,128)(2,1)S(1)} %pad_maximum_fusion.refs_3_, ...), custom_call_target="tpu_custom_call" | custom-call | tf_op jit(solution)/shard_map/rk_steps_4/pallas_call | solution.py:138
  57.1 1.5 %fusion.15 = (f32[2,512,127]{2,1,0:T(8,128)S(1)}, f32[2,512,127]{2,1,0:T(8,128)S(1)}) fusion(f32[2,512,128]{2,1,0:T(8,128)} %rk_steps_4.1), kind=kLoop, calls=%fused_computation.56 | loop fusion | bytes 2080768 | tf_op jit(solution)/shard_map/slice | solution.py:218
  58.6 2.7 %collective-permute-start.21 = (f32[2,1,128]{2,1,0:T(1,128)S(1)}, f32[2,1,128]{2,1,0:T(1,128)S(1)}, u32[]{:S(2)}, u32[]{:S(2)}) collective-permute-start(f32[2,1,128]{2,1,0:T(1,128)S(1)} %get-tuple-element.12), channel_id=1, source_target_pairs={{0,3},{1,0},{2,1},{3,2},{4,7},{5,4},{6,5},{7,6},{8,11},{9,8},{10,9... | collective-permute-start | bytes 3080 | tf_op jit(solution)/shard_map/ppermute | solution.py:166
  61.3 2.2 %collective-permute-start.22 = (f32[2,1,128]{2,1,0:T(1,128)S(1)}, f32[2,1,128]{2,1,0:T(1,128)S(1)}, u32[]{:S(2)}, u32[]{:S(2)}) collective-permute-start(f32[2,1,128]{2,1,0:T(1,128)S(1)} %get-tuple-element.13), channel_id=1, source_target_pairs={{0,1},{1,2},{2,3},{3,0},{4,5},{5,6},{6,7},{7,4},{8,9},{9,10},{10,1... | collective-permute-start | bytes 3080 | tf_op jit(solution)/shard_map/ppermute | solution.py:166
  64.1 1.9 %collective-permute-start.19 = (f32[2,512]{1,0:T(2,128)S(1)}, f32[2,512]{1,0:T(2,128)S(1)}, u32[]{:S(2)}, u32[]{:S(2)}) collective-permute-start(f32[2,512]{1,0:T(2,128)S(1)} %get-tuple-element.3), channel_id=1, source_target_pairs={{0,28},{4,0},{8,4},{12,8},{16,12},{20,16},{24,20},{28,24},{1,29},{... | collective-permute-start | bytes 12296 | tf_op jit(solution)/shard_map/ppermute | solution.py:166
  66.0 1.6 %collective-permute-done.22 = f32[2,1,128]{2,1,0:T(1,128)S(1)} collective-permute-done((f32[2,1,128]{2,1,0:T(1,128)S(1)}, f32[2,1,128]{2,1,0:T(1,128)S(1)}, u32[]{:S(2)}, u32[]{:S(2)}) %collective-permute-start.22) | collective-permute-done | bytes 1056 | tf_op jit(solution)/shard_map/ppermute | solution.py:166
  67.9 2.0 %collective-permute-done.20 = f32[2,512]{1,0:T(2,128)S(1)} collective-permute-done((f32[2,512]{1,0:T(2,128)S(1)}, f32[2,512]{1,0:T(2,128)S(1)}, u32[]{:S(2)}, u32[]{:S(2)}) %collective-permute-start.20) | collective-permute-done | bytes 4128 | tf_op jit(solution)/shard_map/ppermute | solution.py:166
  70.5 1.0 %multiply_bitcast_fusion = f32[512,128]{1,0:T(8,128)} fusion(f32[2,512,128]{2,1,0:T(8,128)S(1)} %fusion.1, f32[2,512,128]{2,1,0:T(8,128)S(1)} %fusion.2), kind=kLoop, calls=%fused_computation.21 | loop fusion | flops 1310720 | bytes 1310720 | tf_op jit(solution)/shard_map/mul | solution.py:161
  (49 shorter events, 4.2 us)
Async XLA Ops:
  1.6 12.0 %collective-permute-start.2 = (bf16[8,96,128]{2,1,0:T(8,128)(2,1)S(1)}, bf16[8,96,128]{2,1,0:T(8,128)(2,1)S(1)}, u32[]{:S(2)}, u32[]{:S(2)}) collective-permute-start(bf16[8,96,128]{2,1,0:T(8,128)(2,1)S(1)} %get-tuple-element.16), channel_id=1, source_target_pairs={{0,1},{1,0},{2,3},{3,2},{4,5},{5,4},{6,7},{7,6},{8,9},{9,8},{10,11... | collective-permute-start | bytes 589832 | tf_op jit(solution)/shard_map/ppermute | solution.py:18
  4.7 17.1 %collective-permute-start.5 = (bf16[8,96,128]{2,1,0:T(8,128)(2,1)S(1)}, bf16[8,96,128]{2,1,0:T(8,128)(2,1)S(1)}, u32[]{:S(2)}, u32[]{:S(2)}) collective-permute-start(bf16[8,96,128]{2,1,0:T(8,128)(2,1)S(1)} %get-tuple-element.16), channel_id=1, source_target_pairs={{0,2},{1,3},{2,0},{3,1},{4,6},{5,7},{6,4},{7,5},{8,10},{9,11},{10,... | collective-permute-start | bytes 589832 | tf_op jit(solution)/shard_map/ppermute | solution.py:18
  7.3 15.6 %collective-permute-start = (bf16[1,8,96,128]{3,2,1,0:T(8,128)(2,1)S(1)}, bf16[1,8,96,128]{3,2,1,0:T(8,128)(2,1)S(1)}, u32[]{:S(2)}, u32[]{:S(2)}) collective-permute-start(bf16[1,8,96,128]{3,2,1,0:T(8,128)(2,1)S(1)} %get-tuple-element.17), channel_id=1, source_target_pairs={{0,8},{4,20},{8,0},{12,28},{16,24},{20,4},{24,16},{28,12},{1,9},{5... | collective-permute-start | bytes 589832 | tf_op jit(solution)/shard_map/ppermute | solution.py:18
  9.7 9.6 %collective-permute-start.15 = (bf16[4,96,128]{2,1,0:T(8,128)(2,1)S(1)}, bf16[4,96,128]{2,1,0:T(8,128)(2,1)S(1)}, u32[]{:S(2)}, u32[]{:S(2)}) collective-permute-start(bf16[4,96,128]{2,1,0:T(8,128)(2,1)S(1)} %get-tuple-element.14), channel_id=1, source_target_pairs={{0,3},{1,2},{2,1},{3,0},{4,7},{5,6},{6,5},{7,4},{8,11},{9,10},{10,... | collective-permute-start | bytes 294920 | tf_op jit(solution)/shard_map/ppermute | solution.py:18
  10.0 10.8 %collective-permute-start.8 = (bf16[4,96,128]{2,1,0:T(8,128)(2,1)S(1)}, bf16[4,96,128]{2,1,0:T(8,128)(2,1)S(1)}, u32[]{:S(2)}, u32[]{:S(2)}) collective-permute-start(bf16[4,96,128]{2,1,0:T(8,128)(2,1)S(1)} %get-tuple-element.15), channel_id=1, source_target_pairs={{0,3},{1,2},{2,1},{3,0},{4,7},{5,6},{6,5},{7,4},{8,11},{9,10},{10,... | collective-permute-start | bytes 294920 | tf_op jit(solution)/shard_map/ppermute | solution.py:18
  13.6 11.4 %collective-permute-start.3 = (bf16[1,8,96,128]{3,2,1,0:T(8,128)(2,1)S(1)}, bf16[1,8,96,128]{3,2,1,0:T(8,128)(2,1)S(1)}, u32[]{:S(2)}, u32[]{:S(2)}) collective-permute-start(bf16[1,8,96,128]{3,2,1,0:T(8,128)(2,1)S(1)} %bitcast.22), channel_id=1, source_target_pairs={{0,8},{4,20},{8,0},{12,28},{16,24},{20,4},{24,16},{28,12},{1,9},{5... | collective-permute-start | bytes 589832 | tf_op jit(solution)/shard_map/ppermute | solution.py:18
  19.3 13.1 %collective-permute-start.16 = (bf16[1,4,96,128]{3,2,1,0:T(8,128)(2,1)S(1)}, bf16[1,4,96,128]{3,2,1,0:T(8,128)(2,1)S(1)}, u32[]{:S(2)}, u32[]{:S(2)}) collective-permute-start(bf16[1,4,96,128]{3,2,1,0:T(8,128)(2,1)S(1)} %bitcast.30), channel_id=1, source_target_pairs={{0,8},{4,20},{8,0},{12,28},{16,24},{20,4},{24,16},{28,12},{1,9},{5... | collective-permute-start | bytes 294920 | tf_op jit(solution)/shard_map/ppermute | solution.py:18
  20.8 13.9 %copy-start.1 = (bf16[4,96,128]{2,1,0:T(8,128)(2,1)}, bf16[4,96,128]{2,1,0:T(8,128)(2,1)S(1)}, u32[]{:S(2)}) copy-start(bf16[4,96,128]{2,1,0:T(8,128)(2,1)S(1)} %collective-permute-done.8) | copy-start | bytes 294916
  20.8 12.2 %collective-permute-start.9 = (bf16[1,4,96,128]{3,2,1,0:T(8,128)(2,1)S(1)}, bf16[1,4,96,128]{3,2,1,0:T(8,128)(2,1)S(1)}, u32[]{:S(2)}, u32[]{:S(2)}) collective-permute-start(bf16[1,4,96,128]{3,2,1,0:T(8,128)(2,1)S(1)} %bitcast.27), channel_id=1, source_target_pairs={{0,8},{4,20},{8,0},{12,28},{16,24},{20,4},{24,16},{28,12},{1,9},{5... | collective-permute-start | bytes 294920 | tf_op jit(solution)/shard_map/ppermute | solution.py:18
  21.8 8.9 %collective-permute-start.6 = (bf16[1,8,96,128]{3,2,1,0:T(8,128)(2,1)S(1)}, bf16[1,8,96,128]{3,2,1,0:T(8,128)(2,1)S(1)}, u32[]{:S(2)}, u32[]{:S(2)}) collective-permute-start(bf16[1,8,96,128]{3,2,1,0:T(8,128)(2,1)S(1)} %bitcast.19), channel_id=1, source_target_pairs={{0,8},{4,20},{8,0},{12,28},{16,24},{20,4},{24,16},{28,12},{1,9},{5... | collective-permute-start | bytes 589832 | tf_op jit(solution)/shard_map/ppermute | solution.py:18
  23.0 11.6 %collective-permute-start.1 = (bf16[2,8,96,128]{3,2,1,0:T(8,128)(2,1)S(1)}, bf16[2,8,96,128]{3,2,1,0:T(8,128)(2,1)S(1)}, u32[]{:S(2)}, u32[]{:S(2)}) collective-permute-start(bf16[2,8,96,128]{3,2,1,0:T(8,128)(2,1)S(1)} %pad_maximum_fusion.5), channel_id=1, source_target_pairs={{0,16},{4,12},{8,24},{12,4},{16,0},{20,28},{24,8},{28,20},{1,17},{... | collective-permute-start | bytes 1179656 | tf_op jit(solution)/shard_map/ppermute | solution.py:18
  25.0 10.0 %collective-permute-start.4 = (bf16[2,8,96,128]{3,2,1,0:T(8,128)(2,1)S(1)}, bf16[2,8,96,128]{3,2,1,0:T(8,128)(2,1)S(1)}, u32[]{:S(2)}, u32[]{:S(2)}) collective-permute-start(bf16[2,8,96,128]{3,2,1,0:T(8,128)(2,1)S(1)} %pad_maximum_fusion.6), channel_id=1, source_target_pairs={{0,16},{4,12},{8,24},{12,4},{16,0},{20,28},{24,8},{28,20},{1,17},{... | collective-permute-start | bytes 1179656 | tf_op jit(solution)/shard_map/ppermute | solution.py:18
  30.8 8.5 %collective-permute-start.7 = (bf16[2,8,96,128]{3,2,1,0:T(8,128)(2,1)S(1)}, bf16[2,8,96,128]{3,2,1,0:T(8,128)(2,1)S(1)}, u32[]{:S(2)}, u32[]{:S(2)}) collective-permute-start(bf16[2,8,96,128]{3,2,1,0:T(8,128)(2,1)S(1)} %pad_maximum_fusion.7), channel_id=1, source_target_pairs={{0,16},{4,12},{8,24},{12,4},{16,0},{20,28},{24,8},{28,20},{1,17},{... | collective-permute-start | bytes 1179656 | tf_op jit(solution)/shard_map/ppermute | solution.py:18
  32.4 8.9 %collective-permute-start.17 = (bf16[2,4,96,128]{3,2,1,0:T(8,128)(2,1)S(1)}, bf16[2,4,96,128]{3,2,1,0:T(8,128)(2,1)S(1)}, u32[]{:S(2)}, u32[]{:S(2)}) collective-permute-start(bf16[2,4,96,128]{3,2,1,0:T(8,128)(2,1)S(1)} %pad_maximum_fusion.12), channel_id=1, source_target_pairs={{0,16},{4,12},{8,24},{12,4},{16,0},{20,28},{24,8},{28,20},{1,17},{... | collective-permute-start | bytes 589832 | tf_op jit(solution)/shard_map/ppermute | solution.py:18
  33.0 10.5 %collective-permute-start.10 = (bf16[2,4,96,128]{3,2,1,0:T(8,128)(2,1)S(1)}, bf16[2,4,96,128]{3,2,1,0:T(8,128)(2,1)S(1)}, u32[]{:S(2)}, u32[]{:S(2)}) collective-permute-start(bf16[2,4,96,128]{3,2,1,0:T(8,128)(2,1)S(1)} %pad_maximum_fusion.11), channel_id=1, source_target_pairs={{0,16},{4,12},{8,24},{12,4},{16,0},{20,28},{24,8},{28,20},{1,17},{... | collective-permute-start | bytes 589832 | tf_op jit(solution)/shard_map/ppermute | solution.py:18
  34.7 9.2 %copy-start.3 = (s32[1,1,8,128]{3,2,1,0:T(8,128)S(1)}, s32[1,1,8,128]{3,2,1,0:T(8,128)}, u32[]{:S(2)}) copy-start(s32[1,1,8,128]{3,2,1,0:T(8,128)} %param.8) | copy-start | bytes 12292
  34.7 10.9 %collective-permute-start.11 = (bf16[4,8,96,128]{3,2,1,0:T(8,128)(2,1)S(1)}, bf16[4,8,96,128]{3,2,1,0:T(8,128)(2,1)S(1)}, u32[]{:S(2)}, u32[]{:S(2)}) collective-permute-start(bf16[4,8,96,128]{3,2,1,0:T(8,128)(2,1)S(1)} %pad_maximum_fusion.refs_3_), channel_id=1, source_target_pairs={{0,4},{4,0},{8,12},{12,8},{16,20},{20,16},{24,28},{28,24},{1,5},{5... | collective-permute-start | bytes 2359304 | tf_op jit(solution)/shard_map/ppermute | solution.py:18
  34.8 8.7 %copy-start.2 = (bf16[4,96,128]{2,1,0:T(8,128)(2,1)S(1)}, bf16[4,96,128]{2,1,0:T(8,128)(2,1)}, u32[]{:S(2)}) copy-start(bf16[4,96,128]{2,1,0:T(8,128)(2,1)} %copy-done.1) | copy-start | bytes 294916
  35.1 10.5 %collective-permute-start.12 = (bf16[4,8,96,128]{3,2,1,0:T(8,128)(2,1)S(1)}, bf16[4,8,96,128]{3,2,1,0:T(8,128)(2,1)}, u32[]{:S(2)}, u32[]{:S(2)}) collective-permute-start(bf16[4,8,96,128]{3,2,1,0:T(8,128)(2,1)S(1)} %pad_maximum_fusion.1.refs_4_), channel_id=1, source_target_pairs={{0,4},{4,0},{8,12},{12,8},{16,20},{20,16},{24,28},{28,24},{1,5},{5... | collective-permute-start | bytes 2359304 | tf_op jit(solution)/shard_map/ppermute | solution.py:18
  39.3 6.3 %collective-permute-start.13 = (bf16[4,8,96,128]{3,2,1,0:T(8,128)(2,1)S(1)}, bf16[4,8,96,128]{3,2,1,0:T(8,128)(2,1)}, u32[]{:S(2)}, u32[]{:S(2)}) collective-permute-start(bf16[4,8,96,128]{3,2,1,0:T(8,128)(2,1)S(1)} %pad_maximum_fusion.2.refs_5_), channel_id=1, source_target_pairs={{0,4},{4,0},{8,12},{12,8},{16,20},{20,16},{24,28},{28,24},{1,5},{5... | collective-permute-start | bytes 2359304 | tf_op jit(solution)/shard_map/ppermute | solution.py:18
  42.2 3.5 %collective-permute-start.18 = (bf16[4,4,96,128]{3,2,1,0:T(8,128)(2,1)}, bf16[4,4,96,128]{3,2,1,0:T(8,128)(2,1)}, u32[]{:S(2)}, u32[]{:S(2)}) collective-permute-start(bf16[4,4,96,128]{3,2,1,0:T(8,128)(2,1)} %pad_maximum_fusion.9.refs_6_), channel_id=1, source_target_pairs={{0,4},{4,0},{8,12},{12,8},{16,20},{20,16},{24,28},{28,24},{1,5},{5... | collective-permute-start | bytes 1179656 | tf_op jit(solution)/shard_map/ppermute | solution.py:18
  43.5 7.5 %collective-permute-start.14 = (bf16[4,4,96,128]{3,2,1,0:T(8,128)(2,1)S(1)}, bf16[4,4,96,128]{3,2,1,0:T(8,128)(2,1)}, u32[]{:S(2)}, u32[]{:S(2)}) collective-permute-start(bf16[4,4,96,128]{3,2,1,0:T(8,128)(2,1)S(1)} %pad_maximum_fusion.8.refs_6_), channel_id=1, source_target_pairs={{0,4},{4,0},{8,12},{12,8},{16,20},{20,16},{24,28},{28,24},{1,5},{5... | collective-permute-start | bytes 1179656 | tf_op jit(solution)/shard_map/ppermute | solution.py:18
  57.1 1.5 %copy-start = (f32[2,512,128]{2,1,0:T(8,128)S(1)}, f32[2,512,128]{2,1,0:T(8,128)}, u32[]{:S(2)}) copy-start(f32[2,512,128]{2,1,0:T(8,128)} %rk_steps_4.1) | copy-start | bytes 1572868
  58.6 7.4 %collective-permute-start.21 = (f32[2,1,128]{2,1,0:T(1,128)S(1)}, f32[2,1,128]{2,1,0:T(1,128)S(1)}, u32[]{:S(2)}, u32[]{:S(2)}) collective-permute-start(f32[2,1,128]{2,1,0:T(1,128)S(1)} %get-tuple-element.12), channel_id=1, source_target_pairs={{0,3},{1,0},{2,1},{3,2},{4,7},{5,4},{6,5},{7,6},{8,11},{9,8},{10,9... | collective-permute-start | bytes 3080 | tf_op jit(solution)/shard_map/ppermute | solution.py:166
  61.3 6.3 %collective-permute-start.22 = (f32[2,1,128]{2,1,0:T(1,128)S(1)}, f32[2,1,128]{2,1,0:T(1,128)S(1)}, u32[]{:S(2)}, u32[]{:S(2)}) collective-permute-start(f32[2,1,128]{2,1,0:T(1,128)S(1)} %get-tuple-element.13), channel_id=1, source_target_pairs={{0,1},{1,2},{2,3},{3,0},{4,5},{5,6},{6,7},{7,4},{8,9},{9,10},{10,1... | collective-permute-start | bytes 3080 | tf_op jit(solution)/shard_map/ppermute | solution.py:166
  64.1 3.6 %collective-permute-start.19 = (f32[2,512]{1,0:T(2,128)S(1)}, f32[2,512]{1,0:T(2,128)S(1)}, u32[]{:S(2)}, u32[]{:S(2)}) collective-permute-start(f32[2,512]{1,0:T(2,128)S(1)} %get-tuple-element.3), channel_id=1, source_target_pairs={{0,28},{4,0},{8,4},{12,8},{16,12},{20,16},{24,20},{28,24},{1,29},{... | collective-permute-start | bytes 12296 | tf_op jit(solution)/shard_map/ppermute | solution.py:166
  66.0 3.9 %collective-permute-start.20 = (f32[2,512]{1,0:T(2,128)S(1)}, f32[2,512]{1,0:T(2,128)S(1)}, u32[]{:S(2)}, u32[]{:S(2)}) collective-permute-start(f32[2,512]{1,0:T(2,128)S(1)} %get-tuple-element.2), channel_id=1, source_target_pairs={{0,4},{4,8},{8,12},{12,16},{16,20},{20,24},{24,28},{28,0},{1,5},{5... | collective-permute-start | bytes 12296 | tf_op jit(solution)/shard_map/ppermute | solution.py:166

commit v2 on v1

v2 whole, which is shorter than its diff:
```python
import functools

import jax
import jax.numpy as jnp
from jax import lax
from jax.experimental import pallas as pl
from jax.experimental.pallas import tpu as pltpu
from jax.sharding import PartitionSpec as P

GROUP_ROWS = 4
TABLE_BYTES = 13 << 20
WAITS = {
    "z3": ("z1",),
    "edge": ("r0.1",),
    "r1.1": ("z1",),
    "r2.1": ("z1",),
    "r1.2": ("r0.2",),
    "c2": ("r3.1",),
}


def after(value, *earlier):
    return lax.optimization_barrier((value, *earlier))[0] if earlier else value


def swap(value, axis, masks):
    count = lax.axis_size(axis)
    pairs = [(i, i ^ masks[i % len(masks)]) for i in range(count)]
    return lax.ppermute(value, axis, pairs)


def plane_masks(n_lon):
    bits = []
    mask = 2
    while mask < n_lon:
        bits.append(mask)
        mask *= 2
    return bits, bits[::-1]


def slot_of(owners, n_lat):
    lon, lat = lax.axis_index("lon"), lax.axis_index("lat")
    even, odd = plane_masks(lax.axis_size("lon"))
    places = 1 << len(even)
    owner_lon, owner_lat = owners // n_lat, owners % n_lat
    apart = owner_lat ^ lat
    foreign = (owner_lon ^ lon) & 1
    base = lon ^ foreign
    diff = owner_lon ^ base
    place = jnp.zeros_like(owners)
    for position, (even_mask, odd_mask) in enumerate(zip(even, odd)):
        mask = jnp.where((base & 1) == 0, even_mask, odd_mask)
        place = place + jnp.where((diff & mask) != 0, 1 << position, 0)
    return (apart * 2 + foreign) * places + place


def advance(along_x, along_y, coeffs):
    vel_x, vel_y, xx, xy, yx, yy = coeffs
    half_x = vel_x + xx * along_x + xy * along_y
    half_y = vel_y + yx * along_x + yy * along_y
    full_x = half_x + half_x
    full_y = half_y + half_y
    third_x = full_x + (xx * half_x + xy * half_y)
    third_y = full_y + (yx * half_x + yy * half_y)
    ratio = 2.0 / 3.0
    second_x = full_x + ratio * (xx * third_x + xy * third_y)
    second_y = full_y + ratio * (yx * third_x + yy * third_y)
    new_x = along_x + (full_x + (xx * second_x + xy * second_y))
    new_y = along_y + (full_y + (yx * second_x + yy * second_y))
    return new_x, new_y


def steps_kernel(first, scale, step_rows, slots, has_start, last, unroll, *refs):
    count = len(slots)
    base_ref, grad_ref, edge_ref, cells_hbm = refs[:4]
    pieces = refs[4 : 4 + count]
    start_ref, start_edge = refs[4 + count : 6 + count] if has_start else (None, None)
    rest = refs[(6 if has_start else 4) + count :]
    flow_ref, out_edge, table, cells_ref, arrived = rest[0], rest[1], *rest[-3:]
    out_ref, out_sides = rest[2:4] if last else (None, None)
    steps, rows, lanes = cells_ref.shape
    fetch = pltpu.make_async_copy(cells_hbm.at[pl.ds(first, steps)], cells_ref, arrived)
    fetch.start()
    for slot, piece in zip(slots, pieces):

        def widen(part, carry, slot=slot, piece=piece):
            place, step = part // steps, part % steps
            source = pl.multiple_of((first + step) * step_rows, step_rows)
            row = pl.multiple_of((slot * steps + part) * step_rows, step_rows)
            values = piece[place, pl.ds(source, step_rows), :].astype(jnp.float32) * scale
            table[pl.ds(row, step_rows), :] = values
            return carry

        lax.fori_loop(0, piece.shape[0] * steps, widen, 0, unroll=4)
    fetch.wait()
    upper = lax.broadcasted_iota(jnp.int32, (8, lanes), 0) < GROUP_ROWS
    lane = lax.broadcasted_iota(jnp.int32, (8, lanes), 1)
    zero = jnp.zeros((8, lanes), jnp.float32)

    def begin_at(ref, row):
        return (ref[0, pl.ds(row, 8), :], ref[1, pl.ds(row, 8), :]) if has_start else (zero, zero)

    def tile(one, two, indices, along_x, along_y):
        for step in range(steps):
            index = indices(step)
            sources = [
                (ref[first + step, one] + k, ref[first + step, two] + k)
                for ref, number in ((base_ref, 2), (grad_ref, 4))
                for k in range(number)
            ]
            coeffs = []
            for above, below in sources:
                values = jnp.where(
                    upper,
                    jnp.broadcast_to(table[pl.ds(above, 1), :], (8, lanes)),
                    jnp.broadcast_to(table[pl.ds(below, 1), :], (8, lanes)),
                )
                coeffs.append(
                    jnp.take_along_axis(values, index, axis=1, mode="promise_in_bounds")
                )
            along_x, along_y = advance(along_x, along_y, coeffs)
        return along_x, along_y

    def tiles(number, carry):
        for inner in range(unroll):
            at = number * unroll + inner
            row = pl.multiple_of(at * 8, 8)
            start = begin_at(start_ref, row)
            end = tile(2 * at, 2 * at + 1, lambda step: cells_ref[step, pl.ds(row, 8), :], *start)
            if last:
                out_ref[0, pl.ds(row, 8), :], out_ref[1, pl.ds(row, 8), :] = end
            flow_ref[0, pl.ds(row, 8), :], flow_ref[1, pl.ds(row, 8), :] = end
        return carry

    lax.fori_loop(0, rows // 8 // unroll, tiles, 0)
    groups = rows // GROUP_ROWS
    start = begin_at(start_edge, 0)
    end = tile(groups, groups + 1, lambda step: edge_ref[first + step], *start)
    out_edge[0], out_edge[1] = end
    if not last:
        return
    half = lanes // 2
    ends = jnp.where(lane < half, 0, lanes - 1)
    for part in range(2):
        sides = [zero] * 4
        for at in range(rows // 8):
            value = flow_ref[part, at * 8 : at * 8 + 8, :]
            value = jnp.take_along_axis(value, ends, axis=1, mode="promise_in_bounds")
            sides[at % 4] = jnp.where((lane & (half - 1)) == at, value, sides[at % 4])
        out_sides[part] = (sides[0] + sides[1]) + (sides[2] + sides[3])


def run_steps(first, last, scale, step_rows, base, grad, edge_cells, cells, items, start):
    num_steps, rows, lanes = cells.shape
    steps = last - first
    pieces = [item[0] for item in items]
    slots = tuple(item[1] for item in items)
    height = sum(piece.shape[0] for piece in pieces) * steps * step_rows
    vmem = pl.BlockSpec(memory_space=pltpu.VMEM)
    smem = pl.BlockSpec(memory_space=pltpu.SMEM)
    need = height * lanes * 4 + steps * rows * lanes * 4
    small = jax.ShapeDtypeStruct((2, 8, lanes), jnp.float32)
    whole = jax.ShapeDtypeStruct((2, rows, lanes), jnp.float32)
    final = last == num_steps
    starts = list(start) if first else []
    return pl.pallas_call(
        functools.partial(steps_kernel, first, scale, step_rows, slots, first > 0, final, 8),
        out_shape=(whole, small) + ((whole, small) if final else ()),
        in_specs=[smem, smem, vmem, pl.BlockSpec(memory_space=pltpu.HBM)] + [vmem] * len(pieces + starts),
        out_specs=(vmem,) * (4 if final else 2),
        scratch_shapes=[
            pltpu.VMEM((height, lanes), jnp.float32),
            pltpu.VMEM((steps, rows, lanes), jnp.int32),
            pltpu.SemaphoreType.DMA(()),
        ],
        cost_estimate=pl.CostEstimate(
            flops=40 * steps * rows * lanes, bytes_accessed=16 << 20, transcendentals=0
        ),
        compiler_params=pltpu.CompilerParams(vmem_limit_bytes=need + (3 << 20)),
        name=f"rk_steps_{first}",
    )(base, grad, edge_cells, cells, *pieces, *starts)


def stretch_kernel(flag_ref, flow_ref, edge_ref, inner_ref, outer_ref, out_ref):
    _, rows, lanes = flow_ref.shape
    half = lanes // 2
    lane = lax.broadcasted_iota(jnp.int32, (8, lanes), 1)
    row = lax.broadcasted_iota(jnp.int32, (8, lanes), 0)
    odd, lowest, highest = flag_ref[0] == 1, flag_ref[1] == 1, flag_ref[2] == 1
    sides, south, north = [], [], []
    for part in range(2):
        inner, outer = inner_ref[part], outer_ref[part]
        west, east = jnp.where(odd, inner, outer), jnp.where(odd, outer, inner)
        sides.append(jnp.where(lane < half, east, west))
        south.append(jnp.where(lowest, flow_ref[part, 0:1, :], edge_ref[part, 0:1, :]))
        beyond = edge_ref[part, GROUP_ROWS : GROUP_ROWS + 1, :]
        north.append(jnp.where(highest, flow_ref[part, rows - 1 : rows, :], beyond))
    tiles = rows // 8
    for at in range(tiles):
        start = at * 8
        index = jnp.where(lane < half, half + at, at)
        diff_lon, diff_lat = [], []
        for part in range(2):
            flow = flow_ref[part, start : start + 8, :]
            halo = jnp.take_along_axis(sides[part], index, axis=1, mode="promise_in_bounds")
            left = jnp.where(lane == 0, halo, pltpu.roll(flow, 1, 1))
            right = jnp.where(lane == lanes - 1, halo, pltpu.roll(flow, lanes - 1, 1))
            diff_lon.append((right - left) * 0.5)
            under = south[part] if at == 0 else flow_ref[part, start - 1 : start, :]
            over = north[part] if at == tiles - 1 else flow_ref[part, start + 8 : start + 9, :]
            below = jnp.where(row == 0, jnp.broadcast_to(under, flow.shape), pltpu.roll(flow, 1, 0))
            above = jnp.where(row == 7, jnp.broadcast_to(over, flow.shape), pltpu.roll(flow, 7, 0))
            diff_lat.append((above - below) * 0.5)
        out_ref[start : start + 8, :] = stretch_rate(diff_lon, diff_lat)


def stretch_rate(diff_lon, diff_lat):
    map_xx = 1.0 + diff_lon[0]
    map_xy = diff_lat[0]
    map_yx = diff_lon[1]
    map_yy = 1.0 + diff_lat[1]
    green_xx = map_xx * map_xx + map_yx * map_yx
    green_yy = map_xy * map_xy + map_yy * map_yy
    green_xy = map_xx * map_xy + map_yx * map_yy
    half_diff = 0.5 * (green_xx - green_yy)
    largest = 0.5 * (green_xx + green_yy) + jnp.sqrt(half_diff * half_diff + green_xy * green_xy)
    return 0.5 * jnp.log(largest)


def body(vel_base, vel_grad, route_dev, route_block, seed_cells):
    n_lon, n_lat = lax.axis_size("lon"), lax.axis_size("lat")
    num_steps, rows, lanes = seed_cells.shape
    blocks = vel_base.shape[3]
    step_rows = 6 * blocks
    shard = jnp.concatenate(
        [
            vel_base.reshape(num_steps, 2 * blocks, lanes),
            vel_grad.reshape(num_steps, 4 * blocks, lanes),
        ],
        axis=1,
    ).reshape(num_steps * step_rows, lanes)
    places = n_lon // 2
    owners = route_dev[0, 0, :, :, 0]
    wanted = route_block[0, 0]
    done = {}

    def gated(value, label):
        return after(value, *[done[name] for name in WAITS.get(label, ())])

    came = [shard]
    for apart in range(1, n_lat):
        done[f"z{apart}"] = swap(gated(shard, f"z{apart}"), "lat", (apart,))
        came.append(done[f"z{apart}"])
    even, odd = plane_masks(n_lon)
    held = [value[None] for value in came]
    for stage, masks in enumerate(zip(even, odd)):
        for apart in range(n_lat):
            label = f"r{apart}.{stage + 1}"
            sent = gated(held[apart], label)
            done[label] = swap(sent, "lon", masks)
            held[apart] = jnp.concatenate([sent, done[label]])
    items = []
    for apart in range(n_lat):
        other = swap(gated(held[apart], f"c{apart}"), "lon", (1,))
        items += [(held[apart], 2 * apart * places), (other, (2 * apart + 1) * places)]

    def edge_of(row):
        value = jnp.stack([seed_cells[:, row, :], owners, wanted])
        return gated(value, "edge")

    south = lax.ppermute(edge_of(-1), "lat", [(i, i + 1) for i in range(n_lat - 1)])
    north = lax.ppermute(edge_of(0), "lat", [(i + 1, i) for i in range(n_lat - 1)])
    edge_cells = jnp.repeat(jnp.stack([south[0], north[0]], axis=1), GROUP_ROWS, axis=1)
    owners = jnp.concatenate([owners, south[1, :, -1:], north[1, :, :1]], axis=1)
    wanted = jnp.concatenate([wanted, south[2, :, -1:], north[2, :, :1]], axis=1)
    lat_index = lax.axis_index("lat")
    state = None
    slots = slot_of(owners, n_lat)
    each = max(1, min(num_steps, TABLE_BYTES // (n_lon * n_lat * step_rows * lanes * 4)))
    for first in range(0, num_steps, each):
        last = min(first + each, num_steps)
        local = jnp.arange(num_steps, dtype=jnp.int32)[:, None] - first
        row = (slots * (last - first) + local) * step_rows
        base = row + 2 * wanted
        grad = row + 2 * blocks + 4 * wanted
        state = run_steps(
            first,
            last,
            -0.5 / num_steps,
            step_rows,
            base,
            grad,
            edge_cells,
            seed_cells,
            items,
            state,
        )
    flow, edge, out, sides = state
    inner = swap(sides, "lon", (1,))
    outer = lax.ppermute(
        sides, "lon", [(i, (i + (1 if i % 2 else -1)) % n_lon) for i in range(n_lon)]
    )
    flags = jnp.stack([lax.axis_index("lon") % 2, lat_index == 0, lat_index == n_lat - 1])
    vmem = pl.BlockSpec(memory_space=pltpu.VMEM)
    field = pl.pallas_call(
        stretch_kernel,
        out_shape=jax.ShapeDtypeStruct((rows, lanes), jnp.float32),
        in_specs=[pl.BlockSpec(memory_space=pltpu.SMEM)] + [vmem] * 4,
        out_specs=vmem,
        compiler_params=pltpu.CompilerParams(vmem_limit_bytes=16 << 20),
        name="stretch",
    )(flags.astype(jnp.int32), flow, edge, inner, outer)
    return (out, field)


def solution(mesh):
    in_specs = (
        P("lon", "lat", None, None, None, None),
        P("lon", "lat", None, None, None, None),
        P("lon", "lat", None, None, None),
        P("lon", "lat", None, None),
        P(None, "lat", "lon"),
    )
    out_specs = (P(None, "lat", "lon"), P("lat", "lon"))
    return jax.shard_map(body, mesh=mesh, in_specs=in_specs, out_specs=out_specs, check_vma=False)
```

time: 71.8 us -> 62.9 us (0.88)
  starting transfers between devices: 31 us -> 25.1 us
  other arithmetic: 5.33 us -> 2.19 us
  local copies, waits for them, and re-layouts: 4.12 us -> 1.06 us
  waiting for transfers between devices: 18.7 us -> 20.8 us
    ppermute x19 -> x16, starting transfers between devices: 24.2 us -> 19 us  [swap(): return lax.ppermute(value, axis, pairs)]
    ppermute x19 -> x16, waiting for transfers between devices: 15.1 us -> 19.3 us  [swap(): return lax.ppermute(value, axis, pairs)]
    slice x4 -> x1, local copies, waits for them, and re-layouts: 3.66 us -> 0.78 us  [edge_of(): value = jnp.stack([seed_cells[:, row, :], owners, wanted])]
    ppermute x4 -> x3, waiting for transfers between devices: 3.57 us -> 1.52 us  [the longest x1 1.46 us: body(): lax.ppermute(sides, 'lon', [(i, (i + (1 if i % 2 else -1)) % n_lon) for i...]
    mul x3 -> x0, other arithmetic: 1.42 us -> none  [the longest x1 0.96 us: stretch_rate(): return 0.5 * jnp.log(largest)]
    concatenate x2 -> x1, other arithmetic: 1.89 us -> 0.92 us  [body(): jnp.concatenate([vel_base.reshape(num_steps, 2 * blocks, lanes), vel_grad...]
    concatenate x10 -> x6, other arithmetic: 1.22 us -> 0.31 us  [body(): held[apart] = jnp.concatenate([sent, done[label]])]
    another operation x0 -> x3, other arithmetic: none -> 0.78 us  [the longest x1 0.71 us: edge_of(): value = jnp.stack([seed_cells[:, row, :], owners, wanted])]
  transfers between devices with their start and end apart: 23 -> 19, of which waited for: 8 -> 10; matrix products, arithmetic and copies ran while one was open for 8% -> 4% of each run, Pallas kernels for 8% -> 0%
where the time goes in v2:
time: 62.9 us; the launch traced here: 61.8 us
  starting transfers between devices  25.1 us (40%)
  waiting for transfers between devices  20.8 us (33%)
  Pallas kernels  11.8 us (19%)
  other arithmetic  2.19 us (3%)
  local copies, waits for them, and re-layouts  1.06 us (2%)
  between operations  0.84 us (1%)
    ppermute x16, waiting for transfers between devices, swap(): return lax.ppermute(value, axis, pairs)  19.3 us
    ppermute x16, starting transfers between devices, swap(): return lax.ppermute(value, axis, pairs)  19 us
    pallas_call x1, Pallas kernels, run_steps(): pl.pallas_call(functools.partial(steps_kernel, first, scale, step_rows, s...  9.9 us
    ppermute x1, starting transfers between devices, body(): lax.ppermute(sides, 'lon', [(i, (i + (1 if i % 2 else -1)) % n_lon) for i...  2.5 us
    ppermute x1, starting transfers between devices, body(): lax.ppermute(edge_of(-1), 'lat', [(i, i + 1) for i in range(n_lat - 1)])  2.34 us
    pallas_call x1, Pallas kernels, body(): pl.pallas_call(stretch_kernel, out_shape=jax.ShapeDtypeStruct((rows, lane...  1.94 us
    ppermute x1, waiting for transfers between devices, body(): lax.ppermute(sides, 'lon', [(i, (i + (1 if i % 2 else -1)) % n_lon) for i...  1.46 us
    ppermute x1, starting transfers between devices, body(): lax.ppermute(edge_of(0), 'lat', [(i + 1, i) for i in range(n_lat - 1)])  1.29 us
  transfers between devices with their start and end apart: 19, of which 10 were waited for; matrix products, arithmetic and copies ran while one was open for 4% of the time, Pallas kernels for 0%

profile of v2, /device:TPU:0, one launch (start us, length us, event | category | flops | bytes accessed | tf_op | source)
XLA Modules:
  0.0 61.8 jit_solution(5365690152686709741)
XLA Ops:
  0.6 0.9 %pad_maximum_fusion.6 = bf16[8,96,128]{2,1,0:T(8,128)(2,1)S(1)} fusion(bf16[8,64,128]{2,1,0:T(8,128)(2,1)} %bitcast.46, bf16[8,32,128]{2,1,0:T(8,128)(2,1)} %bitcast.47), kind=kLoop, calls=%fused_computation.6 | loop fusion | flops 393216 | bytes 393216 | tf_op jit(solution)/shard_map/concatenate | solution.py:235
  1.6 4.1 %collective-permute-start.9 = (bf16[768,128]{1,0:T(8,128)(2,1)S(1)}, bf16[768,128]{1,0:T(8,128)(2,1)S(1)}, u32[]{:S(2)}, u32[]{:S(2)}) collective-permute-start(bf16[768,128]{1,0:T(8,128)(2,1)S(1)} %bitcast.32), channel_id=1, source_target_pairs={{0,2},{1,3},{2,0},{3,1},{4,6},{5,7},{6,4},{7,5},{8,10},{9,11},{10,... | collective-permute-start | bytes 589832 | tf_op jit(solution)/shard_map/ppermute | solution.py:29
  5.7 1.6 %collective-permute-start.5 = (bf16[768,128]{1,0:T(8,128)(2,1)S(1)}, bf16[768,128]{1,0:T(8,128)(2,1)S(1)}, u32[]{:S(2)}, u32[]{:S(2)}) collective-permute-start(bf16[768,128]{1,0:T(8,128)(2,1)S(1)} %bitcast.33), channel_id=1, source_target_pairs={{0,1},{1,0},{2,3},{3,2},{4,5},{5,4},{6,7},{7,6},{8,9},{9,8},{10,11... | collective-permute-start | bytes 589832 | tf_op jit(solution)/shard_map/ppermute | solution.py:29
  7.2 1.5 %collective-permute-start = (bf16[1,768,128]{2,1,0:T(8,128)(2,1)S(1)}, bf16[1,768,128]{2,1,0:T(8,128)(2,1)S(1)}, u32[]{:S(2)}, u32[]{:S(2)}) collective-permute-start(bf16[1,768,128]{2,1,0:T(8,128)(2,1)S(1)} %bitcast.34), channel_id=1, source_target_pairs={{0,8},{4,20},{8,0},{12,28},{16,24},{20,4},{24,16},{28,12},{1,9},{5... | collective-permute-start | bytes 589832 | tf_op jit(solution)/shard_map/ppermute | solution.py:29
  8.7 0.8 %fusion.11 = (s32[8,1,128]{2,1,0:T(1,128)S(1)}, s32[8,1,128]{2,1,0:T(1,128)S(1)}) fusion(s32[8,512,128]{2,1,0:T(8,128)} %refs_3_.1), kind=kLoop, calls=%fused_computation.48 | loop fusion | bytes 16384 | tf_op jit(solution)/shard_map/slice | solution.py:268
  9.5 0.7 %pad_add_fusion.1 = (s32[3,8,128]{2,1,0:T(8,128)S(1)}, s32[3,8,128]{2,1,0:T(8,128)S(1)}) fusion(s32[1,8,128]{2,1,0:T(8,128)} %bitcast.48, s32[1,8,128]{2,1,0:T(8,128)} %bitcast.53, s32[1,8,128]{2,1,0:T(8,128)S(1)} %bitcast.51, s32[1,8,128]{2,1,0:T(8,128)S(1)} %bitcast.52), kind=kLoop, calls=%fused_computation.8 | loop fusion | flops 12288 | bytes 40960 | tf_op jit(solution)/shard_map/stack | solution.py:268
  10.2 2.7 %collective-permute-done = bf16[1,768,128]{2,1,0:T(8,128)(2,1)S(1)} collective-permute-done((bf16[1,768,128]{2,1,0:T(8,128)(2,1)S(1)}, bf16[1,768,128]{2,1,0:T(8,128)(2,1)S(1)}, u32[]{:S(2)}, u32[]{:S(2)}) %collective-permute-start) | collective-permute-done | bytes 196640 | tf_op jit(solution)/shard_map/ppermute | solution.py:29
  12.9 2.3 %collective-permute-start.1 = (s32[3,8,128]{2,1,0:T(8,128)S(1)}, s32[3,8,128]{2,1,0:T(8,128)S(1)}, u32[]{:S(2)}, u32[]{:S(2)}) collective-permute-start(s32[3,8,128]{2,1,0:T(8,128)S(1)} %get-tuple-element.13), channel_id=1, source_target_pairs={{0,1},{1,2},{2,3},{4,5},{5,6},{6,7},{8,9},{9,10},{10,11},{12,13},{... | collective-permute-start | bytes 36872 | tf_op jit(solution)/shard_map/ppermute | solution.py:271
  15.3 1.3 %collective-permute-start.2 = (s32[3,8,128]{2,1,0:T(8,128)S(1)}, s32[3,8,128]{2,1,0:T(8,128)S(1)}, u32[]{:S(2)}, u32[]{:S(2)}) collective-permute-start(s32[3,8,128]{2,1,0:T(8,128)S(1)} %get-tuple-element.14), channel_id=1, source_target_pairs={{1,0},{2,1},{3,2},{5,4},{6,5},{7,6},{9,8},{10,9},{11,10},{13,12},{... | collective-permute-start | bytes 36872 | tf_op jit(solution)/shard_map/ppermute | solution.py:272
  16.6 1.6 %collective-permute-start.10 = (bf16[1,768,128]{2,1,0:T(8,128)(2,1)S(1)}, bf16[1,768,128]{2,1,0:T(8,128)(2,1)S(1)}, u32[]{:S(2)}, u32[]{:S(2)}) collective-permute-start(bf16[1,768,128]{2,1,0:T(8,128)(2,1)S(1)} %bitcast.41), channel_id=1, source_target_pairs={{0,8},{4,20},{8,0},{12,28},{16,24},{20,4},{24,16},{28,12},{1,9},{5... | collective-permute-start | bytes 589832 | tf_op jit(solution)/shard_map/ppermute | solution.py:29
  18.1 2.4 %collective-permute-start.12 = (bf16[768,128]{1,0:T(8,128)(2,1)S(1)}, bf16[768,128]{1,0:T(8,128)(2,1)S(1)}, u32[]{:S(2)}, u32[]{:S(2)}) collective-permute-start(bf16[768,128]{1,0:T(8,128)(2,1)S(1)} %bitcast.35), channel_id=1, source_target_pairs={{0,3},{1,2},{2,1},{3,0},{4,7},{5,6},{6,5},{7,4},{8,11},{9,10},{10,... | collective-permute-start | bytes 589832 | tf_op jit(solution)/shard_map/ppermute | solution.py:29
  20.6 0.3 collective-permute-start.6
  20.9 1.8 %collective-permute-start.3 = (bf16[2,768,128]{2,1,0:T(8,128)(2,1)S(1)}, bf16[2,768,128]{2,1,0:T(8,128)(2,1)S(1)}, u32[]{:S(2)}, u32[]{:S(2)}) collective-permute-start(bf16[2,768,128]{2,1,0:T(8,128)(2,1)S(1)} %pad_maximum_fusion.2), channel_id=1, source_target_pairs={{0,16},{4,12},{8,24},{12,4},{16,0},{20,28},{24,8},{28,20},{1,17},{... | collective-permute-start | bytes 1179656 | tf_op jit(solution)/shard_map/ppermute | solution.py:29
  22.8 2.9 %collective-permute-done.12 = bf16[768,128]{1,0:T(8,128)(2,1)S(1)} collective-permute-done((bf16[768,128]{1,0:T(8,128)(2,1)S(1)}, bf16[768,128]{1,0:T(8,128)(2,1)S(1)}, u32[]{:S(2)}, u32[]{:S(2)}) %collective-permute-start.12) | collective-permute-done | bytes 196640 | tf_op jit(solution)/shard_map/ppermute | solution.py:29
  25.7 0.7 %collective-permute-start.13 = (bf16[1,768,128]{2,1,0:T(8,128)(2,1)S(1)}, bf16[1,768,128]{2,1,0:T(8,128)(2,1)S(1)}, u32[]{:S(2)}, u32[]{:S(2)}) collective-permute-start(bf16[1,768,128]{2,1,0:T(8,128)(2,1)S(1)} %bitcast.38), channel_id=1, source_target_pairs={{0,8},{4,20},{8,0},{12,28},{16,24},{20,4},{24,16},{28,12},{1,9},{5... | collective-permute-start | bytes 589832 | tf_op jit(solution)/shard_map/ppermute | solution.py:29
  26.5 1.4 %collective-permute-start.11 = (bf16[2,768,128]{2,1,0:T(8,128)(2,1)S(1)}, bf16[2,768,128]{2,1,0:T(8,128)(2,1)S(1)}, u32[]{:S(2)}, u32[]{:S(2)}) collective-permute-start(bf16[2,768,128]{2,1,0:T(8,128)(2,1)S(1)} %pad_maximum_fusion.4), channel_id=1, source_target_pairs={{0,16},{4,12},{8,24},{12,4},{16,0},{20,28},{24,8},{28,20},{1,17},{... | collective-permute-start | bytes 1179656 | tf_op jit(solution)/shard_map/ppermute | solution.py:29
  27.9 0.5 collective-permute-done.6
  28.5 2.4 %collective-permute-done.3 = bf16[2,768,128]{2,1,0:T(8,128)(2,1)S(1)} collective-permute-done((bf16[2,768,128]{2,1,0:T(8,128)(2,1)S(1)}, bf16[2,768,128]{2,1,0:T(8,128)(2,1)S(1)}, u32[]{:S(2)}, u32[]{:S(2)}) %collective-permute-start.3) | collective-permute-done | bytes 393248 | tf_op jit(solution)/shard_map/ppermute | solution.py:29
  30.9 1.2 %collective-permute-start.7 = (bf16[2,768,128]{2,1,0:T(8,128)(2,1)S(1)}, bf16[2,768,128]{2,1,0:T(8,128)(2,1)S(1)}, u32[]{:S(2)}, u32[]{:S(2)}) collective-permute-start(bf16[2,768,128]{2,1,0:T(8,128)(2,1)S(1)} %pad_maximum_fusion.3), channel_id=1, source_target_pairs={{0,16},{4,12},{8,24},{12,4},{16,0},{20,28},{24,8},{28,20},{1,17},{... | collective-permute-start | bytes 1179656 | tf_op jit(solution)/shard_map/ppermute | solution.py:29
  32.1 1.5 %collective-permute-done.13 = bf16[1,768,128]{2,1,0:T(8,128)(2,1)S(1)} collective-permute-done((bf16[1,768,128]{2,1,0:T(8,128)(2,1)S(1)}, bf16[1,768,128]{2,1,0:T(8,128)(2,1)S(1)}, u32[]{:S(2)}, u32[]{:S(2)}) %collective-permute-start.13) | collective-permute-done | bytes 196640 | tf_op jit(solution)/shard_map/ppermute | solution.py:29
  33.6 1.6 %collective-permute-start.15 = (bf16[2,768,128]{2,1,0:T(8,128)(2,1)S(1)}, bf16[2,768,128]{2,1,0:T(8,128)(2,1)S(1)}, u32[]{:S(2)}, u32[]{:S(2)}) collective-permute-start(bf16[2,768,128]{2,1,0:T(8,128)(2,1)S(1)} %pad_maximum_fusion.5), channel_id=1, source_target_pairs={{0,16},{4,12},{8,24},{12,4},{16,0},{20,28},{24,8},{28,20},{1,17},{... | collective-permute-start | bytes 1179656 | tf_op jit(solution)/shard_map/ppermute | solution.py:29
  35.2 0.1 pad_maximum_fusion.refs_4_
  35.5 0.6 collective-permute-start.14
  36.0 3.3 %collective-permute-done.7 = bf16[2,768,128]{2,1,0:T(8,128)(2,1)S(1)} collective-permute-done((bf16[2,768,128]{2,1,0:T(8,128)(2,1)S(1)}, bf16[2,768,128]{2,1,0:T(8,128)(2,1)S(1)}, u32[]{:S(2)}, u32[]{:S(2)}) %collective-permute-start.7) | collective-permute-done | bytes 393248 | tf_op jit(solution)/shard_map/ppermute | solution.py:29
  39.4 4.1 %collective-permute-done.15 = bf16[2,768,128]{2,1,0:T(8,128)(2,1)S(1)} collective-permute-done((bf16[2,768,128]{2,1,0:T(8,128)(2,1)S(1)}, bf16[2,768,128]{2,1,0:T(8,128)(2,1)S(1)}, u32[]{:S(2)}, u32[]{:S(2)}) %collective-permute-start.15) | collective-permute-done | bytes 393248 | tf_op jit(solution)/shard_map/ppermute | solution.py:29
  43.5 0.1 pad_maximum_fusion.1.refs_10_
  43.8 0.1 multiply_add_fusion
  44.0 2.0 %collective-permute-done.16.refs_11_ = bf16[4,768,128]{2,1,0:T(8,128)(2,1)S(1)} collective-permute-done((bf16[4,768,128]{2,1,0:T(8,128)(2,1)S(1)}, bf16[4,768,128]{2,1,0:T(8,128)(2,1)S(1)}, u32[]{:S(2)}, u32[]{:S(2)}) %collective-permute-start.16) | collective-permute-done | bytes 786464 | tf_op jit(solution)/shard_map/ppermute | solution.py:29
  46.0 9.9 %rk_steps_0.1 = (f32[2,512,128]{2,1,0:T(8,128)S(1)}, f32[2,8,128]{2,1,0:T(8,128)S(1)}, f32[2,512,128]{2,1,0:T(8,128)}, f32[2,8,128]{2,1,0:T(8,128)S(1)}) custom-call(s32[8,130]{1,0:T(8,128)S(1)} %multiply_add_fusion.1.refs_0_, s32[8,130]{1,0:T(8,128)S(1)} %get-tuple-element.24.refs_1_, s32[8,8,128]{2,1,0:T(8,128)S(1)} %bitcast.31, ...), custom_call_target="tpu_custom_call" | custom-call | flops 20971520 | bytes 16777216 | tf_op jit(solution)/shard_map/rk_steps_0/pallas_call | solution.py:166
  55.9 2.5 %collective-permute-start.18 = (f32[2,8,128]{2,1,0:T(8,128)S(1)}, f32[2,8,128]{2,1,0:T(8,128)S(1)}, u32[]{:S(2)}, u32[]{:S(2)}) collective-permute-start(f32[2,8,128]{2,1,0:T(8,128)S(1)} %get-tuple-element.23), channel_id=1, source_target_pairs={{0,28},{4,8},{8,4},{12,16},{16,12},{20,24},{24,20},{28,0},{1,29},{... | collective-permute-start | bytes 24584 | tf_op jit(solution)/shard_map/ppermute | solution.py:300
  58.4 1.5 %collective-permute-done.18.outer_ref = f32[2,8,128]{2,1,0:T(8,128)S(1)} collective-permute-done((f32[2,8,128]{2,1,0:T(8,128)S(1)}, f32[2,8,128]{2,1,0:T(8,128)S(1)}, u32[]{:S(2)}, u32[]{:S(2)}) %collective-permute-start.18) | collective-permute-done | bytes 8224 | tf_op jit(solution)/shard_map/ppermute | solution.py:300
  59.9 1.9 %stretch.1 = f32[512,128]{1,0:T(8,128)} custom-call(s32[3]{0:T(128)S(1)} %pad_add_fusion.7.flag_ref, f32[2,512,128]{2,1,0:T(8,128)S(1)} %get-tuple-element.21.flow_ref, f32[2,8,128]{2,1,0:T(8,128)S(1)} %get-tuple-element.22.edge_ref, f32[2,8,128]{2,1,0:T(8,128)S(1)} %collective-permute-done.17.inner_ref, f32[2,8,128]{2,1,0:T(8,128)S(1)} %collective-permute-done.18.outer_ref), custom_call_target="tpu_custom_call" | custom-call | tf_op jit(solution)/shard_map/stretch/pallas_call | solution.py:305
  (38 shorter events, 0.9 us)
Async XLA Ops:
  1.6 15.0 %collective-permute-start.9 = (bf16[768,128]{1,0:T(8,128)(2,1)S(1)}, bf16[768,128]{1,0:T(8,128)(2,1)S(1)}, u32[]{:S(2)}, u32[]{:S(2)}) collective-permute-start(bf16[768,128]{1,0:T(8,128)(2,1)S(1)} %bitcast.32), channel_id=1, source_target_pairs={{0,2},{1,3},{2,0},{3,1},{4,6},{5,7},{6,4},{7,5},{8,10},{9,11},{10,... | collective-permute-start | bytes 589832 | tf_op jit(solution)/shard_map/ppermute | solution.py:29
  5.7 10.9 %collective-permute-start.5 = (bf16[768,128]{1,0:T(8,128)(2,1)S(1)}, bf16[768,128]{1,0:T(8,128)(2,1)S(1)}, u32[]{:S(2)}, u32[]{:S(2)}) collective-permute-start(bf16[768,128]{1,0:T(8,128)(2,1)S(1)} %bitcast.33), channel_id=1, source_target_pairs={{0,1},{1,0},{2,3},{3,2},{4,5},{5,4},{6,7},{7,6},{8,9},{9,8},{10,11... | collective-permute-start | bytes 589832 | tf_op jit(solution)/shard_map/ppermute | solution.py:29
  7.2 5.7 %collective-permute-start = (bf16[1,768,128]{2,1,0:T(8,128)(2,1)S(1)}, bf16[1,768,128]{2,1,0:T(8,128)(2,1)S(1)}, u32[]{:S(2)}, u32[]{:S(2)}) collective-permute-start(bf16[1,768,128]{2,1,0:T(8,128)(2,1)S(1)} %bitcast.34), channel_id=1, source_target_pairs={{0,8},{4,20},{8,0},{12,28},{16,24},{20,4},{24,16},{28,12},{1,9},{5... | collective-permute-start | bytes 589832 | tf_op jit(solution)/shard_map/ppermute | solution.py:29
  12.9 8.0 %collective-permute-start.1 = (s32[3,8,128]{2,1,0:T(8,128)S(1)}, s32[3,8,128]{2,1,0:T(8,128)S(1)}, u32[]{:S(2)}, u32[]{:S(2)}) collective-permute-start(s32[3,8,128]{2,1,0:T(8,128)S(1)} %get-tuple-element.13), channel_id=1, source_target_pairs={{0,1},{1,2},{2,3},{4,5},{5,6},{6,7},{8,9},{9,10},{10,11},{12,13},{... | collective-permute-start | bytes 36872 | tf_op jit(solution)/shard_map/ppermute | solution.py:271
  15.3 7.5 %collective-permute-start.2 = (s32[3,8,128]{2,1,0:T(8,128)S(1)}, s32[3,8,128]{2,1,0:T(8,128)S(1)}, u32[]{:S(2)}, u32[]{:S(2)}) collective-permute-start(s32[3,8,128]{2,1,0:T(8,128)S(1)} %get-tuple-element.14), channel_id=1, source_target_pairs={{1,0},{2,1},{3,2},{5,4},{6,5},{7,6},{9,8},{10,9},{11,10},{13,12},{... | collective-permute-start | bytes 36872 | tf_op jit(solution)/shard_map/ppermute | solution.py:272
  16.6 9.8 %collective-permute-start.10 = (bf16[1,768,128]{2,1,0:T(8,128)(2,1)S(1)}, bf16[1,768,128]{2,1,0:T(8,128)(2,1)S(1)}, u32[]{:S(2)}, u32[]{:S(2)}) collective-permute-start(bf16[1,768,128]{2,1,0:T(8,128)(2,1)S(1)} %bitcast.41), channel_id=1, source_target_pairs={{0,8},{4,20},{8,0},{12,28},{16,24},{20,4},{24,16},{28,12},{1,9},{5... | collective-permute-start | bytes 589832 | tf_op jit(solution)/shard_map/ppermute | solution.py:29
  18.1 7.6 %collective-permute-start.12 = (bf16[768,128]{1,0:T(8,128)(2,1)S(1)}, bf16[768,128]{1,0:T(8,128)(2,1)S(1)}, u32[]{:S(2)}, u32[]{:S(2)}) collective-permute-start(bf16[768,128]{1,0:T(8,128)(2,1)S(1)} %bitcast.35), channel_id=1, source_target_pairs={{0,3},{1,2},{2,1},{3,0},{4,7},{5,6},{6,5},{7,4},{8,11},{9,10},{10,... | collective-permute-start | bytes 589832 | tf_op jit(solution)/shard_map/ppermute | solution.py:29
  20.6 7.8 %collective-permute-start.6 = (bf16[1,768,128]{2,1,0:T(8,128)(2,1)S(1)}, bf16[1,768,128]{2,1,0:T(8,128)(2,1)S(1)}, u32[]{:S(2)}, u32[]{:S(2)}) collective-permute-start(bf16[1,768,128]{2,1,0:T(8,128)(2,1)S(1)} %bitcast.44), channel_id=1, source_target_pairs={{0,8},{4,20},{8,0},{12,28},{16,24},{20,4},{24,16},{28,12},{1,9},{5... | collective-permute-start | bytes 589832 | tf_op jit(solution)/shard_map/ppermute | solution.py:29
  20.9 9.9 %collective-permute-start.3 = (bf16[2,768,128]{2,1,0:T(8,128)(2,1)S(1)}, bf16[2,768,128]{2,1,0:T(8,128)(2,1)S(1)}, u32[]{:S(2)}, u32[]{:S(2)}) collective-permute-start(bf16[2,768,128]{2,1,0:T(8,128)(2,1)S(1)} %pad_maximum_fusion.2), channel_id=1, source_target_pairs={{0,16},{4,12},{8,24},{12,4},{16,0},{20,28},{24,8},{28,20},{1,17},{... | collective-permute-start | bytes 1179656 | tf_op jit(solution)/shard_map/ppermute | solution.py:29
  25.7 7.8 %collective-permute-start.13 = (bf16[1,768,128]{2,1,0:T(8,128)(2,1)S(1)}, bf16[1,768,128]{2,1,0:T(8,128)(2,1)S(1)}, u32[]{:S(2)}, u32[]{:S(2)}) collective-permute-start(bf16[1,768,128]{2,1,0:T(8,128)(2,1)S(1)} %bitcast.38), channel_id=1, source_target_pairs={{0,8},{4,20},{8,0},{12,28},{16,24},{20,4},{24,16},{28,12},{1,9},{5... | collective-permute-start | bytes 589832 | tf_op jit(solution)/shard_map/ppermute | solution.py:29
  26.5 9.0 %collective-permute-start.11 = (bf16[2,768,128]{2,1,0:T(8,128)(2,1)S(1)}, bf16[2,768,128]{2,1,0:T(8,128)(2,1)S(1)}, u32[]{:S(2)}, u32[]{:S(2)}) collective-permute-start(bf16[2,768,128]{2,1,0:T(8,128)(2,1)S(1)} %pad_maximum_fusion.4), channel_id=1, source_target_pairs={{0,16},{4,12},{8,24},{12,4},{16,0},{20,28},{24,8},{28,20},{1,17},{... | collective-permute-start | bytes 1179656 | tf_op jit(solution)/shard_map/ppermute | solution.py:29
  30.9 8.4 %collective-permute-start.7 = (bf16[2,768,128]{2,1,0:T(8,128)(2,1)S(1)}, bf16[2,768,128]{2,1,0:T(8,128)(2,1)S(1)}, u32[]{:S(2)}, u32[]{:S(2)}) collective-permute-start(bf16[2,768,128]{2,1,0:T(8,128)(2,1)S(1)} %pad_maximum_fusion.3), channel_id=1, source_target_pairs={{0,16},{4,12},{8,24},{12,4},{16,0},{20,28},{24,8},{28,20},{1,17},{... | collective-permute-start | bytes 1179656 | tf_op jit(solution)/shard_map/ppermute | solution.py:29
  33.6 9.9 %collective-permute-start.15 = (bf16[2,768,128]{2,1,0:T(8,128)(2,1)S(1)}, bf16[2,768,128]{2,1,0:T(8,128)(2,1)S(1)}, u32[]{:S(2)}, u32[]{:S(2)}) collective-permute-start(bf16[2,768,128]{2,1,0:T(8,128)(2,1)S(1)} %pad_maximum_fusion.5), channel_id=1, source_target_pairs={{0,16},{4,12},{8,24},{12,4},{16,0},{20,28},{24,8},{28,20},{1,17},{... | collective-permute-start | bytes 1179656 | tf_op jit(solution)/shard_map/ppermute | solution.py:29
  35.3 8.5 %copy-start.1 = (s32[1,1,8,128]{3,2,1,0:T(8,128)S(1)}, s32[1,1,8,128]{3,2,1,0:T(8,128)}, u32[]{:S(2)}) copy-start(s32[1,1,8,128]{3,2,1,0:T(8,128)} %param.8) | copy-start | bytes 12292
  35.3 8.5 %copy-start.2 = (s32[1,1,8,128,1]{3,4,2,1,0:T(1,128)S(1)}, s32[1,1,8,128,1]{3,4,2,1,0:T(1,128)}, u32[]{:S(2)}) copy-start(s32[1,1,8,128,1]{3,4,2,1,0:T(1,128)} %param.7) | copy-start | bytes 12292
  35.3 10.7 %copy-start = (s32[8,512,128]{2,1,0:T(8,128)S(1)}, s32[8,512,128]{2,1,0:T(8,128)}, u32[]{:S(2)}) copy-start(s32[8,512,128]{2,1,0:T(8,128)} %refs_3_.1) | copy-start | bytes 6291460
  35.3 8.7 %collective-permute-start.4 = (bf16[4,768,128]{2,1,0:T(8,128)(2,1)S(1)}, bf16[4,768,128]{2,1,0:T(8,128)(2,1)S(1)}, u32[]{:S(2)}, u32[]{:S(2)}) collective-permute-start(bf16[4,768,128]{2,1,0:T(8,128)(2,1)S(1)} %pad_maximum_fusion.refs_4_), channel_id=1, source_target_pairs={{0,4},{4,0},{8,12},{12,8},{16,20},{20,16},{24,28},{28,24},{1,5},{5... | collective-permute-start | bytes 2359304 | tf_op jit(solution)/shard_map/ppermute | solution.py:29
  35.5 8.5 %collective-permute-start.14 = (bf16[4,768,128]{2,1,0:T(8,128)(2,1)S(1)}, bf16[4,768,128]{2,1,0:T(8,128)(2,1)S(1)}, u32[]{:S(2)}, u32[]{:S(2)}) collective-permute-start(bf16[4,768,128]{2,1,0:T(8,128)(2,1)S(1)} %constant_dynamic-update-slice_fusion.2.refs_8_), channel_id=1, source_target_pairs={{0,4},{4,0},{8,12},{12,8},{16,20},{20,16},{24,28},{28,24},{1,5},{5... | collective-permute-start | bytes 2359304 | tf_op jit(solution)/shard_map/ppermute | solution.py:29
  39.3 4.6 %collective-permute-start.8 = (bf16[4,768,128]{2,1,0:T(8,128)(2,1)S(1)}, bf16[4,768,128]{2,1,0:T(8,128)(2,1)S(1)}, u32[]{:S(2)}, u32[]{:S(2)}) collective-permute-start(bf16[4,768,128]{2,1,0:T(8,128)(2,1)S(1)} %constant_dynamic-update-slice_fusion.refs_6_), channel_id=1, source_target_pairs={{0,4},{4,0},{8,12},{12,8},{16,20},{20,16},{24,28},{28,24},{1,5},{5... | collective-permute-start | bytes 2359304 | tf_op jit(solution)/shard_map/ppermute | solution.py:29
  43.6 2.4 %collective-permute-start.16 = (bf16[4,768,128]{2,1,0:T(8,128)(2,1)S(1)}, bf16[4,768,128]{2,1,0:T(8,128)(2,1)S(1)}, u32[]{:S(2)}, u32[]{:S(2)}) collective-permute-start(bf16[4,768,128]{2,1,0:T(8,128)(2,1)S(1)} %pad_maximum_fusion.1.refs_10_), channel_id=1, source_target_pairs={{0,4},{4,0},{8,12},{12,8},{16,20},{20,16},{24,28},{28,24},{1,5},{5... | collective-permute-start | bytes 2359304 | tf_op jit(solution)/shard_map/ppermute | solution.py:29
  55.9 4.0 %collective-permute-start.18 = (f32[2,8,128]{2,1,0:T(8,128)S(1)}, f32[2,8,128]{2,1,0:T(8,128)S(1)}, u32[]{:S(2)}, u32[]{:S(2)}) collective-permute-start(f32[2,8,128]{2,1,0:T(8,128)S(1)} %get-tuple-element.23), channel_id=1, source_target_pairs={{0,28},{4,8},{8,4},{12,16},{16,12},{20,24},{24,20},{28,0},{1,29},{... | collective-permute-start | bytes 24584 | tf_op jit(solution)/shard_map/ppermute | solution.py:300
  58.4 1.5 %collective-permute-start.17 = (f32[2,8,128]{2,1,0:T(8,128)S(1)}, f32[2,8,128]{2,1,0:T(8,128)S(1)}, u32[]{:S(2)}, u32[]{:S(2)}) collective-permute-start(f32[2,8,128]{2,1,0:T(8,128)S(1)} %get-tuple-element.23), channel_id=1, source_target_pairs={{0,4},{4,0},{8,12},{12,8},{16,20},{20,16},{24,28},{28,24},{1,5},{5... | collective-permute-start | bytes 24584 | tf_op jit(solution)/shard_map/ppermute | solution.py:29

commit v3 on v2

--- a/solution.py
+++ b/solution.py
@@ -9,13 +9,18 @@
 
 GROUP_ROWS = 4
 TABLE_BYTES = 13 << 20
+EARLY = ((0, 1, 2, 3, 4, 5),)
+LATE = (6, 7)
 WAITS = {
     "z3": ("z1",),
-    "edge": ("r0.1",),
+    "edge": ("z1",),
     "r1.1": ("z1",),
     "r2.1": ("z1",),
     "r1.2": ("r0.2",),
+    "r2.2": ("z2",),
+    "c1": ("r2.1",),
     "c2": ("r3.1",),
+    "c3": ("r1.1",),
 }
 
 
@@ -70,17 +75,7 @@
     return new_x, new_y
 
 
-def steps_kernel(first, scale, step_rows, slots, has_start, last, unroll, *refs):
-    count = len(slots)
-    base_ref, grad_ref, edge_ref, cells_hbm = refs[:4]
-    pieces = refs[4 : 4 + count]
-    start_ref, start_edge = refs[4 + count : 6 + count] if has_start else (None, None)
-    rest = refs[(6 if has_start else 4) + count :]
-    flow_ref, out_edge, table, cells_ref, arrived = rest[0], rest[1], *rest[-3:]
-    out_ref, out_sides = rest[2:4] if last else (None, None)
-    steps, rows, lanes = cells_ref.shape
-    fetch = pltpu.make_async_copy(cells_hbm.at[pl.ds(first, steps)], cells_ref, arrived)
-    fetch.start()
+def widen_pieces(table, slots, pieces, first, steps, step_rows, scale):
     for slot, piece in zip(slots, pieces):
 
         def widen(part, carry, slot=slot, piece=piece):
@@ -92,10 +87,53 @@
             return carry
 
         lax.fori_loop(0, piece.shape[0] * steps, widen, 0, unroll=4)
+
+
+def widen_kernel(slots, has_table, first, steps, step_rows, scale, *refs):
+    pieces = refs[1:-1] if has_table else refs[:-1]
+    widen_pieces(refs[-1], slots, pieces, first, steps, step_rows, scale)
+
+
+def run_widen(table, height, items, first, last, step_rows, scale):
+    pieces = [item[0] for item in items]
+    slots = tuple(item[1] for item in items)
+    lanes = pieces[0].shape[-1]
+    vmem = pl.BlockSpec(memory_space=pltpu.VMEM)
+    given = [table] if table is not None else []
+    return pl.pallas_call(
+        functools.partial(
+            widen_kernel, slots, table is not None, first, last - first, step_rows, scale
+        ),
+        out_shape=jax.ShapeDtypeStruct((height, lanes), jnp.float32),
+        in_specs=[vmem] * len(given + pieces),
+        out_specs=vmem,
+        input_output_aliases={0: 0} if given else {},
+        cost_estimate=pl.CostEstimate(flops=0, bytes_accessed=8 << 20, transcendentals=0),
+        compiler_params=pltpu.CompilerParams(vmem_limit_bytes=4 << 20),
+        name=f"widen_{first}",
+    )(*given, *pieces)
+
+
+def steps_kernel(first, scale, step_rows, slots, has_table, has_start, last, unroll, *refs):
+    count = len(slots)
+    rows_ref, edge_ref, cells_hbm = refs[:3]
+    given = refs[4:] if has_table else refs[3:]
+    pieces = given[:count]
+    start_ref, start_edge = given[count : count + 2] if has_start else (None, None)
+    rest = given[count + 2 :] if has_start else given[count:]
+    table, rest = (rest[0], rest[1:]) if has_table else (rest[-4], rest)
+    flow_ref, out_edge = rest[:2]
+    out_hbm, out_sides = rest[2:4] if last else (None, None)
+    cells_ref, arrived, written = rest[-3:]
+    steps, rows, lanes = cells_ref.shape
+    fetch = pltpu.make_async_copy(cells_hbm.at[pl.ds(first, steps)], cells_ref, arrived)
+    fetch.start()
+    widen_pieces(table, slots, pieces, first, steps, step_rows, scale)
     fetch.wait()
     upper = lax.broadcasted_iota(jnp.int32, (8, lanes), 0) < GROUP_ROWS
     lane = lax.broadcasted_iota(jnp.int32, (8, lanes), 1)
     zero = jnp.zeros((8, lanes), jnp.float32)
+    groups = rows // GROUP_ROWS
 
     def begin_at(ref, row):
         return (ref[0, pl.ds(row, 8), :], ref[1, pl.ds(row, 8), :]) if has_start else (zero, zero)
@@ -104,8 +142,8 @@
         for step in range(steps):
             index = indices(step)
             sources = [
-                (ref[first + step, one] + k, ref[first + step, two] + k)
-                for ref, number in ((base_ref, 2), (grad_ref, 4))
+                (rows_ref[kind, first + step, one] + k, rows_ref[kind, first + step, two] + k)
+                for kind, number in ((0, 2), (1, 4))
                 for k in range(number)
             ]
             coeffs = []
@@ -121,19 +159,24 @@
             along_x, along_y = advance(along_x, along_y, coeffs)
         return along_x, along_y
 
+    block = 8 * unroll
+
+    def send(number):
+        part = pl.ds(pl.multiple_of(number * block, block), block)
+        return pltpu.make_async_copy(flow_ref.at[:, part], out_hbm.at[:, part], written.at[number])
+
     def tiles(number, carry):
         for inner in range(unroll):
             at = number * unroll + inner
             row = pl.multiple_of(at * 8, 8)
             start = begin_at(start_ref, row)
             end = tile(2 * at, 2 * at + 1, lambda step: cells_ref[step, pl.ds(row, 8), :], *start)
-            if last:
-                out_ref[0, pl.ds(row, 8), :], out_ref[1, pl.ds(row, 8), :] = end
             flow_ref[0, pl.ds(row, 8), :], flow_ref[1, pl.ds(row, 8), :] = end
+        if last:
+            send(number).start()
         return carry
 
-    lax.fori_loop(0, rows // 8 // unroll, tiles, 0)
-    groups = rows // GROUP_ROWS
+    lax.fori_loop(0, rows // block, tiles, 0)
     start = begin_at(start_edge, 0)
     end = tile(groups, groups + 1, lambda step: edge_ref[first + step], *start)
     out_edge[0], out_edge[1] = end
@@ -148,53 +191,60 @@
             value = jnp.take_along_axis(value, ends, axis=1, mode="promise_in_bounds")
             sides[at % 4] = jnp.where((lane & (half - 1)) == at, value, sides[at % 4])
         out_sides[part] = (sides[0] + sides[1]) + (sides[2] + sides[3])
-
-
-def run_steps(first, last, scale, step_rows, base, grad, edge_cells, cells, items, start):
+    for number in range(rows // block):
+        send(number).wait()
+
+
+def run_steps(
+    first, last, scale, step_rows, height, table_rows, edge_cells, cells, table, items, start
+):
     num_steps, rows, lanes = cells.shape
     steps = last - first
     pieces = [item[0] for item in items]
     slots = tuple(item[1] for item in items)
-    height = sum(piece.shape[0] for piece in pieces) * steps * step_rows
     vmem = pl.BlockSpec(memory_space=pltpu.VMEM)
     smem = pl.BlockSpec(memory_space=pltpu.SMEM)
-    need = height * lanes * 4 + steps * rows * lanes * 4
+    hbm = pl.BlockSpec(memory_space=pltpu.HBM)
+    need = steps * rows * lanes * 4
     small = jax.ShapeDtypeStruct((2, 8, lanes), jnp.float32)
     whole = jax.ShapeDtypeStruct((2, rows, lanes), jnp.float32)
     final = last == num_steps
     starts = list(start) if first else []
-    return pl.pallas_call(
-        functools.partial(steps_kernel, first, scale, step_rows, slots, first > 0, final, 8),
-        out_shape=(whole, small) + ((whole, small) if final else ()),
-        in_specs=[smem, smem, vmem, pl.BlockSpec(memory_space=pltpu.HBM)] + [vmem] * len(pieces + starts),
-        out_specs=(vmem,) * (4 if final else 2),
-        scratch_shapes=[
-            pltpu.VMEM((height, lanes), jnp.float32),
+    given = [table] if table is not None else []
+    shape = jax.ShapeDtypeStruct((height, lanes), jnp.float32)
+    need += 0 if given else height * lanes * 4
+    unroll = 8
+    results = pl.pallas_call(
+        functools.partial(
+            steps_kernel, first, scale, step_rows, slots, len(given) > 0, first > 0, final, unroll
+        ),
+        out_shape=(shape,) * len(given) + (whole, small) + ((whole, small) if final else ()),
+        in_specs=[smem, vmem, hbm] + [vmem] * len(given + pieces + starts),
+        out_specs=(vmem,) * len(given) + (vmem, vmem) + ((hbm, vmem) if final else ()),
+        input_output_aliases={3: 0} if given else {},
+        scratch_shapes=([] if given else [pltpu.VMEM(shape.shape, shape.dtype)])
+        + [
             pltpu.VMEM((steps, rows, lanes), jnp.int32),
             pltpu.SemaphoreType.DMA(()),
+            pltpu.SemaphoreType.DMA((rows // 8 // unroll,)),
         ],
         cost_estimate=pl.CostEstimate(
             flops=40 * steps * rows * lanes, bytes_accessed=16 << 20, transcendentals=0
         ),
-        compiler_params=pltpu.CompilerParams(vmem_limit_bytes=need + (3 << 20)),
+        compiler_params=pltpu.CompilerParams(vmem_limit_bytes=need + (4 << 20)),
         name=f"rk_steps_{first}",
-    )(base, grad, edge_cells, cells, *pieces, *starts)
-
-
-def stretch_kernel(flag_ref, flow_ref, edge_ref, inner_ref, outer_ref, out_ref):
+    )(table_rows, edge_cells, cells, *given, *pieces, *starts)
+    return results[len(given) :]
+
+
+def stretch_kernel(flow_ref, edge_ref, sides_ref, out_ref):
     _, rows, lanes = flow_ref.shape
     half = lanes // 2
     lane = lax.broadcasted_iota(jnp.int32, (8, lanes), 1)
     row = lax.broadcasted_iota(jnp.int32, (8, lanes), 0)
-    odd, lowest, highest = flag_ref[0] == 1, flag_ref[1] == 1, flag_ref[2] == 1
-    sides, south, north = [], [], []
-    for part in range(2):
-        inner, outer = inner_ref[part], outer_ref[part]
-        west, east = jnp.where(odd, inner, outer), jnp.where(odd, outer, inner)
-        sides.append(jnp.where(lane < half, east, west))
-        south.append(jnp.where(lowest, flow_ref[part, 0:1, :], edge_ref[part, 0:1, :]))
-        beyond = edge_ref[part, GROUP_ROWS : GROUP_ROWS + 1, :]
-        north.append(jnp.where(highest, flow_ref[part, rows - 1 : rows, :], beyond))
+    sides = [sides_ref[part] for part in range(2)]
+    south = [edge_ref[part, 0:1, :] for part in range(2)]
+    north = [edge_ref[part, GROUP_ROWS : GROUP_ROWS + 1, :] for part in range(2)]
     tiles = rows // 8
     for at in range(tiles):
         start = at * 8
@@ -259,11 +309,6 @@
             sent = gated(held[apart], label)
             done[label] = swap(sent, "lon", masks)
             held[apart] = jnp.concatenate([sent, done[label]])
-    items = []
-    for apart in range(n_lat):
-        other = swap(gated(held[apart], f"c{apart}"), "lon", (1,))
-        items += [(held[apart], 2 * apart * places), (other, (2 * apart + 1) * places)]
-
     def edge_of(row):
         value = jnp.stack([seed_cells[:, row, :], owners, wanted])
         return gated(value, "edge")
@@ -274,25 +319,39 @@
     owners = jnp.concatenate([owners, south[1, :, -1:], north[1, :, :1]], axis=1)
     wanted = jnp.concatenate([wanted, south[2, :, -1:], north[2, :, :1]], axis=1)
     lat_index = lax.axis_index("lat")
+    each = max(1, min(num_steps, TABLE_BYTES // (n_lon * n_lat * step_rows * lanes * 4)))
+    spans = [(first, min(first + each, num_steps)) for first in range(0, num_steps, each)]
+    slots = slot_of(owners, n_lat)
+    local = jnp.arange(num_steps, dtype=jnp.int32)[:, None]
+    rows_of = []
+    for first, last in spans:
+        row = (slots * (last - first) + local - first) * step_rows
+        rows_of.append(jnp.stack([row + 2 * wanted, row + 2 * blocks + 4 * wanted]))
+    done["rows"] = rows_of[-1]
+    items = []
+    for apart in range(n_lat):
+        other = swap(gated(held[apart], f"c{apart}"), "lon", (1,))
+        items += [(held[apart], 2 * apart * places), (other, (2 * apart + 1) * places)]
     state = None
-    slots = slot_of(owners, n_lat)
-    each = max(1, min(num_steps, TABLE_BYTES // (n_lon * n_lat * step_rows * lanes * 4)))
-    for first in range(0, num_steps, each):
-        last = min(first + each, num_steps)
-        local = jnp.arange(num_steps, dtype=jnp.int32)[:, None] - first
-        row = (slots * (last - first) + local) * step_rows
-        base = row + 2 * wanted
-        grad = row + 2 * blocks + 4 * wanted
+    for (first, last), table_rows in zip(spans, rows_of):
+        height = len(items) * places * (last - first) * step_rows
+        scale = -0.5 / num_steps
+        table = None
+        for chosen in EARLY:
+            chosen = [items[number] for number in chosen]
+            table = run_widen(table, height, chosen, first, last, step_rows, scale)
+        chosen = [items[number] for number in LATE]
         state = run_steps(
             first,
             last,
-            -0.5 / num_steps,
+            scale,
             step_rows,
-            base,
-            grad,
+            height,
+            table_rows,
             edge_cells,
             seed_cells,
-            items,
+            table,
+            chosen,
             state,
         )
     flow, edge, out, sides = state
@@ -300,16 +359,21 @@
     outer = lax.ppermute(
         sides, "lon", [(i, (i + (1 if i % 2 else -1)) % n_lon) for i in range(n_lon)]
     )
-    flags = jnp.stack([lax.axis_index("lon") % 2, lat_index == 0, lat_index == n_lat - 1])
+    south = jnp.where(lat_index == 0, flow[:, :1], edge[:, :1])
+    north = jnp.where(lat_index == n_lat - 1, flow[:, -1:], edge[:, GROUP_ROWS : GROUP_ROWS + 1])
+    edge = jnp.repeat(jnp.concatenate([south, north], axis=1), GROUP_ROWS, axis=1)
+    lane = lax.broadcasted_iota(jnp.int32, sides.shape, 2)
+    from_inner = (lane < lanes // 2) == (lax.axis_index("lon") % 2 == 0)
+    sides = jnp.where(from_inner, inner, outer)
     vmem = pl.BlockSpec(memory_space=pltpu.VMEM)
     field = pl.pallas_call(
         stretch_kernel,
         out_shape=jax.ShapeDtypeStruct((rows, lanes), jnp.float32),
-        in_specs=[pl.BlockSpec(memory_space=pltpu.SMEM)] + [vmem] * 4,
+        in_specs=[vmem] * 3,
         out_specs=vmem,
         compiler_params=pltpu.CompilerParams(vmem_limit_bytes=16 << 20),
         name="stretch",
-    )(flags.astype(jnp.int32), flow, edge, inner, outer)
+    )(flow, edge, sides)
     return (out, field)
 
 

time: 62.9 us -> 61.3 us (0.975)
  starting transfers between devices: 25.1 us -> 23.3 us
  other arithmetic: 2.19 us -> 3.54 us
    ppermute x16, waiting for transfers between devices: 19.3 us -> 16.5 us  [swap(): return lax.ppermute(value, axis, pairs)]
    pallas_call x1, Pallas kernels: 9.9 us -> 8.05 us  [run_steps(): pl.pallas_call(functools.partial(steps_kernel, first, scale, step_rows, s...]
    pallas_call x0 -> x1, Pallas kernels: none -> 1.75 us  [run_widen(): pl.pallas_call(functools.partial(widen_kernel, slots, table is not None,...]
    ppermute x1, waiting for transfers between devices: 0.01 us -> 1.44 us  [body(): lax.ppermute(edge_of(-1), 'lat', [(i, i + 1) for i in range(n_lat - 1)])]
    add x2, other arithmetic: 0.18 us -> 1.56 us  [body(): rows_of.append(jnp.stack([row + 2 * wanted, row + 2 * blocks + 4 * wanted]))]
    ppermute x1, starting transfers between devices: 2.5 us -> 1.13 us  [body(): lax.ppermute(sides, 'lon', [(i, (i + (1 if i % 2 else -1)) % n_lon) for i...]
    ppermute x1, waiting for transfers between devices: 1.46 us -> 2.82 us  [body(): lax.ppermute(sides, 'lon', [(i, (i + (1 if i % 2 else -1)) % n_lon) for i...]
  transfers between devices with their start and end apart: 19 -> 19, of which waited for: 10 -> 7; matrix products, arithmetic and copies ran while one was open for 4% -> 6% of each run, Pallas kernels for 0% -> 3%
where the time goes in v3:
time: 61.3 us; the launch traced here: 60.7 us
  starting transfers between devices  23.3 us (38%)
  waiting for transfers between devices  20.8 us (34%)
  Pallas kernels  11.2 us (18%)
  other arithmetic  3.54 us (6%)
  local copies, waits for them, and re-layouts  1.04 us (2%)
  between operations  0.85 us (1%)
    ppermute x16, starting transfers between devices, swap(): return lax.ppermute(value, axis, pairs)  19 us
    ppermute x16, waiting for transfers between devices, swap(): return lax.ppermute(value, axis, pairs)  16.5 us
    pallas_call x1, Pallas kernels, run_steps(): pl.pallas_call(functools.partial(steps_kernel, first, scale, step_rows, s...  8.05 us
    ppermute x1, waiting for transfers between devices, body(): lax.ppermute(sides, 'lon', [(i, (i + (1 if i % 2 else -1)) % n_lon) for i...  2.82 us
    ppermute x1, starting transfers between devices, body(): lax.ppermute(edge_of(-1), 'lat', [(i, i + 1) for i in range(n_lat - 1)])  1.9 us
    pallas_call x1, Pallas kernels, run_widen(): pl.pallas_call(functools.partial(widen_kernel, slots, table is not None,...  1.75 us
    add x2, other arithmetic, body(): rows_of.append(jnp.stack([row + 2 * wanted, row + 2 * blocks + 4 * wanted]))  1.56 us
    ppermute x1, waiting for transfers between devices, body(): lax.ppermute(edge_of(-1), 'lat', [(i, i + 1) for i in range(n_lat - 1)])  1.44 us
  transfers between devices with their start and end apart: 19, of which 7 were waited for; matrix products, arithmetic and copies ran while one was open for 6% of the time, Pallas kernels for 3%

profile of v3, /device:TPU:0, one launch (start us, length us, event | category | flops | bytes accessed | tf_op | source)
XLA Modules:
  0.0 60.7 jit_solution(14069320367065836980)
XLA Ops:
  0.6 0.9 %pad_maximum_fusion.6 = bf16[8,96,128]{2,1,0:T(8,128)(2,1)S(1)} fusion(bf16[8,64,128]{2,1,0:T(8,128)(2,1)} %bitcast.36, bf16[8,32,128]{2,1,0:T(8,128)(2,1)} %bitcast.37), kind=kLoop, calls=%fused_computation.6 | loop fusion | flops 393216 | bytes 393216 | tf_op jit(solution)/shard_map/concatenate | solution.py:285
  1.6 3.1 %collective-permute-start = (bf16[768,128]{1,0:T(8,128)(2,1)S(1)}, bf16[768,128]{1,0:T(8,128)(2,1)S(1)}, u32[]{:S(2)}, u32[]{:S(2)}) collective-permute-start(bf16[768,128]{1,0:T(8,128)(2,1)S(1)} %bitcast.23), channel_id=1, source_target_pairs={{0,1},{1,0},{2,3},{3,2},{4,5},{5,4},{6,7},{7,6},{8,9},{9,8},{10,11... | collective-permute-start | bytes 589832 | tf_op jit(solution)/shard_map/ppermute | solution.py:34
  4.6 2.6 %collective-permute-start.8 = (bf16[768,128]{1,0:T(8,128)(2,1)S(1)}, bf16[768,128]{1,0:T(8,128)(2,1)S(1)}, u32[]{:S(2)}, u32[]{:S(2)}) collective-permute-start(bf16[768,128]{1,0:T(8,128)(2,1)S(1)} %bitcast.24), channel_id=1, source_target_pairs={{0,2},{1,3},{2,0},{3,1},{4,6},{5,7},{6,4},{7,5},{8,10},{9,11},{10,... | collective-permute-start | bytes 589832 | tf_op jit(solution)/shard_map/ppermute | solution.py:34
  7.2 1.5 %collective-permute-start.3 = (bf16[1,768,128]{2,1,0:T(8,128)(2,1)S(1)}, bf16[1,768,128]{2,1,0:T(8,128)(2,1)S(1)}, u32[]{:S(2)}, u32[]{:S(2)}) collective-permute-start(bf16[1,768,128]{2,1,0:T(8,128)(2,1)S(1)} %bitcast.25), channel_id=1, source_target_pairs={{0,8},{4,20},{8,0},{12,28},{16,24},{20,4},{24,16},{28,12},{1,9},{5... | collective-permute-start | bytes 589832 | tf_op jit(solution)/shard_map/ppermute | solution.py:34
  8.7 0.8 %fusion.11 = (s32[8,1,128]{2,1,0:T(1,128)S(1)}, s32[8,1,128]{2,1,0:T(1,128)S(1)}) fusion(s32[8,512,128]{2,1,0:T(8,128)} %refs_2_.1), kind=kLoop, calls=%fused_computation.48 | loop fusion | bytes 16384 | tf_op jit(solution)/shard_map/slice | solution.py:313
  9.5 0.7 %pad_add_fusion.2 = (s32[3,8,128]{2,1,0:T(8,128)S(1)}, s32[3,8,128]{2,1,0:T(8,128)S(1)}) fusion(s32[1,8,128]{2,1,0:T(8,128)} %bitcast.38, s32[1,8,128]{2,1,0:T(8,128)} %bitcast.43, s32[1,8,128]{2,1,0:T(8,128)S(1)} %bitcast.41, s32[1,8,128]{2,1,0:T(8,128)S(1)} %bitcast.42), kind=kLoop, calls=%fused_computation.9 | loop fusion | flops 12288 | bytes 40960 | tf_op jit(solution)/shard_map/stack | solution.py:313
  10.2 3.4 %collective-permute-done = bf16[768,128]{1,0:T(8,128)(2,1)S(1)} collective-permute-done((bf16[768,128]{1,0:T(8,128)(2,1)S(1)}, bf16[768,128]{1,0:T(8,128)(2,1)S(1)}, u32[]{:S(2)}, u32[]{:S(2)}) %collective-permute-start) | collective-permute-done | bytes 196640 | tf_op jit(solution)/shard_map/ppermute | solution.py:34
  13.6 1.7 %collective-permute-start.6 = (bf16[1,768,128]{2,1,0:T(8,128)(2,1)S(1)}, bf16[1,768,128]{2,1,0:T(8,128)(2,1)S(1)}, u32[]{:S(2)}, u32[]{:S(2)}) collective-permute-start(bf16[1,768,128]{2,1,0:T(8,128)(2,1)S(1)} %bitcast.32), channel_id=1, source_target_pairs={{0,8},{4,20},{8,0},{12,28},{16,24},{20,4},{24,16},{28,12},{1,9},{5... | collective-permute-start | bytes 589832 | tf_op jit(solution)/shard_map/ppermute | solution.py:34
  15.3 1.3 %collective-permute-start.2 = (s32[3,8,128]{2,1,0:T(8,128)S(1)}, s32[3,8,128]{2,1,0:T(8,128)S(1)}, u32[]{:S(2)}, u32[]{:S(2)}) collective-permute-start(s32[3,8,128]{2,1,0:T(8,128)S(1)} %get-tuple-element.17), channel_id=1, source_target_pairs={{1,0},{2,1},{3,2},{5,4},{6,5},{7,6},{9,8},{10,9},{11,10},{13,12},{... | collective-permute-start | bytes 36872 | tf_op jit(solution)/shard_map/ppermute | solution.py:317
  16.6 1.6 %collective-permute-start.4 = (bf16[2,768,128]{2,1,0:T(8,128)(2,1)S(1)}, bf16[2,768,128]{2,1,0:T(8,128)(2,1)S(1)}, u32[]{:S(2)}, u32[]{:S(2)}) collective-permute-start(bf16[2,768,128]{2,1,0:T(8,128)(2,1)S(1)} %pad_maximum_fusion.2), channel_id=1, source_target_pairs={{0,16},{4,12},{8,24},{12,4},{16,0},{20,28},{24,8},{28,20},{1,17},{... | collective-permute-start | bytes 1179656 | tf_op jit(solution)/shard_map/ppermute | solution.py:34
  18.2 0.5 collective-permute-start.9
  18.8 2.6 %collective-permute-start.12 = (bf16[768,128]{1,0:T(8,128)(2,1)S(1)}, bf16[768,128]{1,0:T(8,128)(2,1)S(1)}, u32[]{:S(2)}, u32[]{:S(2)}) collective-permute-start(bf16[768,128]{1,0:T(8,128)(2,1)S(1)} %bitcast.27), channel_id=1, source_target_pairs={{0,3},{1,2},{2,1},{3,0},{4,7},{5,6},{6,5},{7,4},{8,11},{9,10},{10,... | collective-permute-start | bytes 589832 | tf_op jit(solution)/shard_map/ppermute | solution.py:34
  21.4 1.9 %collective-permute-start.1 = (s32[3,8,128]{2,1,0:T(8,128)S(1)}, s32[3,8,128]{2,1,0:T(8,128)S(1)}, u32[]{:S(2)}, u32[]{:S(2)}) collective-permute-start(s32[3,8,128]{2,1,0:T(8,128)S(1)} %get-tuple-element.16), channel_id=1, source_target_pairs={{0,1},{1,2},{2,3},{4,5},{5,6},{6,7},{8,9},{9,10},{10,11},{12,13},{... | collective-permute-start | bytes 36872 | tf_op jit(solution)/shard_map/ppermute | solution.py:316
  23.3 1.4 %collective-permute-done.1 = s32[3,8,128]{2,1,0:T(8,128)S(1)} collective-permute-done((s32[3,8,128]{2,1,0:T(8,128)S(1)}, s32[3,8,128]{2,1,0:T(8,128)S(1)}, u32[]{:S(2)}, u32[]{:S(2)}) %collective-permute-start.1) | collective-permute-done | bytes 12320 | tf_op jit(solution)/shard_map/ppermute | solution.py:316
  24.8 1.3 %collective-permute-done.9 = bf16[1,768,128]{2,1,0:T(8,128)(2,1)S(1)} collective-permute-done((bf16[1,768,128]{2,1,0:T(8,128)(2,1)S(1)}, bf16[1,768,128]{2,1,0:T(8,128)(2,1)S(1)}, u32[]{:S(2)}, u32[]{:S(2)}) %collective-permute-start.9) | collective-permute-done | bytes 196640 | tf_op jit(solution)/shard_map/ppermute | solution.py:34
  26.1 1.2 %collective-permute-start.11 = (bf16[2,768,128]{2,1,0:T(8,128)(2,1)S(1)}, bf16[2,768,128]{2,1,0:T(8,128)(2,1)S(1)}, u32[]{:S(2)}, u32[]{:S(2)}) collective-permute-start(bf16[2,768,128]{2,1,0:T(8,128)(2,1)S(1)} %pad_maximum_fusion.4), channel_id=1, source_target_pairs={{0,16},{4,12},{8,24},{12,4},{16,0},{20,28},{24,8},{28,20},{1,17},{... | collective-permute-start | bytes 1179656 | tf_op jit(solution)/shard_map/ppermute | solution.py:34
  27.4 1.5 %collective-permute-start.13 = (bf16[1,768,128]{2,1,0:T(8,128)(2,1)S(1)}, bf16[1,768,128]{2,1,0:T(8,128)(2,1)S(1)}, u32[]{:S(2)}, u32[]{:S(2)}) collective-permute-start(bf16[1,768,128]{2,1,0:T(8,128)(2,1)S(1)} %bitcast.29), channel_id=1, source_target_pairs={{0,8},{4,20},{8,0},{12,28},{16,24},{20,4},{24,16},{28,12},{1,9},{5... | collective-permute-start | bytes 589832 | tf_op jit(solution)/shard_map/ppermute | solution.py:34
  29.0 0.4 collective-permute-start.7
  29.4 5.8 %collective-permute-done.13 = bf16[1,768,128]{2,1,0:T(8,128)(2,1)S(1)} collective-permute-done((bf16[1,768,128]{2,1,0:T(8,128)(2,1)S(1)}, bf16[1,768,128]{2,1,0:T(8,128)(2,1)S(1)}, u32[]{:S(2)}, u32[]{:S(2)}) %collective-permute-start.13) | collective-permute-done | bytes 196640 | tf_op jit(solution)/shard_map/ppermute | solution.py:34
  35.2 0.9 %collective-permute-start.15 = (bf16[2,768,128]{2,1,0:T(8,128)(2,1)S(1)}, bf16[2,768,128]{2,1,0:T(8,128)(2,1)S(1)}, u32[]{:S(2)}, u32[]{:S(2)}) collective-permute-start(bf16[2,768,128]{2,1,0:T(8,128)(2,1)S(1)} %pad_maximum_fusion.5), channel_id=1, source_target_pairs={{0,16},{4,12},{8,24},{12,4},{16,0},{20,28},{24,8},{28,20},{1,17},{... | collective-permute-start | bytes 1179656 | tf_op jit(solution)/shard_map/ppermute | solution.py:34
  36.2 0.1 pad_maximum_fusion.refs_0_
  36.4 0.6 collective-permute-start.14
  37.0 1.2 %collective-permute-done.7 = bf16[2,768,128]{2,1,0:T(8,128)(2,1)S(1)} collective-permute-done((bf16[2,768,128]{2,1,0:T(8,128)(2,1)S(1)}, bf16[2,768,128]{2,1,0:T(8,128)(2,1)S(1)}, u32[]{:S(2)}, u32[]{:S(2)}) %collective-permute-start.7) | collective-permute-done | bytes 393248 | tf_op jit(solution)/shard_map/ppermute | solution.py:34
  38.3 4.8 %collective-permute-done.15 = bf16[2,768,128]{2,1,0:T(8,128)(2,1)S(1)} collective-permute-done((bf16[2,768,128]{2,1,0:T(8,128)(2,1)S(1)}, bf16[2,768,128]{2,1,0:T(8,128)(2,1)S(1)}, u32[]{:S(2)}, u32[]{:S(2)}) %collective-permute-start.15) | collective-permute-done | bytes 393248 | tf_op jit(solution)/shard_map/ppermute | solution.py:34
  43.3 0.8 %multiply_add_fusion.1 = (s32[1,8,130]{2,1,0:T(8,128)S(1)}, s32[1,8,130]{2,1,0:T(8,128)S(1)}) fusion(s32[1,8,1]{2,1,0:T(8,128)S(1)} %get-tuple-element.39, s32[1,8,1]{2,1,0:T(8,128)S(1)} %get-tuple-element.37, s32[1,8,128]{2,1,0:T(8,128)} %bitcast.39, s32[]{:T(128)S(6)} %axis_index.33, s32[]{:T(128)S(6)} %axis_index.14, ...), kind=kLoop, calls=%fused_computation.33 | loop fusion | flops 49920 | bytes 16648 | tf_op jit(solution)/shard_map/add | solution.py:329
  44.1 0.8 %multiply_add_fusion = s32[1,8,130]{2,1,0:T(8,128)S(1)} fusion(s32[1,8,130]{2,1,0:T(8,128)S(1)} %get-tuple-element.31, s32[1,8,1]{2,1,0:T(8,128)S(1)} %get-tuple-element.39, s32[1,8,1]{2,1,0:T(8,128)S(1)} %get-tuple-element.37, s32[1,8,128]{2,1,0:T(8,128)} %bitcast.40), kind=kLoop, calls=%fused_computation.32 | loop fusion | flops 5200 | bytes 12480 | tf_op jit(solution)/shard_map/add | solution.py:329
  44.9 1.7 %widen_0.1.refs_3_ = f32[24576,128]{1,0:T(8,128)S(1)} custom-call(bf16[4,768,128]{2,1,0:T(8,128)(2,1)S(1)} %pad_maximum_fusion.refs_0_, bf16[4,768,128]{2,1,0:T(8,128)(2,1)S(1)} %collective-permute-done.5.refs_1_, bf16[4,768,128]{2,1,0:T(8,128)(2,1)S(1)} %constant_dynamic-update-slice_fusion.refs_2_, ...), custom_call_target="tpu_custom_call" | custom-call | bytes 8388608 | tf_op jit(solution)/shard_map/widen_0/pallas_call | solution.py:103
  46.7 8.0 %rk_steps_0.1 = (f32[24576,128]{1,0:T(8,128)S(1)}, f32[2,512,128]{2,1,0:T(8,128)S(1)}, f32[2,8,128]{2,1,0:T(8,128)S(1)}, f32[2,512,128]{2,1,0:T(8,128)}, f32[2,8,128]{2,1,0:T(8,128)S(1)}) custom-call(s32[2,8,130]{2,1,0:T(8,128)S(1)} %pad_add_fusion.refs_0_, s32[8,8,128]{2,1,0:T(8,128)S(1)} %bitcast.21, ...), custom_call_target="tpu_custom_call", output_to_operand_aliasing={{0}: (3, {})} | custom-call | flops 20971520 | bytes 16777216 | tf_op jit(solution)/shard_map/rk_steps_0/pallas_call | solution.py:217
  54.8 0.6 collective-permute-start.17
  55.3 1.1 %collective-permute-start.18 = (f32[2,8,128]{2,1,0:T(8,128)S(1)}, f32[2,8,128]{2,1,0:T(8,128)S(1)}, u32[]{:S(2)}, u32[]{:S(2)}) collective-permute-start(f32[2,8,128]{2,1,0:T(8,128)S(1)} %get-tuple-element.29), channel_id=1, source_target_pairs={{0,28},{4,8},{8,4},{12,16},{16,12},{20,24},{24,20},{28,0},{1,29},{... | collective-permute-start | bytes 24584 | tf_op jit(solution)/shard_map/ppermute | solution.py:359
  56.5 2.8 %collective-permute-done.18 = f32[2,8,128]{2,1,0:T(8,128)S(1)} collective-permute-done((f32[2,8,128]{2,1,0:T(8,128)S(1)}, f32[2,8,128]{2,1,0:T(8,128)S(1)}, u32[]{:S(2)}, u32[]{:S(2)}) %collective-permute-start.18) | collective-permute-done | bytes 8224 | tf_op jit(solution)/shard_map/ppermute | solution.py:359
  59.3 1.4 %stretch.1 = f32[512,128]{1,0:T(8,128)} custom-call(f32[2,512,128]{2,1,0:T(8,128)S(1)} %get-tuple-element.27.flow_ref, f32[2,8,128]{2,1,0:T(8,128)S(1)} %bitcast.22, f32[2,8,128]{2,1,0:T(8,128)S(1)} %broadcast_select_fusion.sides_ref), custom_call_target="tpu_custom_call" | custom-call | tf_op jit(solution)/shard_map/stretch/pallas_call | solution.py:369
  (39 shorter events, 0.8 us)
Async XLA Ops:
  1.6 12.1 %collective-permute-start = (bf16[768,128]{1,0:T(8,128)(2,1)S(1)}, bf16[768,128]{1,0:T(8,128)(2,1)S(1)}, u32[]{:S(2)}, u32[]{:S(2)}) collective-permute-start(bf16[768,128]{1,0:T(8,128)(2,1)S(1)} %bitcast.23), channel_id=1, source_target_pairs={{0,1},{1,0},{2,3},{3,2},{4,5},{5,4},{6,7},{7,6},{8,9},{9,8},{10,11... | collective-permute-start | bytes 589832 | tf_op jit(solution)/shard_map/ppermute | solution.py:34
  4.6 13.6 %collective-permute-start.8 = (bf16[768,128]{1,0:T(8,128)(2,1)S(1)}, bf16[768,128]{1,0:T(8,128)(2,1)S(1)}, u32[]{:S(2)}, u32[]{:S(2)}) collective-permute-start(bf16[768,128]{1,0:T(8,128)(2,1)S(1)} %bitcast.24), channel_id=1, source_target_pairs={{0,2},{1,3},{2,0},{3,1},{4,6},{5,7},{6,4},{7,5},{8,10},{9,11},{10,... | collective-permute-start | bytes 589832 | tf_op jit(solution)/shard_map/ppermute | solution.py:34
  7.2 9.4 %collective-permute-start.3 = (bf16[1,768,128]{2,1,0:T(8,128)(2,1)S(1)}, bf16[1,768,128]{2,1,0:T(8,128)(2,1)S(1)}, u32[]{:S(2)}, u32[]{:S(2)}) collective-permute-start(bf16[1,768,128]{2,1,0:T(8,128)(2,1)S(1)} %bitcast.25), channel_id=1, source_target_pairs={{0,8},{4,20},{8,0},{12,28},{16,24},{20,4},{24,16},{28,12},{1,9},{5... | collective-permute-start | bytes 589832 | tf_op jit(solution)/shard_map/ppermute | solution.py:34
  13.6 15.3 %collective-permute-start.6 = (bf16[1,768,128]{2,1,0:T(8,128)(2,1)S(1)}, bf16[1,768,128]{2,1,0:T(8,128)(2,1)S(1)}, u32[]{:S(2)}, u32[]{:S(2)}) collective-permute-start(bf16[1,768,128]{2,1,0:T(8,128)(2,1)S(1)} %bitcast.32), channel_id=1, source_target_pairs={{0,8},{4,20},{8,0},{12,28},{16,24},{20,4},{24,16},{28,12},{1,9},{5... | collective-permute-start | bytes 589832 | tf_op jit(solution)/shard_map/ppermute | solution.py:34
  15.3 6.1 %collective-permute-start.2 = (s32[3,8,128]{2,1,0:T(8,128)S(1)}, s32[3,8,128]{2,1,0:T(8,128)S(1)}, u32[]{:S(2)}, u32[]{:S(2)}) collective-permute-start(s32[3,8,128]{2,1,0:T(8,128)S(1)} %get-tuple-element.17), channel_id=1, source_target_pairs={{1,0},{2,1},{3,2},{5,4},{6,5},{7,6},{9,8},{10,9},{11,10},{13,12},{... | collective-permute-start | bytes 36872 | tf_op jit(solution)/shard_map/ppermute | solution.py:317
  16.6 12.3 %collective-permute-start.4 = (bf16[2,768,128]{2,1,0:T(8,128)(2,1)S(1)}, bf16[2,768,128]{2,1,0:T(8,128)(2,1)S(1)}, u32[]{:S(2)}, u32[]{:S(2)}) collective-permute-start(bf16[2,768,128]{2,1,0:T(8,128)(2,1)S(1)} %pad_maximum_fusion.2), channel_id=1, source_target_pairs={{0,16},{4,12},{8,24},{12,4},{16,0},{20,28},{24,8},{28,20},{1,17},{... | collective-permute-start | bytes 1179656 | tf_op jit(solution)/shard_map/ppermute | solution.py:34
  18.2 7.8 %collective-permute-start.9 = (bf16[1,768,128]{2,1,0:T(8,128)(2,1)S(1)}, bf16[1,768,128]{2,1,0:T(8,128)(2,1)S(1)}, u32[]{:S(2)}, u32[]{:S(2)}) collective-permute-start(bf16[1,768,128]{2,1,0:T(8,128)(2,1)S(1)} %bitcast.34), channel_id=1, source_target_pairs={{0,8},{4,20},{8,0},{12,28},{16,24},{20,4},{24,16},{28,12},{1,9},{5... | collective-permute-start | bytes 589832 | tf_op jit(solution)/shard_map/ppermute | solution.py:34
  18.8 8.6 %collective-permute-start.12 = (bf16[768,128]{1,0:T(8,128)(2,1)S(1)}, bf16[768,128]{1,0:T(8,128)(2,1)S(1)}, u32[]{:S(2)}, u32[]{:S(2)}) collective-permute-start(bf16[768,128]{1,0:T(8,128)(2,1)S(1)} %bitcast.27), channel_id=1, source_target_pairs={{0,3},{1,2},{2,1},{3,0},{4,7},{5,6},{6,5},{7,4},{8,11},{9,10},{10,... | collective-permute-start | bytes 589832 | tf_op jit(solution)/shard_map/ppermute | solution.py:34
  21.4 3.4 %collective-permute-start.1 = (s32[3,8,128]{2,1,0:T(8,128)S(1)}, s32[3,8,128]{2,1,0:T(8,128)S(1)}, u32[]{:S(2)}, u32[]{:S(2)}) collective-permute-start(s32[3,8,128]{2,1,0:T(8,128)S(1)} %get-tuple-element.16), channel_id=1, source_target_pairs={{0,1},{1,2},{2,3},{4,5},{5,6},{6,7},{8,9},{9,10},{10,11},{12,13},{... | collective-permute-start | bytes 36872 | tf_op jit(solution)/shard_map/ppermute | solution.py:316
  26.1 10.2 %collective-permute-start.11 = (bf16[2,768,128]{2,1,0:T(8,128)(2,1)S(1)}, bf16[2,768,128]{2,1,0:T(8,128)(2,1)S(1)}, u32[]{:S(2)}, u32[]{:S(2)}) collective-permute-start(bf16[2,768,128]{2,1,0:T(8,128)(2,1)S(1)} %pad_maximum_fusion.4), channel_id=1, source_target_pairs={{0,16},{4,12},{8,24},{12,4},{16,0},{20,28},{24,8},{28,20},{1,17},{... | collective-permute-start | bytes 1179656 | tf_op jit(solution)/shard_map/ppermute | solution.py:34
  27.4 19.3 %copy-start = (s32[8,512,128]{2,1,0:T(8,128)S(1)}, s32[8,512,128]{2,1,0:T(8,128)}, u32[]{:S(2)}) copy-start(s32[8,512,128]{2,1,0:T(8,128)} %refs_2_.1) | copy-start | bytes 6291460
  27.4 7.8 %collective-permute-start.13 = (bf16[1,768,128]{2,1,0:T(8,128)(2,1)S(1)}, bf16[1,768,128]{2,1,0:T(8,128)(2,1)S(1)}, u32[]{:S(2)}, u32[]{:S(2)}) collective-permute-start(bf16[1,768,128]{2,1,0:T(8,128)(2,1)S(1)} %bitcast.29), channel_id=1, source_target_pairs={{0,8},{4,20},{8,0},{12,28},{16,24},{20,4},{24,16},{28,12},{1,9},{5... | collective-permute-start | bytes 589832 | tf_op jit(solution)/shard_map/ppermute | solution.py:34
  29.0 9.2 %collective-permute-start.7 = (bf16[2,768,128]{2,1,0:T(8,128)(2,1)S(1)}, bf16[2,768,128]{2,1,0:T(8,128)(2,1)S(1)}, u32[]{:S(2)}, u32[]{:S(2)}) collective-permute-start(bf16[2,768,128]{2,1,0:T(8,128)(2,1)S(1)} %pad_maximum_fusion.3), channel_id=1, source_target_pairs={{0,16},{4,12},{8,24},{12,4},{16,0},{20,28},{24,8},{28,20},{1,17},{... | collective-permute-start | bytes 1179656 | tf_op jit(solution)/shard_map/ppermute | solution.py:34
  35.2 7.8 %collective-permute-start.15 = (bf16[2,768,128]{2,1,0:T(8,128)(2,1)S(1)}, bf16[2,768,128]{2,1,0:T(8,128)(2,1)S(1)}, u32[]{:S(2)}, u32[]{:S(2)}) collective-permute-start(bf16[2,768,128]{2,1,0:T(8,128)(2,1)S(1)} %pad_maximum_fusion.5), channel_id=1, source_target_pairs={{0,16},{4,12},{8,24},{12,4},{16,0},{20,28},{24,8},{28,20},{1,17},{... | collective-permute-start | bytes 1179656 | tf_op jit(solution)/shard_map/ppermute | solution.py:34
  36.2 8.7 %collective-permute-start.5 = (bf16[4,768,128]{2,1,0:T(8,128)(2,1)S(1)}, bf16[4,768,128]{2,1,0:T(8,128)(2,1)S(1)}, u32[]{:S(2)}, u32[]{:S(2)}) collective-permute-start(bf16[4,768,128]{2,1,0:T(8,128)(2,1)S(1)} %pad_maximum_fusion.refs_0_), channel_id=1, source_target_pairs={{0,4},{4,0},{8,12},{12,8},{16,20},{20,16},{24,28},{28,24},{1,5},{5... | collective-permute-start | bytes 2359304 | tf_op jit(solution)/shard_map/ppermute | solution.py:34
  36.4 8.5 %collective-permute-start.14 = (bf16[4,768,128]{2,1,0:T(8,128)(2,1)S(1)}, bf16[4,768,128]{2,1,0:T(8,128)(2,1)S(1)}, u32[]{:S(2)}, u32[]{:S(2)}) collective-permute-start(bf16[4,768,128]{2,1,0:T(8,128)(2,1)S(1)} %constant_dynamic-update-slice_fusion.2.refs_4_), channel_id=1, source_target_pairs={{0,4},{4,0},{8,12},{12,8},{16,20},{20,16},{24,28},{28,24},{1,5},{5... | collective-permute-start | bytes 2359304 | tf_op jit(solution)/shard_map/ppermute | solution.py:34
  38.2 6.7 %collective-permute-start.10 = (bf16[4,768,128]{2,1,0:T(8,128)(2,1)S(1)}, bf16[4,768,128]{2,1,0:T(8,128)(2,1)S(1)}, u32[]{:S(2)}, u32[]{:S(2)}) collective-permute-start(bf16[4,768,128]{2,1,0:T(8,128)(2,1)S(1)} %constant_dynamic-update-slice_fusion.refs_2_), channel_id=1, source_target_pairs={{0,4},{4,0},{8,12},{12,8},{16,20},{20,16},{24,28},{28,24},{1,5},{5... | collective-permute-start | bytes 2359304 | tf_op jit(solution)/shard_map/ppermute | solution.py:34
  43.2 3.5 %collective-permute-start.16 = (bf16[4,768,128]{2,1,0:T(8,128)(2,1)S(1)}, bf16[4,768,128]{2,1,0:T(8,128)(2,1)S(1)}, u32[]{:S(2)}, u32[]{:S(2)}) collective-permute-start(bf16[4,768,128]{2,1,0:T(8,128)(2,1)S(1)} %pad_maximum_fusion.1.refs_4_), channel_id=1, source_target_pairs={{0,4},{4,0},{8,12},{12,8},{16,20},{20,16},{24,28},{28,24},{1,5},{5... | collective-permute-start | bytes 2359304 | tf_op jit(solution)/shard_map/ppermute | solution.py:34
  54.8 1.7 %collective-permute-start.17 = (f32[2,8,128]{2,1,0:T(8,128)S(1)}, f32[2,8,128]{2,1,0:T(8,128)S(1)}, u32[]{:S(2)}, u32[]{:S(2)}) collective-permute-start(f32[2,8,128]{2,1,0:T(8,128)S(1)} %get-tuple-element.29), channel_id=1, source_target_pairs={{0,4},{4,0},{8,12},{12,8},{16,20},{20,16},{24,28},{28,24},{1,5},{5... | collective-permute-start | bytes 24584 | tf_op jit(solution)/shard_map/ppermute | solution.py:34
  55.3 4.0 %collective-permute-start.18 = (f32[2,8,128]{2,1,0:T(8,128)S(1)}, f32[2,8,128]{2,1,0:T(8,128)S(1)}, u32[]{:S(2)}, u32[]{:S(2)}) collective-permute-start(f32[2,8,128]{2,1,0:T(8,128)S(1)} %get-tuple-element.29), channel_id=1, source_target_pairs={{0,28},{4,8},{8,4},{12,16},{16,12},{20,24},{24,20},{28,0},{1,29},{... | collective-permute-start | bytes 24584 | tf_op jit(solution)/shard_map/ppermute | solution.py:359

commit v4 on v3

--- a/solution.py
+++ b/solution.py
@@ -20,7 +20,6 @@
     "r2.2": ("z2",),
     "c1": ("r2.1",),
     "c2": ("r3.1",),
-    "c3": ("r1.1",),
 }
 
 
@@ -134,6 +133,8 @@
     lane = lax.broadcasted_iota(jnp.int32, (8, lanes), 1)
     zero = jnp.zeros((8, lanes), jnp.float32)
     groups = rows // GROUP_ROWS
+    blocks = step_rows // 6
+    shift = (blocks - 1).bit_length()
 
     def begin_at(ref, row):
         return (ref[0, pl.ds(row, 8), :], ref[1, pl.ds(row, 8), :]) if has_start else (zero, zero)
@@ -141,8 +142,14 @@
     def tile(one, two, indices, along_x, along_y):
         for step in range(steps):
             index = indices(step)
+            places = []
+            for which in (one, two):
+                code = rows_ref[first + step, which]
+                block = code & ((1 << shift) - 1)
+                start = lax.shift_right_logical(code, shift)
+                places.append((start + 2 * block, start + 2 * blocks + 4 * block))
             sources = [
-                (rows_ref[kind, first + step, one] + k, rows_ref[kind, first + step, two] + k)
+                (places[0][kind] + k, places[1][kind] + k)
                 for kind, number in ((0, 2), (1, 4))
                 for k in range(number)
             ]
@@ -326,8 +333,7 @@
     rows_of = []
     for first, last in spans:
         row = (slots * (last - first) + local - first) * step_rows
-        rows_of.append(jnp.stack([row + 2 * wanted, row + 2 * blocks + 4 * wanted]))
-    done["rows"] = rows_of[-1]
+        rows_of.append((row << (blocks - 1).bit_length()) + wanted)
     items = []
     for apart in range(n_lat):
         other = swap(gated(held[apart], f"c{apart}"), "lon", (1,))

time: 61.3 us -> 60.1 us (0.980)
  other arithmetic: 3.54 us -> 2.77 us
    ppermute x16, waiting for transfers between devices: 16.5 us -> 18 us  [swap(): return lax.ppermute(value, axis, pairs)]
    ppermute x1, waiting for transfers between devices: 1.44 us -> 0.01 us  [body(): lax.ppermute(edge_of(-1), 'lat', [(i, i + 1) for i in range(n_lat - 1)])]
    add x2 -> x1, other arithmetic: 1.56 us -> 0.8 us  [body(): rows_of.append((row << (blocks - 1).bit_length()) + wanted)]
  transfers between devices with their start and end apart: 19 -> 19, of which waited for: 7 -> 6; matrix products, arithmetic and copies ran while one was open for 6% -> 5% of each run, Pallas kernels for 3% -> 3%
where the time goes in v4:
time: 60.1 us; the launch traced here: 59.8 us
  starting transfers between devices  23.3 us (39%)
  waiting for transfers between devices  20.8 us (35%)
  Pallas kernels  11 us (18%)
  other arithmetic  2.77 us (5%)
  local copies, waits for them, and re-layouts  1.04 us (2%)
  between operations  0.88 us (1%)
    ppermute x16, starting transfers between devices, swap(): return lax.ppermute(value, axis, pairs)  19 us
    ppermute x16, waiting for transfers between devices, swap(): return lax.ppermute(value, axis, pairs)  18 us
    pallas_call x1, Pallas kernels, run_steps(): pl.pallas_call(functools.partial(steps_kernel, first, scale, step_rows, s...  7.88 us
    ppermute x1, waiting for transfers between devices, body(): lax.ppermute(sides, 'lon', [(i, (i + (1 if i % 2 else -1)) % n_lon) for i...  2.82 us
    ppermute x1, starting transfers between devices, body(): lax.ppermute(edge_of(-1), 'lat', [(i, i + 1) for i in range(n_lat - 1)])  1.9 us
    pallas_call x1, Pallas kernels, run_widen(): pl.pallas_call(functools.partial(widen_kernel, slots, table is not None,...  1.75 us
    pallas_call x1, Pallas kernels, body(): pl.pallas_call(stretch_kernel, out_shape=jax.ShapeDtypeStruct((rows, lane...  1.4 us
    ppermute x1, starting transfers between devices, body(): lax.ppermute(edge_of(0), 'lat', [(i + 1, i) for i in range(n_lat - 1)])  1.28 us
  transfers between devices with their start and end apart: 19, of which 6 were waited for; matrix products, arithmetic and copies ran while one was open for 5% of the time, Pallas kernels for 3%

profile of v4, /device:TPU:0, one launch (start us, length us, event | category | flops | bytes accessed | tf_op | source)
XLA Modules:
  0.0 59.8 jit_solution(10444776761671216304)
XLA Ops:
  0.6 0.9 %pad_maximum_fusion.6 = bf16[8,96,128]{2,1,0:T(8,128)(2,1)S(1)} fusion(bf16[8,64,128]{2,1,0:T(8,128)(2,1)} %bitcast.44, bf16[8,32,128]{2,1,0:T(8,128)(2,1)} %bitcast.45), kind=kLoop, calls=%fused_computation.6 | loop fusion | flops 393216 | bytes 393216 | tf_op jit(solution)/shard_map/concatenate | solution.py:292
  1.6 3.1 %collective-permute-start = (bf16[768,128]{1,0:T(8,128)(2,1)S(1)}, bf16[768,128]{1,0:T(8,128)(2,1)S(1)}, u32[]{:S(2)}, u32[]{:S(2)}) collective-permute-start(bf16[768,128]{1,0:T(8,128)(2,1)S(1)} %bitcast.31), channel_id=1, source_target_pairs={{0,1},{1,0},{2,3},{3,2},{4,5},{5,4},{6,7},{7,6},{8,9},{9,8},{10,11... | collective-permute-start | bytes 589832 | tf_op jit(solution)/shard_map/ppermute | solution.py:33
  4.6 2.6 %collective-permute-start.8 = (bf16[768,128]{1,0:T(8,128)(2,1)S(1)}, bf16[768,128]{1,0:T(8,128)(2,1)S(1)}, u32[]{:S(2)}, u32[]{:S(2)}) collective-permute-start(bf16[768,128]{1,0:T(8,128)(2,1)S(1)} %bitcast.32), channel_id=1, source_target_pairs={{0,2},{1,3},{2,0},{3,1},{4,6},{5,7},{6,4},{7,5},{8,10},{9,11},{10,... | collective-permute-start | bytes 589832 | tf_op jit(solution)/shard_map/ppermute | solution.py:33
  7.2 1.5 %collective-permute-start.3 = (bf16[1,768,128]{2,1,0:T(8,128)(2,1)S(1)}, bf16[1,768,128]{2,1,0:T(8,128)(2,1)S(1)}, u32[]{:S(2)}, u32[]{:S(2)}) collective-permute-start(bf16[1,768,128]{2,1,0:T(8,128)(2,1)S(1)} %bitcast.33), channel_id=1, source_target_pairs={{0,8},{4,20},{8,0},{12,28},{16,24},{20,4},{24,16},{28,12},{1,9},{5... | collective-permute-start | bytes 589832 | tf_op jit(solution)/shard_map/ppermute | solution.py:33
  8.7 0.8 %fusion.12 = (s32[8,1,128]{2,1,0:T(1,128)S(1)}, s32[8,1,128]{2,1,0:T(1,128)S(1)}) fusion(s32[8,512,128]{2,1,0:T(8,128)} %refs_2_.1), kind=kLoop, calls=%fused_computation.50 | loop fusion | bytes 16384 | tf_op jit(solution)/shard_map/slice | solution.py:320
  9.5 0.7 %pad_add_fusion.1 = (s32[3,8,128]{2,1,0:T(8,128)S(1)}, s32[3,8,128]{2,1,0:T(8,128)S(1)}) fusion(s32[1,8,128]{2,1,0:T(8,128)} %bitcast.46, s32[1,8,128]{2,1,0:T(8,128)} %bitcast.48, s32[1,8,128]{2,1,0:T(8,128)S(1)} %bitcast.50, s32[1,8,128]{2,1,0:T(8,128)S(1)} %bitcast.51), kind=kLoop, calls=%fused_computation.8 | loop fusion | flops 12288 | bytes 40960 | tf_op jit(solution)/shard_map/stack | solution.py:320
  10.2 3.4 %collective-permute-done = bf16[768,128]{1,0:T(8,128)(2,1)S(1)} collective-permute-done((bf16[768,128]{1,0:T(8,128)(2,1)S(1)}, bf16[768,128]{1,0:T(8,128)(2,1)S(1)}, u32[]{:S(2)}, u32[]{:S(2)}) %collective-permute-start) | collective-permute-done | bytes 196640 | tf_op jit(solution)/shard_map/ppermute | solution.py:33
  13.6 1.7 %collective-permute-start.6 = (bf16[1,768,128]{2,1,0:T(8,128)(2,1)S(1)}, bf16[1,768,128]{2,1,0:T(8,128)(2,1)S(1)}, u32[]{:S(2)}, u32[]{:S(2)}) collective-permute-start(bf16[1,768,128]{2,1,0:T(8,128)(2,1)S(1)} %bitcast.40), channel_id=1, source_target_pairs={{0,8},{4,20},{8,0},{12,28},{16,24},{20,4},{24,16},{28,12},{1,9},{5... | collective-permute-start | bytes 589832 | tf_op jit(solution)/shard_map/ppermute | solution.py:33
  15.3 1.3 %collective-permute-start.2 = (s32[3,8,128]{2,1,0:T(8,128)S(1)}, s32[3,8,128]{2,1,0:T(8,128)S(1)}, u32[]{:S(2)}, u32[]{:S(2)}) collective-permute-start(s32[3,8,128]{2,1,0:T(8,128)S(1)} %get-tuple-element.16), channel_id=1, source_target_pairs={{1,0},{2,1},{3,2},{5,4},{6,5},{7,6},{9,8},{10,9},{11,10},{13,12},{... | collective-permute-start | bytes 36872 | tf_op jit(solution)/shard_map/ppermute | solution.py:324
  16.6 1.6 %collective-permute-start.4 = (bf16[2,768,128]{2,1,0:T(8,128)(2,1)S(1)}, bf16[2,768,128]{2,1,0:T(8,128)(2,1)S(1)}, u32[]{:S(2)}, u32[]{:S(2)}) collective-permute-start(bf16[2,768,128]{2,1,0:T(8,128)(2,1)S(1)} %pad_maximum_fusion.2), channel_id=1, source_target_pairs={{0,16},{4,12},{8,24},{12,4},{16,0},{20,28},{24,8},{28,20},{1,17},{... | collective-permute-start | bytes 1179656 | tf_op jit(solution)/shard_map/ppermute | solution.py:33
  18.2 0.5 collective-permute-start.9
  18.8 2.6 %collective-permute-start.12 = (bf16[768,128]{1,0:T(8,128)(2,1)S(1)}, bf16[768,128]{1,0:T(8,128)(2,1)S(1)}, u32[]{:S(2)}, u32[]{:S(2)}) collective-permute-start(bf16[768,128]{1,0:T(8,128)(2,1)S(1)} %bitcast.35), channel_id=1, source_target_pairs={{0,3},{1,2},{2,1},{3,0},{4,7},{5,6},{6,5},{7,4},{8,11},{9,10},{10,... | collective-permute-start | bytes 589832 | tf_op jit(solution)/shard_map/ppermute | solution.py:33
  21.4 1.9 %collective-permute-start.1 = (s32[3,8,128]{2,1,0:T(8,128)S(1)}, s32[3,8,128]{2,1,0:T(8,128)S(1)}, u32[]{:S(2)}, u32[]{:S(2)}) collective-permute-start(s32[3,8,128]{2,1,0:T(8,128)S(1)} %get-tuple-element.15), channel_id=1, source_target_pairs={{0,1},{1,2},{2,3},{4,5},{5,6},{6,7},{8,9},{9,10},{10,11},{12,13},{... | collective-permute-start | bytes 36872 | tf_op jit(solution)/shard_map/ppermute | solution.py:323
  23.3 2.7 %collective-permute-done.9 = bf16[1,768,128]{2,1,0:T(8,128)(2,1)S(1)} collective-permute-done((bf16[1,768,128]{2,1,0:T(8,128)(2,1)S(1)}, bf16[1,768,128]{2,1,0:T(8,128)(2,1)S(1)}, u32[]{:S(2)}, u32[]{:S(2)}) %collective-permute-start.9) | collective-permute-done | bytes 196640 | tf_op jit(solution)/shard_map/ppermute | solution.py:33
  26.1 1.2 %collective-permute-start.11 = (bf16[2,768,128]{2,1,0:T(8,128)(2,1)S(1)}, bf16[2,768,128]{2,1,0:T(8,128)(2,1)S(1)}, u32[]{:S(2)}, u32[]{:S(2)}) collective-permute-start(bf16[2,768,128]{2,1,0:T(8,128)(2,1)S(1)} %pad_maximum_fusion.4), channel_id=1, source_target_pairs={{0,16},{4,12},{8,24},{12,4},{16,0},{20,28},{24,8},{28,20},{1,17},{... | collective-permute-start | bytes 1179656 | tf_op jit(solution)/shard_map/ppermute | solution.py:33
  27.4 1.5 %collective-permute-start.13 = (bf16[1,768,128]{2,1,0:T(8,128)(2,1)S(1)}, bf16[1,768,128]{2,1,0:T(8,128)(2,1)S(1)}, u32[]{:S(2)}, u32[]{:S(2)}) collective-permute-start(bf16[1,768,128]{2,1,0:T(8,128)(2,1)S(1)} %bitcast.37), channel_id=1, source_target_pairs={{0,8},{4,20},{8,0},{12,28},{16,24},{20,4},{24,16},{28,12},{1,9},{5... | collective-permute-start | bytes 589832 | tf_op jit(solution)/shard_map/ppermute | solution.py:33
  29.0 0.4 collective-permute-start.7
  29.4 5.8 %collective-permute-done.13 = bf16[1,768,128]{2,1,0:T(8,128)(2,1)S(1)} collective-permute-done((bf16[1,768,128]{2,1,0:T(8,128)(2,1)S(1)}, bf16[1,768,128]{2,1,0:T(8,128)(2,1)S(1)}, u32[]{:S(2)}, u32[]{:S(2)}) %collective-permute-start.13) | collective-permute-done | bytes 196640 | tf_op jit(solution)/shard_map/ppermute | solution.py:33
  35.2 0.9 %collective-permute-start.15 = (bf16[2,768,128]{2,1,0:T(8,128)(2,1)S(1)}, bf16[2,768,128]{2,1,0:T(8,128)(2,1)S(1)}, u32[]{:S(2)}, u32[]{:S(2)}) collective-permute-start(bf16[2,768,128]{2,1,0:T(8,128)(2,1)S(1)} %pad_maximum_fusion.5), channel_id=1, source_target_pairs={{0,16},{4,12},{8,24},{12,4},{16,0},{20,28},{24,8},{28,20},{1,17},{... | collective-permute-start | bytes 1179656 | tf_op jit(solution)/shard_map/ppermute | solution.py:33
  36.2 0.1 pad_maximum_fusion.refs_0_
  36.4 0.6 collective-permute-start.14
  37.0 1.2 %collective-permute-done.7 = bf16[2,768,128]{2,1,0:T(8,128)(2,1)S(1)} collective-permute-done((bf16[2,768,128]{2,1,0:T(8,128)(2,1)S(1)}, bf16[2,768,128]{2,1,0:T(8,128)(2,1)S(1)}, u32[]{:S(2)}, u32[]{:S(2)}) %collective-permute-start.7) | collective-permute-done | bytes 393248 | tf_op jit(solution)/shard_map/ppermute | solution.py:33
  38.3 4.8 %collective-permute-done.15 = bf16[2,768,128]{2,1,0:T(8,128)(2,1)S(1)} collective-permute-done((bf16[2,768,128]{2,1,0:T(8,128)(2,1)S(1)}, bf16[2,768,128]{2,1,0:T(8,128)(2,1)S(1)}, u32[]{:S(2)}, u32[]{:S(2)}) %collective-permute-start.15) | collective-permute-done | bytes 393248 | tf_op jit(solution)/shard_map/ppermute | solution.py:33
  43.1 0.1 pad_maximum_fusion.1.refs_4_
  43.3 0.1 slice_bitcast_fusion.5
  43.4 0.8 %fusion.9.refs_0_ = s32[8,130]{1,0:T(8,128)S(1)} fusion(s32[8,1]{1,0:T(8,128)S(1)} %get-tuple-element.35, s32[8,1]{1,0:T(8,128)S(1)} %get-tuple-element.33, s32[8,128]{1,0:T(8,128)} %bitcast.47, s32[8,1]{1,0:T(8,128)S(1)} %get-tuple-element.34, s32[8,1]{1,0:T(8,128)S(1)} %get-tuple-element.32, s32[8,128]{1,0:T(8,128)} %bitcast.49, s32[]{:T(128)S(6)} %axis_index.33, ...), kind=kLoop, calls=%fused_computation.29 | loop fusion | flops 49920 | bytes 12488 | tf_op jit(solution)/shard_map/add | solution.py:336
  44.2 1.7 %widen_0.1.refs_3_ = f32[24576,128]{1,0:T(8,128)S(1)} custom-call(bf16[4,768,128]{2,1,0:T(8,128)(2,1)S(1)} %pad_maximum_fusion.refs_0_, bf16[4,768,128]{2,1,0:T(8,128)(2,1)S(1)} %collective-permute-done.5.refs_1_, bf16[4,768,128]{2,1,0:T(8,128)(2,1)S(1)} %constant_dynamic-update-slice_fusion.refs_2_, ...), custom_call_target="tpu_custom_call" | custom-call | bytes 8388608 | tf_op jit(solution)/shard_map/widen_0/pallas_call | solution.py:102
  46.0 7.9 %rk_steps_0.1 = (f32[24576,128]{1,0:T(8,128)S(1)}, f32[2,512,128]{2,1,0:T(8,128)S(1)}, f32[2,8,128]{2,1,0:T(8,128)S(1)}, f32[2,512,128]{2,1,0:T(8,128)}, f32[2,8,128]{2,1,0:T(8,128)S(1)}) custom-call(s32[8,130]{1,0:T(8,128)S(1)} %fusion.9.refs_0_, s32[8,8,128]{2,1,0:T(8,128)S(1)} %bitcast.29, ...), custom_call_target="tpu_custom_call", output_to_operand_aliasing={{0}: (3, {})} | custom-call | flops 20971520 | bytes 16777216 | tf_op jit(solution)/shard_map/rk_steps_0/pallas_call | solution.py:224
  53.9 0.5 collective-permute-start.17
  54.4 1.1 %collective-permute-start.18 = (f32[2,8,128]{2,1,0:T(8,128)S(1)}, f32[2,8,128]{2,1,0:T(8,128)S(1)}, u32[]{:S(2)}, u32[]{:S(2)}) collective-permute-start(f32[2,8,128]{2,1,0:T(8,128)S(1)} %get-tuple-element.27), channel_id=1, source_target_pairs={{0,28},{4,8},{8,4},{12,16},{16,12},{20,24},{24,20},{28,0},{1,29},{... | collective-permute-start | bytes 24584 | tf_op jit(solution)/shard_map/ppermute | solution.py:365
  55.6 2.8 %collective-permute-done.18 = f32[2,8,128]{2,1,0:T(8,128)S(1)} collective-permute-done((f32[2,8,128]{2,1,0:T(8,128)S(1)}, f32[2,8,128]{2,1,0:T(8,128)S(1)}, u32[]{:S(2)}, u32[]{:S(2)}) %collective-permute-start.18) | collective-permute-done | bytes 8224 | tf_op jit(solution)/shard_map/ppermute | solution.py:365
  58.4 1.4 %stretch.1 = f32[512,128]{1,0:T(8,128)} custom-call(f32[2,512,128]{2,1,0:T(8,128)S(1)} %get-tuple-element.25.flow_ref, f32[2,8,128]{2,1,0:T(8,128)S(1)} %bitcast.30, f32[2,8,128]{2,1,0:T(8,128)S(1)} %broadcast_select_fusion.sides_ref), custom_call_target="tpu_custom_call" | custom-call | tf_op jit(solution)/shard_map/stretch/pallas_call | solution.py:375
  (37 shorter events, 0.6 us)
Async XLA Ops:
  1.6 12.1 %collective-permute-start = (bf16[768,128]{1,0:T(8,128)(2,1)S(1)}, bf16[768,128]{1,0:T(8,128)(2,1)S(1)}, u32[]{:S(2)}, u32[]{:S(2)}) collective-permute-start(bf16[768,128]{1,0:T(8,128)(2,1)S(1)} %bitcast.31), channel_id=1, source_target_pairs={{0,1},{1,0},{2,3},{3,2},{4,5},{5,4},{6,7},{7,6},{8,9},{9,8},{10,11... | collective-permute-start | bytes 589832 | tf_op jit(solution)/shard_map/ppermute | solution.py:33
  4.6 13.6 %collective-permute-start.8 = (bf16[768,128]{1,0:T(8,128)(2,1)S(1)}, bf16[768,128]{1,0:T(8,128)(2,1)S(1)}, u32[]{:S(2)}, u32[]{:S(2)}) collective-permute-start(bf16[768,128]{1,0:T(8,128)(2,1)S(1)} %bitcast.32), channel_id=1, source_target_pairs={{0,2},{1,3},{2,0},{3,1},{4,6},{5,7},{6,4},{7,5},{8,10},{9,11},{10,... | collective-permute-start | bytes 589832 | tf_op jit(solution)/shard_map/ppermute | solution.py:33
  7.2 9.4 %collective-permute-start.3 = (bf16[1,768,128]{2,1,0:T(8,128)(2,1)S(1)}, bf16[1,768,128]{2,1,0:T(8,128)(2,1)S(1)}, u32[]{:S(2)}, u32[]{:S(2)}) collective-permute-start(bf16[1,768,128]{2,1,0:T(8,128)(2,1)S(1)} %bitcast.33), channel_id=1, source_target_pairs={{0,8},{4,20},{8,0},{12,28},{16,24},{20,4},{24,16},{28,12},{1,9},{5... | collective-permute-start | bytes 589832 | tf_op jit(solution)/shard_map/ppermute | solution.py:33
  13.6 15.3 %collective-permute-start.6 = (bf16[1,768,128]{2,1,0:T(8,128)(2,1)S(1)}, bf16[1,768,128]{2,1,0:T(8,128)(2,1)S(1)}, u32[]{:S(2)}, u32[]{:S(2)}) collective-permute-start(bf16[1,768,128]{2,1,0:T(8,128)(2,1)S(1)} %bitcast.40), channel_id=1, source_target_pairs={{0,8},{4,20},{8,0},{12,28},{16,24},{20,4},{24,16},{28,12},{1,9},{5... | collective-permute-start | bytes 589832 | tf_op jit(solution)/shard_map/ppermute | solution.py:33
  15.3 6.1 %collective-permute-start.2 = (s32[3,8,128]{2,1,0:T(8,128)S(1)}, s32[3,8,128]{2,1,0:T(8,128)S(1)}, u32[]{:S(2)}, u32[]{:S(2)}) collective-permute-start(s32[3,8,128]{2,1,0:T(8,128)S(1)} %get-tuple-element.16), channel_id=1, source_target_pairs={{1,0},{2,1},{3,2},{5,4},{6,5},{7,6},{9,8},{10,9},{11,10},{13,12},{... | collective-permute-start | bytes 36872 | tf_op jit(solution)/shard_map/ppermute | solution.py:324
  16.6 12.3 %collective-permute-start.4 = (bf16[2,768,128]{2,1,0:T(8,128)(2,1)S(1)}, bf16[2,768,128]{2,1,0:T(8,128)(2,1)S(1)}, u32[]{:S(2)}, u32[]{:S(2)}) collective-permute-start(bf16[2,768,128]{2,1,0:T(8,128)(2,1)S(1)} %pad_maximum_fusion.2), channel_id=1, source_target_pairs={{0,16},{4,12},{8,24},{12,4},{16,0},{20,28},{24,8},{28,20},{1,17},{... | collective-permute-start | bytes 1179656 | tf_op jit(solution)/shard_map/ppermute | solution.py:33
  18.2 7.8 %collective-permute-start.9 = (bf16[1,768,128]{2,1,0:T(8,128)(2,1)S(1)}, bf16[1,768,128]{2,1,0:T(8,128)(2,1)S(1)}, u32[]{:S(2)}, u32[]{:S(2)}) collective-permute-start(bf16[1,768,128]{2,1,0:T(8,128)(2,1)S(1)} %bitcast.42), channel_id=1, source_target_pairs={{0,8},{4,20},{8,0},{12,28},{16,24},{20,4},{24,16},{28,12},{1,9},{5... | collective-permute-start | bytes 589832 | tf_op jit(solution)/shard_map/ppermute | solution.py:33
  18.8 8.6 %collective-permute-start.12 = (bf16[768,128]{1,0:T(8,128)(2,1)S(1)}, bf16[768,128]{1,0:T(8,128)(2,1)S(1)}, u32[]{:S(2)}, u32[]{:S(2)}) collective-permute-start(bf16[768,128]{1,0:T(8,128)(2,1)S(1)} %bitcast.35), channel_id=1, source_target_pairs={{0,3},{1,2},{2,1},{3,0},{4,7},{5,6},{6,5},{7,4},{8,11},{9,10},{10,... | collective-permute-start | bytes 589832 | tf_op jit(solution)/shard_map/ppermute | solution.py:33
  21.4 21.8 %collective-permute-start.1 = (s32[3,8,128]{2,1,0:T(8,128)S(1)}, s32[3,8,128]{2,1,0:T(8,128)S(1)}, u32[]{:S(2)}, u32[]{:S(2)}) collective-permute-start(s32[3,8,128]{2,1,0:T(8,128)S(1)} %get-tuple-element.15), channel_id=1, source_target_pairs={{0,1},{1,2},{2,3},{4,5},{5,6},{6,7},{8,9},{9,10},{10,11},{12,13},{... | collective-permute-start | bytes 36872 | tf_op jit(solution)/shard_map/ppermute | solution.py:323
  26.1 10.2 %collective-permute-start.11 = (bf16[2,768,128]{2,1,0:T(8,128)(2,1)S(1)}, bf16[2,768,128]{2,1,0:T(8,128)(2,1)S(1)}, u32[]{:S(2)}, u32[]{:S(2)}) collective-permute-start(bf16[2,768,128]{2,1,0:T(8,128)(2,1)S(1)} %pad_maximum_fusion.4), channel_id=1, source_target_pairs={{0,16},{4,12},{8,24},{12,4},{16,0},{20,28},{24,8},{28,20},{1,17},{... | collective-permute-start | bytes 1179656 | tf_op jit(solution)/shard_map/ppermute | solution.py:33
  27.4 18.6 %copy-start = (s32[8,512,128]{2,1,0:T(8,128)S(1)}, s32[8,512,128]{2,1,0:T(8,128)}, u32[]{:S(2)}) copy-start(s32[8,512,128]{2,1,0:T(8,128)} %refs_2_.1) | copy-start | bytes 6291460
  27.4 7.8 %collective-permute-start.13 = (bf16[1,768,128]{2,1,0:T(8,128)(2,1)S(1)}, bf16[1,768,128]{2,1,0:T(8,128)(2,1)S(1)}, u32[]{:S(2)}, u32[]{:S(2)}) collective-permute-start(bf16[1,768,128]{2,1,0:T(8,128)(2,1)S(1)} %bitcast.37), channel_id=1, source_target_pairs={{0,8},{4,20},{8,0},{12,28},{16,24},{20,4},{24,16},{28,12},{1,9},{5... | collective-permute-start | bytes 589832 | tf_op jit(solution)/shard_map/ppermute | solution.py:33
  29.0 9.2 %collective-permute-start.7 = (bf16[2,768,128]{2,1,0:T(8,128)(2,1)S(1)}, bf16[2,768,128]{2,1,0:T(8,128)(2,1)S(1)}, u32[]{:S(2)}, u32[]{:S(2)}) collective-permute-start(bf16[2,768,128]{2,1,0:T(8,128)(2,1)S(1)} %pad_maximum_fusion.3), channel_id=1, source_target_pairs={{0,16},{4,12},{8,24},{12,4},{16,0},{20,28},{24,8},{28,20},{1,17},{... | collective-permute-start | bytes 1179656 | tf_op jit(solution)/shard_map/ppermute | solution.py:33
  35.2 7.8 %collective-permute-start.15 = (bf16[2,768,128]{2,1,0:T(8,128)(2,1)S(1)}, bf16[2,768,128]{2,1,0:T(8,128)(2,1)S(1)}, u32[]{:S(2)}, u32[]{:S(2)}) collective-permute-start(bf16[2,768,128]{2,1,0:T(8,128)(2,1)S(1)} %pad_maximum_fusion.5), channel_id=1, source_target_pairs={{0,16},{4,12},{8,24},{12,4},{16,0},{20,28},{24,8},{28,20},{1,17},{... | collective-permute-start | bytes 1179656 | tf_op jit(solution)/shard_map/ppermute | solution.py:33
  36.2 7.9 %collective-permute-start.5 = (bf16[4,768,128]{2,1,0:T(8,128)(2,1)S(1)}, bf16[4,768,128]{2,1,0:T(8,128)(2,1)S(1)}, u32[]{:S(2)}, u32[]{:S(2)}) collective-permute-start(bf16[4,768,128]{2,1,0:T(8,128)(2,1)S(1)} %pad_maximum_fusion.refs_0_), channel_id=1, source_target_pairs={{0,4},{4,0},{8,12},{12,8},{16,20},{20,16},{24,28},{28,24},{1,5},{5... | collective-permute-start | bytes 2359304 | tf_op jit(solution)/shard_map/ppermute | solution.py:33
  36.4 7.8 %collective-permute-start.14 = (bf16[4,768,128]{2,1,0:T(8,128)(2,1)S(1)}, bf16[4,768,128]{2,1,0:T(8,128)(2,1)S(1)}, u32[]{:S(2)}, u32[]{:S(2)}) collective-permute-start(bf16[4,768,128]{2,1,0:T(8,128)(2,1)S(1)} %constant_dynamic-update-slice_fusion.2.refs_4_), channel_id=1, source_target_pairs={{0,4},{4,0},{8,12},{12,8},{16,20},{20,16},{24,28},{28,24},{1,5},{5... | collective-permute-start | bytes 2359304 | tf_op jit(solution)/shard_map/ppermute | solution.py:33
  38.2 6.0 %collective-permute-start.10 = (bf16[4,768,128]{2,1,0:T(8,128)(2,1)S(1)}, bf16[4,768,128]{2,1,0:T(8,128)(2,1)S(1)}, u32[]{:S(2)}, u32[]{:S(2)}) collective-permute-start(bf16[4,768,128]{2,1,0:T(8,128)(2,1)S(1)} %constant_dynamic-update-slice_fusion.refs_2_), channel_id=1, source_target_pairs={{0,4},{4,0},{8,12},{12,8},{16,20},{20,16},{24,28},{28,24},{1,5},{5... | collective-permute-start | bytes 2359304 | tf_op jit(solution)/shard_map/ppermute | solution.py:33
  43.2 2.8 %collective-permute-start.16 = (bf16[4,768,128]{2,1,0:T(8,128)(2,1)S(1)}, bf16[4,768,128]{2,1,0:T(8,128)(2,1)S(1)}, u32[]{:S(2)}, u32[]{:S(2)}) collective-permute-start(bf16[4,768,128]{2,1,0:T(8,128)(2,1)S(1)} %pad_maximum_fusion.1.refs_4_), channel_id=1, source_target_pairs={{0,4},{4,0},{8,12},{12,8},{16,20},{20,16},{24,28},{28,24},{1,5},{5... | collective-permute-start | bytes 2359304 | tf_op jit(solution)/shard_map/ppermute | solution.py:33
  53.9 1.7 %collective-permute-start.17 = (f32[2,8,128]{2,1,0:T(8,128)S(1)}, f32[2,8,128]{2,1,0:T(8,128)S(1)}, u32[]{:S(2)}, u32[]{:S(2)}) collective-permute-start(f32[2,8,128]{2,1,0:T(8,128)S(1)} %get-tuple-element.27), channel_id=1, source_target_pairs={{0,4},{4,0},{8,12},{12,8},{16,20},{20,16},{24,28},{28,24},{1,5},{5... | collective-permute-start | bytes 24584 | tf_op jit(solution)/shard_map/ppermute | solution.py:33
  54.4 4.0 %collective-permute-start.18 = (f32[2,8,128]{2,1,0:T(8,128)S(1)}, f32[2,8,128]{2,1,0:T(8,128)S(1)}, u32[]{:S(2)}, u32[]{:S(2)}) collective-permute-start(f32[2,8,128]{2,1,0:T(8,128)S(1)} %get-tuple-element.27), channel_id=1, source_target_pairs={{0,28},{4,8},{8,4},{12,16},{16,12},{20,24},{24,20},{28,0},{1,29},{... | collective-permute-start | bytes 24584 | tf_op jit(solution)/shard_map/ppermute | solution.py:365

commit v5 on v4

--- a/solution.py
+++ b/solution.py
@@ -85,7 +85,7 @@
             table[pl.ds(row, step_rows), :] = values
             return carry
 
-        lax.fori_loop(0, piece.shape[0] * steps, widen, 0, unroll=4)
+        lax.fori_loop(0, piece.shape[0] * steps, widen, 0, unroll=8)
 
 
 def widen_kernel(slots, has_table, first, steps, step_rows, scale, *refs):
@@ -220,7 +220,7 @@
     given = [table] if table is not None else []
     shape = jax.ShapeDtypeStruct((height, lanes), jnp.float32)
     need += 0 if given else height * lanes * 4
-    unroll = 8
+    unroll = 16
     results = pl.pallas_call(
         functools.partial(
             steps_kernel, first, scale, step_rows, slots, len(given) > 0, first > 0, final, unroll

time: 60.1 us -> 59.4 us (0.988)
  Pallas kernels: 11 us -> 10.3 us
where the time goes in v5:
time: 59.4 us; the launch traced here: 59.1 us
  starting transfers between devices  23.3 us (39%)
  waiting for transfers between devices  20.8 us (35%)
  Pallas kernels  10.3 us (17%)
  other arithmetic  2.77 us (5%)
  local copies, waits for them, and re-layouts  1.04 us (2%)
  between operations  0.88 us (1%)
    ppermute x16, starting transfers between devices, swap(): return lax.ppermute(value, axis, pairs)  19 us
    ppermute x16, waiting for transfers between devices, swap(): return lax.ppermute(value, axis, pairs)  18 us
    pallas_call x1, Pallas kernels, run_steps(): pl.pallas_call(functools.partial(steps_kernel, first, scale, step_rows, s...  7.38 us
    ppermute x1, waiting for transfers between devices, body(): lax.ppermute(sides, 'lon', [(i, (i + (1 if i % 2 else -1)) % n_lon) for i...  2.83 us
    ppermute x1, starting transfers between devices, body(): lax.ppermute(edge_of(-1), 'lat', [(i, i + 1) for i in range(n_lat - 1)])  1.9 us
    pallas_call x1, Pallas kernels, run_widen(): pl.pallas_call(functools.partial(widen_kernel, slots, table is not None,...  1.56 us
    pallas_call x1, Pallas kernels, body(): pl.pallas_call(stretch_kernel, out_shape=jax.ShapeDtypeStruct((rows, lane...  1.4 us
    ppermute x1, starting transfers between devices, body(): lax.ppermute(edge_of(0), 'lat', [(i + 1, i) for i in range(n_lat - 1)])  1.28 us
  transfers between devices with their start and end apart: 19, of which 6 were waited for; matrix products, arithmetic and copies ran while one was open for 5% of the time, Pallas kernels for 3%

profile of v5, /device:TPU:0, one launch (start us, length us, event | category | flops | bytes accessed | tf_op | source)
XLA Modules:
  0.0 59.1 jit_solution(16243176585300866429)
XLA Ops:
  0.6 0.9 %pad_maximum_fusion.6 = bf16[8,96,128]{2,1,0:T(8,128)(2,1)S(1)} fusion(bf16[8,64,128]{2,1,0:T(8,128)(2,1)} %bitcast.44, bf16[8,32,128]{2,1,0:T(8,128)(2,1)} %bitcast.45), kind=kLoop, calls=%fused_computation.6 | loop fusion | flops 393216 | bytes 393216 | tf_op jit(solution)/shard_map/concatenate | solution.py:292
  1.6 3.1 %collective-permute-start = (bf16[768,128]{1,0:T(8,128)(2,1)S(1)}, bf16[768,128]{1,0:T(8,128)(2,1)S(1)}, u32[]{:S(2)}, u32[]{:S(2)}) collective-permute-start(bf16[768,128]{1,0:T(8,128)(2,1)S(1)} %bitcast.31), channel_id=1, source_target_pairs={{0,1},{1,0},{2,3},{3,2},{4,5},{5,4},{6,7},{7,6},{8,9},{9,8},{10,11... | collective-permute-start | bytes 589832 | tf_op jit(solution)/shard_map/ppermute | solution.py:33
  4.6 2.6 %collective-permute-start.8 = (bf16[768,128]{1,0:T(8,128)(2,1)S(1)}, bf16[768,128]{1,0:T(8,128)(2,1)S(1)}, u32[]{:S(2)}, u32[]{:S(2)}) collective-permute-start(bf16[768,128]{1,0:T(8,128)(2,1)S(1)} %bitcast.32), channel_id=1, source_target_pairs={{0,2},{1,3},{2,0},{3,1},{4,6},{5,7},{6,4},{7,5},{8,10},{9,11},{10,... | collective-permute-start | bytes 589832 | tf_op jit(solution)/shard_map/ppermute | solution.py:33
  7.2 1.5 %collective-permute-start.3 = (bf16[1,768,128]{2,1,0:T(8,128)(2,1)S(1)}, bf16[1,768,128]{2,1,0:T(8,128)(2,1)S(1)}, u32[]{:S(2)}, u32[]{:S(2)}) collective-permute-start(bf16[1,768,128]{2,1,0:T(8,128)(2,1)S(1)} %bitcast.33), channel_id=1, source_target_pairs={{0,8},{4,20},{8,0},{12,28},{16,24},{20,4},{24,16},{28,12},{1,9},{5... | collective-permute-start | bytes 589832 | tf_op jit(solution)/shard_map/ppermute | solution.py:33
  8.7 0.8 %fusion.12 = (s32[8,1,128]{2,1,0:T(1,128)S(1)}, s32[8,1,128]{2,1,0:T(1,128)S(1)}) fusion(s32[8,512,128]{2,1,0:T(8,128)} %refs_2_.1), kind=kLoop, calls=%fused_computation.50 | loop fusion | bytes 16384 | tf_op jit(solution)/shard_map/slice | solution.py:320
  9.5 0.7 %pad_add_fusion.1 = (s32[3,8,128]{2,1,0:T(8,128)S(1)}, s32[3,8,128]{2,1,0:T(8,128)S(1)}) fusion(s32[1,8,128]{2,1,0:T(8,128)} %bitcast.46, s32[1,8,128]{2,1,0:T(8,128)} %bitcast.48, s32[1,8,128]{2,1,0:T(8,128)S(1)} %bitcast.50, s32[1,8,128]{2,1,0:T(8,128)S(1)} %bitcast.51), kind=kLoop, calls=%fused_computation.8 | loop fusion | flops 12288 | bytes 40960 | tf_op jit(solution)/shard_map/stack | solution.py:320
  10.2 3.4 %collective-permute-done = bf16[768,128]{1,0:T(8,128)(2,1)S(1)} collective-permute-done((bf16[768,128]{1,0:T(8,128)(2,1)S(1)}, bf16[768,128]{1,0:T(8,128)(2,1)S(1)}, u32[]{:S(2)}, u32[]{:S(2)}) %collective-permute-start) | collective-permute-done | bytes 196640 | tf_op jit(solution)/shard_map/ppermute | solution.py:33
  13.6 1.7 %collective-permute-start.6 = (bf16[1,768,128]{2,1,0:T(8,128)(2,1)S(1)}, bf16[1,768,128]{2,1,0:T(8,128)(2,1)S(1)}, u32[]{:S(2)}, u32[]{:S(2)}) collective-permute-start(bf16[1,768,128]{2,1,0:T(8,128)(2,1)S(1)} %bitcast.40), channel_id=1, source_target_pairs={{0,8},{4,20},{8,0},{12,28},{16,24},{20,4},{24,16},{28,12},{1,9},{5... | collective-permute-start | bytes 589832 | tf_op jit(solution)/shard_map/ppermute | solution.py:33
  15.3 1.3 %collective-permute-start.2 = (s32[3,8,128]{2,1,0:T(8,128)S(1)}, s32[3,8,128]{2,1,0:T(8,128)S(1)}, u32[]{:S(2)}, u32[]{:S(2)}) collective-permute-start(s32[3,8,128]{2,1,0:T(8,128)S(1)} %get-tuple-element.16), channel_id=1, source_target_pairs={{1,0},{2,1},{3,2},{5,4},{6,5},{7,6},{9,8},{10,9},{11,10},{13,12},{... | collective-permute-start | bytes 36872 | tf_op jit(solution)/shard_map/ppermute | solution.py:324
  16.6 1.6 %collective-permute-start.4 = (bf16[2,768,128]{2,1,0:T(8,128)(2,1)S(1)}, bf16[2,768,128]{2,1,0:T(8,128)(2,1)S(1)}, u32[]{:S(2)}, u32[]{:S(2)}) collective-permute-start(bf16[2,768,128]{2,1,0:T(8,128)(2,1)S(1)} %pad_maximum_fusion.2), channel_id=1, source_target_pairs={{0,16},{4,12},{8,24},{12,4},{16,0},{20,28},{24,8},{28,20},{1,17},{... | collective-permute-start | bytes 1179656 | tf_op jit(solution)/shard_map/ppermute | solution.py:33
  18.2 0.5 collective-permute-start.9
  18.8 2.6 %collective-permute-start.12 = (bf16[768,128]{1,0:T(8,128)(2,1)S(1)}, bf16[768,128]{1,0:T(8,128)(2,1)S(1)}, u32[]{:S(2)}, u32[]{:S(2)}) collective-permute-start(bf16[768,128]{1,0:T(8,128)(2,1)S(1)} %bitcast.35), channel_id=1, source_target_pairs={{0,3},{1,2},{2,1},{3,0},{4,7},{5,6},{6,5},{7,4},{8,11},{9,10},{10,... | collective-permute-start | bytes 589832 | tf_op jit(solution)/shard_map/ppermute | solution.py:33
  21.4 1.9 %collective-permute-start.1 = (s32[3,8,128]{2,1,0:T(8,128)S(1)}, s32[3,8,128]{2,1,0:T(8,128)S(1)}, u32[]{:S(2)}, u32[]{:S(2)}) collective-permute-start(s32[3,8,128]{2,1,0:T(8,128)S(1)} %get-tuple-element.15), channel_id=1, source_target_pairs={{0,1},{1,2},{2,3},{4,5},{5,6},{6,7},{8,9},{9,10},{10,11},{12,13},{... | collective-permute-start | bytes 36872 | tf_op jit(solution)/shard_map/ppermute | solution.py:323
  23.3 2.7 %collective-permute-done.9 = bf16[1,768,128]{2,1,0:T(8,128)(2,1)S(1)} collective-permute-done((bf16[1,768,128]{2,1,0:T(8,128)(2,1)S(1)}, bf16[1,768,128]{2,1,0:T(8,128)(2,1)S(1)}, u32[]{:S(2)}, u32[]{:S(2)}) %collective-permute-start.9) | collective-permute-done | bytes 196640 | tf_op jit(solution)/shard_map/ppermute | solution.py:33
  26.1 1.2 %collective-permute-start.11 = (bf16[2,768,128]{2,1,0:T(8,128)(2,1)S(1)}, bf16[2,768,128]{2,1,0:T(8,128)(2,1)S(1)}, u32[]{:S(2)}, u32[]{:S(2)}) collective-permute-start(bf16[2,768,128]{2,1,0:T(8,128)(2,1)S(1)} %pad_maximum_fusion.4), channel_id=1, source_target_pairs={{0,16},{4,12},{8,24},{12,4},{16,0},{20,28},{24,8},{28,20},{1,17},{... | collective-permute-start | bytes 1179656 | tf_op jit(solution)/shard_map/ppermute | solution.py:33
  27.4 1.5 %collective-permute-start.13 = (bf16[1,768,128]{2,1,0:T(8,128)(2,1)S(1)}, bf16[1,768,128]{2,1,0:T(8,128)(2,1)S(1)}, u32[]{:S(2)}, u32[]{:S(2)}) collective-permute-start(bf16[1,768,128]{2,1,0:T(8,128)(2,1)S(1)} %bitcast.37), channel_id=1, source_target_pairs={{0,8},{4,20},{8,0},{12,28},{16,24},{20,4},{24,16},{28,12},{1,9},{5... | collective-permute-start | bytes 589832 | tf_op jit(solution)/shard_map/ppermute | solution.py:33
  29.0 0.4 collective-permute-start.7
  29.4 5.8 %collective-permute-done.13 = bf16[1,768,128]{2,1,0:T(8,128)(2,1)S(1)} collective-permute-done((bf16[1,768,128]{2,1,0:T(8,128)(2,1)S(1)}, bf16[1,768,128]{2,1,0:T(8,128)(2,1)S(1)}, u32[]{:S(2)}, u32[]{:S(2)}) %collective-permute-start.13) | collective-permute-done | bytes 196640 | tf_op jit(solution)/shard_map/ppermute | solution.py:33
  35.2 0.9 %collective-permute-start.15 = (bf16[2,768,128]{2,1,0:T(8,128)(2,1)S(1)}, bf16[2,768,128]{2,1,0:T(8,128)(2,1)S(1)}, u32[]{:S(2)}, u32[]{:S(2)}) collective-permute-start(bf16[2,768,128]{2,1,0:T(8,128)(2,1)S(1)} %pad_maximum_fusion.5), channel_id=1, source_target_pairs={{0,16},{4,12},{8,24},{12,4},{16,0},{20,28},{24,8},{28,20},{1,17},{... | collective-permute-start | bytes 1179656 | tf_op jit(solution)/shard_map/ppermute | solution.py:33
  36.2 0.1 pad_maximum_fusion.refs_0_
  36.4 0.6 collective-permute-start.14
  37.0 1.2 %collective-permute-done.7 = bf16[2,768,128]{2,1,0:T(8,128)(2,1)S(1)} collective-permute-done((bf16[2,768,128]{2,1,0:T(8,128)(2,1)S(1)}, bf16[2,768,128]{2,1,0:T(8,128)(2,1)S(1)}, u32[]{:S(2)}, u32[]{:S(2)}) %collective-permute-start.7) | collective-permute-done | bytes 393248 | tf_op jit(solution)/shard_map/ppermute | solution.py:33
  38.3 4.8 %collective-permute-done.15 = bf16[2,768,128]{2,1,0:T(8,128)(2,1)S(1)} collective-permute-done((bf16[2,768,128]{2,1,0:T(8,128)(2,1)S(1)}, bf16[2,768,128]{2,1,0:T(8,128)(2,1)S(1)}, u32[]{:S(2)}, u32[]{:S(2)}) %collective-permute-start.15) | collective-permute-done | bytes 393248 | tf_op jit(solution)/shard_map/ppermute | solution.py:33
  43.1 0.1 pad_maximum_fusion.1.refs_4_
  43.3 0.1 slice_bitcast_fusion.5
  43.4 0.8 %fusion.9.refs_0_ = s32[8,130]{1,0:T(8,128)S(1)} fusion(s32[8,1]{1,0:T(8,128)S(1)} %get-tuple-element.35, s32[8,1]{1,0:T(8,128)S(1)} %get-tuple-element.33, s32[8,128]{1,0:T(8,128)} %bitcast.47, s32[8,1]{1,0:T(8,128)S(1)} %get-tuple-element.34, s32[8,1]{1,0:T(8,128)S(1)} %get-tuple-element.32, s32[8,128]{1,0:T(8,128)} %bitcast.49, s32[]{:T(128)S(6)} %axis_index.33, ...), kind=kLoop, calls=%fused_computation.29 | loop fusion | flops 49920 | bytes 12488 | tf_op jit(solution)/shard_map/add | solution.py:336
  44.2 1.6 %widen_0.1.refs_3_ = f32[24576,128]{1,0:T(8,128)S(1)} custom-call(bf16[4,768,128]{2,1,0:T(8,128)(2,1)S(1)} %pad_maximum_fusion.refs_0_, bf16[4,768,128]{2,1,0:T(8,128)(2,1)S(1)} %collective-permute-done.5.refs_1_, bf16[4,768,128]{2,1,0:T(8,128)(2,1)S(1)} %constant_dynamic-update-slice_fusion.refs_2_, ...), custom_call_target="tpu_custom_call" | custom-call | bytes 8388608 | tf_op jit(solution)/shard_map/widen_0/pallas_call | solution.py:102
  45.8 7.4 %rk_steps_0.1 = (f32[24576,128]{1,0:T(8,128)S(1)}, f32[2,512,128]{2,1,0:T(8,128)S(1)}, f32[2,8,128]{2,1,0:T(8,128)S(1)}, f32[2,512,128]{2,1,0:T(8,128)}, f32[2,8,128]{2,1,0:T(8,128)S(1)}) custom-call(s32[8,130]{1,0:T(8,128)S(1)} %fusion.9.refs_0_, s32[8,8,128]{2,1,0:T(8,128)S(1)} %bitcast.29, ...), custom_call_target="tpu_custom_call", output_to_operand_aliasing={{0}: (3, {})} | custom-call | flops 20971520 | bytes 16777216 | tf_op jit(solution)/shard_map/rk_steps_0/pallas_call | solution.py:224
  53.2 0.5 collective-permute-start.17
  53.7 1.1 %collective-permute-start.18 = (f32[2,8,128]{2,1,0:T(8,128)S(1)}, f32[2,8,128]{2,1,0:T(8,128)S(1)}, u32[]{:S(2)}, u32[]{:S(2)}) collective-permute-start(f32[2,8,128]{2,1,0:T(8,128)S(1)} %get-tuple-element.27), channel_id=1, source_target_pairs={{0,28},{4,8},{8,4},{12,16},{16,12},{20,24},{24,20},{28,0},{1,29},{... | collective-permute-start | bytes 24584 | tf_op jit(solution)/shard_map/ppermute | solution.py:365
  54.9 2.8 %collective-permute-done.18 = f32[2,8,128]{2,1,0:T(8,128)S(1)} collective-permute-done((f32[2,8,128]{2,1,0:T(8,128)S(1)}, f32[2,8,128]{2,1,0:T(8,128)S(1)}, u32[]{:S(2)}, u32[]{:S(2)}) %collective-permute-start.18) | collective-permute-done | bytes 8224 | tf_op jit(solution)/shard_map/ppermute | solution.py:365
  57.7 1.4 %stretch.1 = f32[512,128]{1,0:T(8,128)} custom-call(f32[2,512,128]{2,1,0:T(8,128)S(1)} %get-tuple-element.25.flow_ref, f32[2,8,128]{2,1,0:T(8,128)S(1)} %bitcast.30, f32[2,8,128]{2,1,0:T(8,128)S(1)} %broadcast_select_fusion.sides_ref), custom_call_target="tpu_custom_call" | custom-call | tf_op jit(solution)/shard_map/stretch/pallas_call | solution.py:375
  (37 shorter events, 0.6 us)
Async XLA Ops:
  1.6 12.1 %collective-permute-start = (bf16[768,128]{1,0:T(8,128)(2,1)S(1)}, bf16[768,128]{1,0:T(8,128)(2,1)S(1)}, u32[]{:S(2)}, u32[]{:S(2)}) collective-permute-start(bf16[768,128]{1,0:T(8,128)(2,1)S(1)} %bitcast.31), channel_id=1, source_target_pairs={{0,1},{1,0},{2,3},{3,2},{4,5},{5,4},{6,7},{7,6},{8,9},{9,8},{10,11... | collective-permute-start | bytes 589832 | tf_op jit(solution)/shard_map/ppermute | solution.py:33
  4.6 13.6 %collective-permute-start.8 = (bf16[768,128]{1,0:T(8,128)(2,1)S(1)}, bf16[768,128]{1,0:T(8,128)(2,1)S(1)}, u32[]{:S(2)}, u32[]{:S(2)}) collective-permute-start(bf16[768,128]{1,0:T(8,128)(2,1)S(1)} %bitcast.32), channel_id=1, source_target_pairs={{0,2},{1,3},{2,0},{3,1},{4,6},{5,7},{6,4},{7,5},{8,10},{9,11},{10,... | collective-permute-start | bytes 589832 | tf_op jit(solution)/shard_map/ppermute | solution.py:33
  7.2 9.4 %collective-permute-start.3 = (bf16[1,768,128]{2,1,0:T(8,128)(2,1)S(1)}, bf16[1,768,128]{2,1,0:T(8,128)(2,1)S(1)}, u32[]{:S(2)}, u32[]{:S(2)}) collective-permute-start(bf16[1,768,128]{2,1,0:T(8,128)(2,1)S(1)} %bitcast.33), channel_id=1, source_target_pairs={{0,8},{4,20},{8,0},{12,28},{16,24},{20,4},{24,16},{28,12},{1,9},{5... | collective-permute-start | bytes 589832 | tf_op jit(solution)/shard_map/ppermute | solution.py:33
  13.6 15.3 %collective-permute-start.6 = (bf16[1,768,128]{2,1,0:T(8,128)(2,1)S(1)}, bf16[1,768,128]{2,1,0:T(8,128)(2,1)S(1)}, u32[]{:S(2)}, u32[]{:S(2)}) collective-permute-start(bf16[1,768,128]{2,1,0:T(8,128)(2,1)S(1)} %bitcast.40), channel_id=1, source_target_pairs={{0,8},{4,20},{8,0},{12,28},{16,24},{20,4},{24,16},{28,12},{1,9},{5... | collective-permute-start | bytes 589832 | tf_op jit(solution)/shard_map/ppermute | solution.py:33
  15.3 6.1 %collective-permute-start.2 = (s32[3,8,128]{2,1,0:T(8,128)S(1)}, s32[3,8,128]{2,1,0:T(8,128)S(1)}, u32[]{:S(2)}, u32[]{:S(2)}) collective-permute-start(s32[3,8,128]{2,1,0:T(8,128)S(1)} %get-tuple-element.16), channel_id=1, source_target_pairs={{1,0},{2,1},{3,2},{5,4},{6,5},{7,6},{9,8},{10,9},{11,10},{13,12},{... | collective-permute-start | bytes 36872 | tf_op jit(solution)/shard_map/ppermute | solution.py:324
  16.6 12.3 %collective-permute-start.4 = (bf16[2,768,128]{2,1,0:T(8,128)(2,1)S(1)}, bf16[2,768,128]{2,1,0:T(8,128)(2,1)S(1)}, u32[]{:S(2)}, u32[]{:S(2)}) collective-permute-start(bf16[2,768,128]{2,1,0:T(8,128)(2,1)S(1)} %pad_maximum_fusion.2), channel_id=1, source_target_pairs={{0,16},{4,12},{8,24},{12,4},{16,0},{20,28},{24,8},{28,20},{1,17},{... | collective-permute-start | bytes 1179656 | tf_op jit(solution)/shard_map/ppermute | solution.py:33
  18.2 7.8 %collective-permute-start.9 = (bf16[1,768,128]{2,1,0:T(8,128)(2,1)S(1)}, bf16[1,768,128]{2,1,0:T(8,128)(2,1)S(1)}, u32[]{:S(2)}, u32[]{:S(2)}) collective-permute-start(bf16[1,768,128]{2,1,0:T(8,128)(2,1)S(1)} %bitcast.42), channel_id=1, source_target_pairs={{0,8},{4,20},{8,0},{12,28},{16,24},{20,4},{24,16},{28,12},{1,9},{5... | collective-permute-start | bytes 589832 | tf_op jit(solution)/shard_map/ppermute | solution.py:33
  18.8 8.6 %collective-permute-start.12 = (bf16[768,128]{1,0:T(8,128)(2,1)S(1)}, bf16[768,128]{1,0:T(8,128)(2,1)S(1)}, u32[]{:S(2)}, u32[]{:S(2)}) collective-permute-start(bf16[768,128]{1,0:T(8,128)(2,1)S(1)} %bitcast.35), channel_id=1, source_target_pairs={{0,3},{1,2},{2,1},{3,0},{4,7},{5,6},{6,5},{7,4},{8,11},{9,10},{10,... | collective-permute-start | bytes 589832 | tf_op jit(solution)/shard_map/ppermute | solution.py:33
  21.4 21.8 %collective-permute-start.1 = (s32[3,8,128]{2,1,0:T(8,128)S(1)}, s32[3,8,128]{2,1,0:T(8,128)S(1)}, u32[]{:S(2)}, u32[]{:S(2)}) collective-permute-start(s32[3,8,128]{2,1,0:T(8,128)S(1)} %get-tuple-element.15), channel_id=1, source_target_pairs={{0,1},{1,2},{2,3},{4,5},{5,6},{6,7},{8,9},{9,10},{10,11},{12,13},{... | collective-permute-start | bytes 36872 | tf_op jit(solution)/shard_map/ppermute | solution.py:323
  26.1 10.2 %collective-permute-start.11 = (bf16[2,768,128]{2,1,0:T(8,128)(2,1)S(1)}, bf16[2,768,128]{2,1,0:T(8,128)(2,1)S(1)}, u32[]{:S(2)}, u32[]{:S(2)}) collective-permute-start(bf16[2,768,128]{2,1,0:T(8,128)(2,1)S(1)} %pad_maximum_fusion.4), channel_id=1, source_target_pairs={{0,16},{4,12},{8,24},{12,4},{16,0},{20,28},{24,8},{28,20},{1,17},{... | collective-permute-start | bytes 1179656 | tf_op jit(solution)/shard_map/ppermute | solution.py:33
  27.4 18.4 %copy-start = (s32[8,512,128]{2,1,0:T(8,128)S(1)}, s32[8,512,128]{2,1,0:T(8,128)}, u32[]{:S(2)}) copy-start(s32[8,512,128]{2,1,0:T(8,128)} %refs_2_.1) | copy-start | bytes 6291460
  27.4 7.8 %collective-permute-start.13 = (bf16[1,768,128]{2,1,0:T(8,128)(2,1)S(1)}, bf16[1,768,128]{2,1,0:T(8,128)(2,1)S(1)}, u32[]{:S(2)}, u32[]{:S(2)}) collective-permute-start(bf16[1,768,128]{2,1,0:T(8,128)(2,1)S(1)} %bitcast.37), channel_id=1, source_target_pairs={{0,8},{4,20},{8,0},{12,28},{16,24},{20,4},{24,16},{28,12},{1,9},{5... | collective-permute-start | bytes 589832 | tf_op jit(solution)/shard_map/ppermute | solution.py:33
  29.0 9.2 %collective-permute-start.7 = (bf16[2,768,128]{2,1,0:T(8,128)(2,1)S(1)}, bf16[2,768,128]{2,1,0:T(8,128)(2,1)S(1)}, u32[]{:S(2)}, u32[]{:S(2)}) collective-permute-start(bf16[2,768,128]{2,1,0:T(8,128)(2,1)S(1)} %pad_maximum_fusion.3), channel_id=1, source_target_pairs={{0,16},{4,12},{8,24},{12,4},{16,0},{20,28},{24,8},{28,20},{1,17},{... | collective-permute-start | bytes 1179656 | tf_op jit(solution)/shard_map/ppermute | solution.py:33
  35.2 7.8 %collective-permute-start.15 = (bf16[2,768,128]{2,1,0:T(8,128)(2,1)S(1)}, bf16[2,768,128]{2,1,0:T(8,128)(2,1)S(1)}, u32[]{:S(2)}, u32[]{:S(2)}) collective-permute-start(bf16[2,768,128]{2,1,0:T(8,128)(2,1)S(1)} %pad_maximum_fusion.5), channel_id=1, source_target_pairs={{0,16},{4,12},{8,24},{12,4},{16,0},{20,28},{24,8},{28,20},{1,17},{... | collective-permute-start | bytes 1179656 | tf_op jit(solution)/shard_map/ppermute | solution.py:33
  36.2 7.9 %collective-permute-start.5 = (bf16[4,768,128]{2,1,0:T(8,128)(2,1)S(1)}, bf16[4,768,128]{2,1,0:T(8,128)(2,1)S(1)}, u32[]{:S(2)}, u32[]{:S(2)}) collective-permute-start(bf16[4,768,128]{2,1,0:T(8,128)(2,1)S(1)} %pad_maximum_fusion.refs_0_), channel_id=1, source_target_pairs={{0,4},{4,0},{8,12},{12,8},{16,20},{20,16},{24,28},{28,24},{1,5},{5... | collective-permute-start | bytes 2359304 | tf_op jit(solution)/shard_map/ppermute | solution.py:33
  36.4 7.8 %collective-permute-start.14 = (bf16[4,768,128]{2,1,0:T(8,128)(2,1)S(1)}, bf16[4,768,128]{2,1,0:T(8,128)(2,1)S(1)}, u32[]{:S(2)}, u32[]{:S(2)}) collective-permute-start(bf16[4,768,128]{2,1,0:T(8,128)(2,1)S(1)} %constant_dynamic-update-slice_fusion.2.refs_4_), channel_id=1, source_target_pairs={{0,4},{4,0},{8,12},{12,8},{16,20},{20,16},{24,28},{28,24},{1,5},{5... | collective-permute-start | bytes 2359304 | tf_op jit(solution)/shard_map/ppermute | solution.py:33
  38.2 6.0 %collective-permute-start.10 = (bf16[4,768,128]{2,1,0:T(8,128)(2,1)S(1)}, bf16[4,768,128]{2,1,0:T(8,128)(2,1)S(1)}, u32[]{:S(2)}, u32[]{:S(2)}) collective-permute-start(bf16[4,768,128]{2,1,0:T(8,128)(2,1)S(1)} %constant_dynamic-update-slice_fusion.refs_2_), channel_id=1, source_target_pairs={{0,4},{4,0},{8,12},{12,8},{16,20},{20,16},{24,28},{28,24},{1,5},{5... | collective-permute-start | bytes 2359304 | tf_op jit(solution)/shard_map/ppermute | solution.py:33
  43.2 2.6 %collective-permute-start.16 = (bf16[4,768,128]{2,1,0:T(8,128)(2,1)S(1)}, bf16[4,768,128]{2,1,0:T(8,128)(2,1)S(1)}, u32[]{:S(2)}, u32[]{:S(2)}) collective-permute-start(bf16[4,768,128]{2,1,0:T(8,128)(2,1)S(1)} %pad_maximum_fusion.1.refs_4_), channel_id=1, source_target_pairs={{0,4},{4,0},{8,12},{12,8},{16,20},{20,16},{24,28},{28,24},{1,5},{5... | collective-permute-start | bytes 2359304 | tf_op jit(solution)/shard_map/ppermute | solution.py:33
  53.2 1.7 %collective-permute-start.17 = (f32[2,8,128]{2,1,0:T(8,128)S(1)}, f32[2,8,128]{2,1,0:T(8,128)S(1)}, u32[]{:S(2)}, u32[]{:S(2)}) collective-permute-start(f32[2,8,128]{2,1,0:T(8,128)S(1)} %get-tuple-element.27), channel_id=1, source_target_pairs={{0,4},{4,0},{8,12},{12,8},{16,20},{20,16},{24,28},{28,24},{1,5},{5... | collective-permute-start | bytes 24584 | tf_op jit(solution)/shard_map/ppermute | solution.py:33
  53.7 4.0 %collective-permute-start.18 = (f32[2,8,128]{2,1,0:T(8,128)S(1)}, f32[2,8,128]{2,1,0:T(8,128)S(1)}, u32[]{:S(2)}, u32[]{:S(2)}) collective-permute-start(f32[2,8,128]{2,1,0:T(8,128)S(1)} %get-tuple-element.27), channel_id=1, source_target_pairs={{0,28},{4,8},{8,4},{12,16},{16,12},{20,24},{24,20},{28,0},{1,29},{... | collective-permute-start | bytes 24584 | tf_op jit(solution)/shard_map/ppermute | solution.py:365

commit v6 on v5

--- a/solution.py
+++ b/solution.py
@@ -361,13 +361,13 @@
             state,
         )
     flow, edge, out, sides = state
-    inner = swap(sides, "lon", (1,))
     outer = lax.ppermute(
         sides, "lon", [(i, (i + (1 if i % 2 else -1)) % n_lon) for i in range(n_lon)]
     )
     south = jnp.where(lat_index == 0, flow[:, :1], edge[:, :1])
     north = jnp.where(lat_index == n_lat - 1, flow[:, -1:], edge[:, GROUP_ROWS : GROUP_ROWS + 1])
     edge = jnp.repeat(jnp.concatenate([south, north], axis=1), GROUP_ROWS, axis=1)
+    inner = swap(after(sides, edge), "lon", (1,))
     lane = lax.broadcasted_iota(jnp.int32, sides.shape, 2)
     from_inner = (lane < lanes // 2) == (lax.axis_index("lon") % 2 == 0)
     sides = jnp.where(from_inner, inner, outer)

time: 59.4 us -> 59 us (level)
  waiting for transfers between devices: 20.8 us -> 20.2 us
    ppermute x1, waiting for transfers between devices: 2.83 us -> 1.24 us  [body(): lax.ppermute(sides, 'lon', [(i, (i + (1 if i % 2 else -1)) % n_lon) for i...]
    ppermute x16, waiting for transfers between devices: 18 us -> 19 us  [swap(): return lax.ppermute(value, axis, pairs)]
  transfers between devices with their start and end apart: 19 -> 19, of which waited for: 6 -> 7; matrix products, arithmetic and copies ran while one was open for 5% -> 5% of each run, Pallas kernels for 3% -> 3%
where the time goes in v6:
time: 59 us; the launch traced here: 58.7 us
  starting transfers between devices  23.4 us (40%)
  waiting for transfers between devices  20.2 us (34%)
  Pallas kernels  10.3 us (17%)
  other arithmetic  2.77 us (5%)
  local copies, waits for them, and re-layouts  1.04 us (2%)
  between operations  0.88 us (1%)
    ppermute x16, waiting for transfers between devices, swap(): return lax.ppermute(value, axis, pairs)  19 us
    ppermute x16, starting transfers between devices, swap(): return lax.ppermute(value, axis, pairs)  18.6 us
    pallas_call x1, Pallas kernels, run_steps(): pl.pallas_call(functools.partial(steps_kernel, first, scale, step_rows, s...  7.38 us
    ppermute x1, starting transfers between devices, body(): lax.ppermute(edge_of(-1), 'lat', [(i, i + 1) for i in range(n_lat - 1)])  1.9 us
    ppermute x1, starting transfers between devices, body(): lax.ppermute(sides, 'lon', [(i, (i + (1 if i % 2 else -1)) % n_lon) for i...  1.58 us
    pallas_call x1, Pallas kernels, run_widen(): pl.pallas_call(functools.partial(widen_kernel, slots, table is not None,...  1.56 us
    pallas_call x1, Pallas kernels, body(): pl.pallas_call(stretch_kernel, out_shape=jax.ShapeDtypeStruct((rows, lane...  1.4 us
    ppermute x1, starting transfers between devices, body(): lax.ppermute(edge_of(0), 'lat', [(i + 1, i) for i in range(n_lat - 1)])  1.28 us
  transfers between devices with their start and end apart: 19, of which 7 were waited for; matrix products, arithmetic and copies ran while one was open for 5% of the time, Pallas kernels for 3%

profile of v6, /device:TPU:0, one launch (start us, length us, event | category | flops | bytes accessed | tf_op | source)
XLA Modules:
  0.0 58.7 jit_solution(6048170711715812073)
XLA Ops:
  0.6 0.9 %pad_maximum_fusion.6 = bf16[8,96,128]{2,1,0:T(8,128)(2,1)S(1)} fusion(bf16[8,64,128]{2,1,0:T(8,128)(2,1)} %bitcast.44, bf16[8,32,128]{2,1,0:T(8,128)(2,1)} %bitcast.45), kind=kLoop, calls=%fused_computation.6 | loop fusion | flops 393216 | bytes 393216 | tf_op jit(solution)/shard_map/concatenate | solution.py:292
  1.6 3.1 %collective-permute-start = (bf16[768,128]{1,0:T(8,128)(2,1)S(1)}, bf16[768,128]{1,0:T(8,128)(2,1)S(1)}, u32[]{:S(2)}, u32[]{:S(2)}) collective-permute-start(bf16[768,128]{1,0:T(8,128)(2,1)S(1)} %bitcast.31), channel_id=1, source_target_pairs={{0,1},{1,0},{2,3},{3,2},{4,5},{5,4},{6,7},{7,6},{8,9},{9,8},{10,11... | collective-permute-start | bytes 589832 | tf_op jit(solution)/shard_map/ppermute | solution.py:33
  4.6 2.6 %collective-permute-start.8 = (bf16[768,128]{1,0:T(8,128)(2,1)S(1)}, bf16[768,128]{1,0:T(8,128)(2,1)S(1)}, u32[]{:S(2)}, u32[]{:S(2)}) collective-permute-start(bf16[768,128]{1,0:T(8,128)(2,1)S(1)} %bitcast.32), channel_id=1, source_target_pairs={{0,2},{1,3},{2,0},{3,1},{4,6},{5,7},{6,4},{7,5},{8,10},{9,11},{10,... | collective-permute-start | bytes 589832 | tf_op jit(solution)/shard_map/ppermute | solution.py:33
  7.2 1.5 %collective-permute-start.3 = (bf16[1,768,128]{2,1,0:T(8,128)(2,1)S(1)}, bf16[1,768,128]{2,1,0:T(8,128)(2,1)S(1)}, u32[]{:S(2)}, u32[]{:S(2)}) collective-permute-start(bf16[1,768,128]{2,1,0:T(8,128)(2,1)S(1)} %bitcast.33), channel_id=1, source_target_pairs={{0,8},{4,20},{8,0},{12,28},{16,24},{20,4},{24,16},{28,12},{1,9},{5... | collective-permute-start | bytes 589832 | tf_op jit(solution)/shard_map/ppermute | solution.py:33
  8.7 0.8 %fusion.12 = (s32[8,1,128]{2,1,0:T(1,128)S(1)}, s32[8,1,128]{2,1,0:T(1,128)S(1)}) fusion(s32[8,512,128]{2,1,0:T(8,128)} %refs_2_.1), kind=kLoop, calls=%fused_computation.50 | loop fusion | bytes 16384 | tf_op jit(solution)/shard_map/slice | solution.py:320
  9.5 0.7 %pad_add_fusion.1 = (s32[3,8,128]{2,1,0:T(8,128)S(1)}, s32[3,8,128]{2,1,0:T(8,128)S(1)}) fusion(s32[1,8,128]{2,1,0:T(8,128)} %bitcast.46, s32[1,8,128]{2,1,0:T(8,128)} %bitcast.48, s32[1,8,128]{2,1,0:T(8,128)S(1)} %bitcast.50, s32[1,8,128]{2,1,0:T(8,128)S(1)} %bitcast.51), kind=kLoop, calls=%fused_computation.8 | loop fusion | flops 12288 | bytes 40960 | tf_op jit(solution)/shard_map/stack | solution.py:320
  10.2 3.4 %collective-permute-done = bf16[768,128]{1,0:T(8,128)(2,1)S(1)} collective-permute-done((bf16[768,128]{1,0:T(8,128)(2,1)S(1)}, bf16[768,128]{1,0:T(8,128)(2,1)S(1)}, u32[]{:S(2)}, u32[]{:S(2)}) %collective-permute-start) | collective-permute-done | bytes 196640 | tf_op jit(solution)/shard_map/ppermute | solution.py:33
  13.6 1.7 %collective-permute-start.6 = (bf16[1,768,128]{2,1,0:T(8,128)(2,1)S(1)}, bf16[1,768,128]{2,1,0:T(8,128)(2,1)S(1)}, u32[]{:S(2)}, u32[]{:S(2)}) collective-permute-start(bf16[1,768,128]{2,1,0:T(8,128)(2,1)S(1)} %bitcast.40), channel_id=1, source_target_pairs={{0,8},{4,20},{8,0},{12,28},{16,24},{20,4},{24,16},{28,12},{1,9},{5... | collective-permute-start | bytes 589832 | tf_op jit(solution)/shard_map/ppermute | solution.py:33
  15.3 1.3 %collective-permute-start.2 = (s32[3,8,128]{2,1,0:T(8,128)S(1)}, s32[3,8,128]{2,1,0:T(8,128)S(1)}, u32[]{:S(2)}, u32[]{:S(2)}) collective-permute-start(s32[3,8,128]{2,1,0:T(8,128)S(1)} %get-tuple-element.17), channel_id=1, source_target_pairs={{1,0},{2,1},{3,2},{5,4},{6,5},{7,6},{9,8},{10,9},{11,10},{13,12},{... | collective-permute-start | bytes 36872 | tf_op jit(solution)/shard_map/ppermute | solution.py:324
  16.6 1.6 %collective-permute-start.4 = (bf16[2,768,128]{2,1,0:T(8,128)(2,1)S(1)}, bf16[2,768,128]{2,1,0:T(8,128)(2,1)S(1)}, u32[]{:S(2)}, u32[]{:S(2)}) collective-permute-start(bf16[2,768,128]{2,1,0:T(8,128)(2,1)S(1)} %pad_maximum_fusion.2), channel_id=1, source_target_pairs={{0,16},{4,12},{8,24},{12,4},{16,0},{20,28},{24,8},{28,20},{1,17},{... | collective-permute-start | bytes 1179656 | tf_op jit(solution)/shard_map/ppermute | solution.py:33
  18.2 0.5 collective-permute-start.9
  18.8 2.6 %collective-permute-start.12 = (bf16[768,128]{1,0:T(8,128)(2,1)S(1)}, bf16[768,128]{1,0:T(8,128)(2,1)S(1)}, u32[]{:S(2)}, u32[]{:S(2)}) collective-permute-start(bf16[768,128]{1,0:T(8,128)(2,1)S(1)} %bitcast.35), channel_id=1, source_target_pairs={{0,3},{1,2},{2,1},{3,0},{4,7},{5,6},{6,5},{7,4},{8,11},{9,10},{10,... | collective-permute-start | bytes 589832 | tf_op jit(solution)/shard_map/ppermute | solution.py:33
  21.4 1.9 %collective-permute-start.1 = (s32[3,8,128]{2,1,0:T(8,128)S(1)}, s32[3,8,128]{2,1,0:T(8,128)S(1)}, u32[]{:S(2)}, u32[]{:S(2)}) collective-permute-start(s32[3,8,128]{2,1,0:T(8,128)S(1)} %get-tuple-element.16), channel_id=1, source_target_pairs={{0,1},{1,2},{2,3},{4,5},{5,6},{6,7},{8,9},{9,10},{10,11},{12,13},{... | collective-permute-start | bytes 36872 | tf_op jit(solution)/shard_map/ppermute | solution.py:323
  23.3 2.7 %collective-permute-done.9 = bf16[1,768,128]{2,1,0:T(8,128)(2,1)S(1)} collective-permute-done((bf16[1,768,128]{2,1,0:T(8,128)(2,1)S(1)}, bf16[1,768,128]{2,1,0:T(8,128)(2,1)S(1)}, u32[]{:S(2)}, u32[]{:S(2)}) %collective-permute-start.9) | collective-permute-done | bytes 196640 | tf_op jit(solution)/shard_map/ppermute | solution.py:33
  26.1 1.2 %collective-permute-start.11 = (bf16[2,768,128]{2,1,0:T(8,128)(2,1)S(1)}, bf16[2,768,128]{2,1,0:T(8,128)(2,1)S(1)}, u32[]{:S(2)}, u32[]{:S(2)}) collective-permute-start(bf16[2,768,128]{2,1,0:T(8,128)(2,1)S(1)} %pad_maximum_fusion.4), channel_id=1, source_target_pairs={{0,16},{4,12},{8,24},{12,4},{16,0},{20,28},{24,8},{28,20},{1,17},{... | collective-permute-start | bytes 1179656 | tf_op jit(solution)/shard_map/ppermute | solution.py:33
  27.4 1.5 %collective-permute-start.13 = (bf16[1,768,128]{2,1,0:T(8,128)(2,1)S(1)}, bf16[1,768,128]{2,1,0:T(8,128)(2,1)S(1)}, u32[]{:S(2)}, u32[]{:S(2)}) collective-permute-start(bf16[1,768,128]{2,1,0:T(8,128)(2,1)S(1)} %bitcast.37), channel_id=1, source_target_pairs={{0,8},{4,20},{8,0},{12,28},{16,24},{20,4},{24,16},{28,12},{1,9},{5... | collective-permute-start | bytes 589832 | tf_op jit(solution)/shard_map/ppermute | solution.py:33
  29.0 0.4 collective-permute-start.7
  29.4 5.8 %collective-permute-done.13 = bf16[1,768,128]{2,1,0:T(8,128)(2,1)S(1)} collective-permute-done((bf16[1,768,128]{2,1,0:T(8,128)(2,1)S(1)}, bf16[1,768,128]{2,1,0:T(8,128)(2,1)S(1)}, u32[]{:S(2)}, u32[]{:S(2)}) %collective-permute-start.13) | collective-permute-done | bytes 196640 | tf_op jit(solution)/shard_map/ppermute | solution.py:33
  35.2 0.9 %collective-permute-start.15 = (bf16[2,768,128]{2,1,0:T(8,128)(2,1)S(1)}, bf16[2,768,128]{2,1,0:T(8,128)(2,1)S(1)}, u32[]{:S(2)}, u32[]{:S(2)}) collective-permute-start(bf16[2,768,128]{2,1,0:T(8,128)(2,1)S(1)} %pad_maximum_fusion.5), channel_id=1, source_target_pairs={{0,16},{4,12},{8,24},{12,4},{16,0},{20,28},{24,8},{28,20},{1,17},{... | collective-permute-start | bytes 1179656 | tf_op jit(solution)/shard_map/ppermute | solution.py:33
  36.2 0.1 pad_maximum_fusion.refs_0_
  36.4 0.6 collective-permute-start.14
  37.0 1.2 %collective-permute-done.7 = bf16[2,768,128]{2,1,0:T(8,128)(2,1)S(1)} collective-permute-done((bf16[2,768,128]{2,1,0:T(8,128)(2,1)S(1)}, bf16[2,768,128]{2,1,0:T(8,128)(2,1)S(1)}, u32[]{:S(2)}, u32[]{:S(2)}) %collective-permute-start.7) | collective-permute-done | bytes 393248 | tf_op jit(solution)/shard_map/ppermute | solution.py:33
  38.3 4.8 %collective-permute-done.15 = bf16[2,768,128]{2,1,0:T(8,128)(2,1)S(1)} collective-permute-done((bf16[2,768,128]{2,1,0:T(8,128)(2,1)S(1)}, bf16[2,768,128]{2,1,0:T(8,128)(2,1)S(1)}, u32[]{:S(2)}, u32[]{:S(2)}) %collective-permute-start.15) | collective-permute-done | bytes 393248 | tf_op jit(solution)/shard_map/ppermute | solution.py:33
  43.1 0.1 pad_maximum_fusion.1.refs_4_
  43.4 0.8 %fusion.9.refs_0_ = s32[8,130]{1,0:T(8,128)S(1)} fusion(s32[8,1]{1,0:T(8,128)S(1)} %get-tuple-element.37, s32[8,1]{1,0:T(8,128)S(1)} %get-tuple-element.35, s32[8,128]{1,0:T(8,128)} %bitcast.47, s32[8,1]{1,0:T(8,128)S(1)} %get-tuple-element.36, s32[8,1]{1,0:T(8,128)S(1)} %get-tuple-element.34, s32[8,128]{1,0:T(8,128)} %bitcast.49, s32[]{:T(128)S(6)} %axis_index.33, ...), kind=kLoop, calls=%fused_computation.29 | loop fusion | flops 49920 | bytes 12488 | tf_op jit(solution)/shard_map/add | solution.py:336
  44.2 1.6 %widen_0.1.refs_3_ = f32[24576,128]{1,0:T(8,128)S(1)} custom-call(bf16[4,768,128]{2,1,0:T(8,128)(2,1)S(1)} %pad_maximum_fusion.refs_0_, bf16[4,768,128]{2,1,0:T(8,128)(2,1)S(1)} %collective-permute-done.5.refs_1_, bf16[4,768,128]{2,1,0:T(8,128)(2,1)S(1)} %constant_dynamic-update-slice_fusion.refs_2_, ...), custom_call_target="tpu_custom_call" | custom-call | bytes 8388608 | tf_op jit(solution)/shard_map/widen_0/pallas_call | solution.py:102
  45.8 7.4 %rk_steps_0.1 = (f32[24576,128]{1,0:T(8,128)S(1)}, f32[2,512,128]{2,1,0:T(8,128)S(1)}, f32[2,8,128]{2,1,0:T(8,128)S(1)}, f32[2,512,128]{2,1,0:T(8,128)}, f32[2,8,128]{2,1,0:T(8,128)S(1)}) custom-call(s32[8,130]{1,0:T(8,128)S(1)} %fusion.9.refs_0_, s32[8,8,128]{2,1,0:T(8,128)S(1)} %bitcast.29, ...), custom_call_target="tpu_custom_call", output_to_operand_aliasing={{0}: (3, {})} | custom-call | flops 20971520 | bytes 16777216 | tf_op jit(solution)/shard_map/rk_steps_0/pallas_call | solution.py:224
  53.2 1.6 %collective-permute-start.18 = (f32[2,8,128]{2,1,0:T(8,128)S(1)}, f32[2,8,128]{2,1,0:T(8,128)S(1)}, u32[]{:S(2)}, u32[]{:S(2)}) collective-permute-start(f32[2,8,128]{2,1,0:T(8,128)S(1)} %get-tuple-element.29), channel_id=1, source_target_pairs={{0,28},{4,8},{8,4},{12,16},{16,12},{20,24},{24,20},{28,0},{1,29},{... | collective-permute-start | bytes 24584 | tf_op jit(solution)/shard_map/ppermute | solution.py:364
  54.8 0.2 collective-permute-start.17
  55.0 1.0 %collective-permute-done.17 = f32[2,8,128]{2,1,0:T(8,128)S(1)} collective-permute-done((f32[2,8,128]{2,1,0:T(8,128)S(1)}, f32[2,8,128]{2,1,0:T(8,128)S(1)}, u32[]{:S(2)}, u32[]{:S(2)}) %collective-permute-start.17) | collective-permute-done | bytes 8224 | tf_op jit(solution)/shard_map/ppermute | solution.py:33
  56.0 1.2 %collective-permute-done.18 = f32[2,8,128]{2,1,0:T(8,128)S(1)} collective-permute-done((f32[2,8,128]{2,1,0:T(8,128)S(1)}, f32[2,8,128]{2,1,0:T(8,128)S(1)}, u32[]{:S(2)}, u32[]{:S(2)}) %collective-permute-start.18) | collective-permute-done | bytes 8224 | tf_op jit(solution)/shard_map/ppermute | solution.py:364
  57.3 1.4 %stretch.1 = f32[512,128]{1,0:T(8,128)} custom-call(f32[2,512,128]{2,1,0:T(8,128)S(1)} %get-tuple-element.26.flow_ref, f32[2,8,128]{2,1,0:T(8,128)S(1)} %bitcast.30, f32[2,8,128]{2,1,0:T(8,128)S(1)} %broadcast_select_fusion.sides_ref), custom_call_target="tpu_custom_call" | custom-call | tf_op jit(solution)/shard_map/stretch/pallas_call | solution.py:375
  (37 shorter events, 0.7 us)
Async XLA Ops:
  1.6 12.1 %collective-permute-start = (bf16[768,128]{1,0:T(8,128)(2,1)S(1)}, bf16[768,128]{1,0:T(8,128)(2,1)S(1)}, u32[]{:S(2)}, u32[]{:S(2)}) collective-permute-start(bf16[768,128]{1,0:T(8,128)(2,1)S(1)} %bitcast.31), channel_id=1, source_target_pairs={{0,1},{1,0},{2,3},{3,2},{4,5},{5,4},{6,7},{7,6},{8,9},{9,8},{10,11... | collective-permute-start | bytes 589832 | tf_op jit(solution)/shard_map/ppermute | solution.py:33
  4.6 13.6 %collective-permute-start.8 = (bf16[768,128]{1,0:T(8,128)(2,1)S(1)}, bf16[768,128]{1,0:T(8,128)(2,1)S(1)}, u32[]{:S(2)}, u32[]{:S(2)}) collective-permute-start(bf16[768,128]{1,0:T(8,128)(2,1)S(1)} %bitcast.32), channel_id=1, source_target_pairs={{0,2},{1,3},{2,0},{3,1},{4,6},{5,7},{6,4},{7,5},{8,10},{9,11},{10,... | collective-permute-start | bytes 589832 | tf_op jit(solution)/shard_map/ppermute | solution.py:33
  7.2 9.4 %collective-permute-start.3 = (bf16[1,768,128]{2,1,0:T(8,128)(2,1)S(1)}, bf16[1,768,128]{2,1,0:T(8,128)(2,1)S(1)}, u32[]{:S(2)}, u32[]{:S(2)}) collective-permute-start(bf16[1,768,128]{2,1,0:T(8,128)(2,1)S(1)} %bitcast.33), channel_id=1, source_target_pairs={{0,8},{4,20},{8,0},{12,28},{16,24},{20,4},{24,16},{28,12},{1,9},{5... | collective-permute-start | bytes 589832 | tf_op jit(solution)/shard_map/ppermute | solution.py:33
  13.6 15.3 %collective-permute-start.6 = (bf16[1,768,128]{2,1,0:T(8,128)(2,1)S(1)}, bf16[1,768,128]{2,1,0:T(8,128)(2,1)S(1)}, u32[]{:S(2)}, u32[]{:S(2)}) collective-permute-start(bf16[1,768,128]{2,1,0:T(8,128)(2,1)S(1)} %bitcast.40), channel_id=1, source_target_pairs={{0,8},{4,20},{8,0},{12,28},{16,24},{20,4},{24,16},{28,12},{1,9},{5... | collective-permute-start | bytes 589832 | tf_op jit(solution)/shard_map/ppermute | solution.py:33
  15.3 6.1 %collective-permute-start.2 = (s32[3,8,128]{2,1,0:T(8,128)S(1)}, s32[3,8,128]{2,1,0:T(8,128)S(1)}, u32[]{:S(2)}, u32[]{:S(2)}) collective-permute-start(s32[3,8,128]{2,1,0:T(8,128)S(1)} %get-tuple-element.17), channel_id=1, source_target_pairs={{1,0},{2,1},{3,2},{5,4},{6,5},{7,6},{9,8},{10,9},{11,10},{13,12},{... | collective-permute-start | bytes 36872 | tf_op jit(solution)/shard_map/ppermute | solution.py:324
  16.6 12.3 %collective-permute-start.4 = (bf16[2,768,128]{2,1,0:T(8,128)(2,1)S(1)}, bf16[2,768,128]{2,1,0:T(8,128)(2,1)S(1)}, u32[]{:S(2)}, u32[]{:S(2)}) collective-permute-start(bf16[2,768,128]{2,1,0:T(8,128)(2,1)S(1)} %pad_maximum_fusion.2), channel_id=1, source_target_pairs={{0,16},{4,12},{8,24},{12,4},{16,0},{20,28},{24,8},{28,20},{1,17},{... | collective-permute-start | bytes 1179656 | tf_op jit(solution)/shard_map/ppermute | solution.py:33
  18.2 7.8 %collective-permute-start.9 = (bf16[1,768,128]{2,1,0:T(8,128)(2,1)S(1)}, bf16[1,768,128]{2,1,0:T(8,128)(2,1)S(1)}, u32[]{:S(2)}, u32[]{:S(2)}) collective-permute-start(bf16[1,768,128]{2,1,0:T(8,128)(2,1)S(1)} %bitcast.42), channel_id=1, source_target_pairs={{0,8},{4,20},{8,0},{12,28},{16,24},{20,4},{24,16},{28,12},{1,9},{5... | collective-permute-start | bytes 589832 | tf_op jit(solution)/shard_map/ppermute | solution.py:33
  18.8 8.6 %collective-permute-start.12 = (bf16[768,128]{1,0:T(8,128)(2,1)S(1)}, bf16[768,128]{1,0:T(8,128)(2,1)S(1)}, u32[]{:S(2)}, u32[]{:S(2)}) collective-permute-start(bf16[768,128]{1,0:T(8,128)(2,1)S(1)} %bitcast.35), channel_id=1, source_target_pairs={{0,3},{1,2},{2,1},{3,0},{4,7},{5,6},{6,5},{7,4},{8,11},{9,10},{10,... | collective-permute-start | bytes 589832 | tf_op jit(solution)/shard_map/ppermute | solution.py:33
  21.4 21.8 %collective-permute-start.1 = (s32[3,8,128]{2,1,0:T(8,128)S(1)}, s32[3,8,128]{2,1,0:T(8,128)S(1)}, u32[]{:S(2)}, u32[]{:S(2)}) collective-permute-start(s32[3,8,128]{2,1,0:T(8,128)S(1)} %get-tuple-element.16), channel_id=1, source_target_pairs={{0,1},{1,2},{2,3},{4,5},{5,6},{6,7},{8,9},{9,10},{10,11},{12,13},{... | collective-permute-start | bytes 36872 | tf_op jit(solution)/shard_map/ppermute | solution.py:323
  26.1 10.2 %collective-permute-start.11 = (bf16[2,768,128]{2,1,0:T(8,128)(2,1)S(1)}, bf16[2,768,128]{2,1,0:T(8,128)(2,1)S(1)}, u32[]{:S(2)}, u32[]{:S(2)}) collective-permute-start(bf16[2,768,128]{2,1,0:T(8,128)(2,1)S(1)} %pad_maximum_fusion.4), channel_id=1, source_target_pairs={{0,16},{4,12},{8,24},{12,4},{16,0},{20,28},{24,8},{28,20},{1,17},{... | collective-permute-start | bytes 1179656 | tf_op jit(solution)/shard_map/ppermute | solution.py:33
  27.4 18.4 %copy-start = (s32[8,512,128]{2,1,0:T(8,128)S(1)}, s32[8,512,128]{2,1,0:T(8,128)}, u32[]{:S(2)}) copy-start(s32[8,512,128]{2,1,0:T(8,128)} %refs_2_.1) | copy-start | bytes 6291460
  27.4 7.8 %collective-permute-start.13 = (bf16[1,768,128]{2,1,0:T(8,128)(2,1)S(1)}, bf16[1,768,128]{2,1,0:T(8,128)(2,1)S(1)}, u32[]{:S(2)}, u32[]{:S(2)}) collective-permute-start(bf16[1,768,128]{2,1,0:T(8,128)(2,1)S(1)} %bitcast.37), channel_id=1, source_target_pairs={{0,8},{4,20},{8,0},{12,28},{16,24},{20,4},{24,16},{28,12},{1,9},{5... | collective-permute-start | bytes 589832 | tf_op jit(solution)/shard_map/ppermute | solution.py:33
  29.0 9.2 %collective-permute-start.7 = (bf16[2,768,128]{2,1,0:T(8,128)(2,1)S(1)}, bf16[2,768,128]{2,1,0:T(8,128)(2,1)S(1)}, u32[]{:S(2)}, u32[]{:S(2)}) collective-permute-start(bf16[2,768,128]{2,1,0:T(8,128)(2,1)S(1)} %pad_maximum_fusion.3), channel_id=1, source_target_pairs={{0,16},{4,12},{8,24},{12,4},{16,0},{20,28},{24,8},{28,20},{1,17},{... | collective-permute-start | bytes 1179656 | tf_op jit(solution)/shard_map/ppermute | solution.py:33
  35.2 7.8 %collective-permute-start.15 = (bf16[2,768,128]{2,1,0:T(8,128)(2,1)S(1)}, bf16[2,768,128]{2,1,0:T(8,128)(2,1)S(1)}, u32[]{:S(2)}, u32[]{:S(2)}) collective-permute-start(bf16[2,768,128]{2,1,0:T(8,128)(2,1)S(1)} %pad_maximum_fusion.5), channel_id=1, source_target_pairs={{0,16},{4,12},{8,24},{12,4},{16,0},{20,28},{24,8},{28,20},{1,17},{... | collective-permute-start | bytes 1179656 | tf_op jit(solution)/shard_map/ppermute | solution.py:33
  36.2 7.9 %collective-permute-start.5 = (bf16[4,768,128]{2,1,0:T(8,128)(2,1)S(1)}, bf16[4,768,128]{2,1,0:T(8,128)(2,1)S(1)}, u32[]{:S(2)}, u32[]{:S(2)}) collective-permute-start(bf16[4,768,128]{2,1,0:T(8,128)(2,1)S(1)} %pad_maximum_fusion.refs_0_), channel_id=1, source_target_pairs={{0,4},{4,0},{8,12},{12,8},{16,20},{20,16},{24,28},{28,24},{1,5},{5... | collective-permute-start | bytes 2359304 | tf_op jit(solution)/shard_map/ppermute | solution.py:33
  36.4 7.8 %collective-permute-start.14 = (bf16[4,768,128]{2,1,0:T(8,128)(2,1)S(1)}, bf16[4,768,128]{2,1,0:T(8,128)(2,1)S(1)}, u32[]{:S(2)}, u32[]{:S(2)}) collective-permute-start(bf16[4,768,128]{2,1,0:T(8,128)(2,1)S(1)} %constant_dynamic-update-slice_fusion.2.refs_4_), channel_id=1, source_target_pairs={{0,4},{4,0},{8,12},{12,8},{16,20},{20,16},{24,28},{28,24},{1,5},{5... | collective-permute-start | bytes 2359304 | tf_op jit(solution)/shard_map/ppermute | solution.py:33
  38.2 6.0 %collective-permute-start.10 = (bf16[4,768,128]{2,1,0:T(8,128)(2,1)S(1)}, bf16[4,768,128]{2,1,0:T(8,128)(2,1)S(1)}, u32[]{:S(2)}, u32[]{:S(2)}) collective-permute-start(bf16[4,768,128]{2,1,0:T(8,128)(2,1)S(1)} %constant_dynamic-update-slice_fusion.refs_2_), channel_id=1, source_target_pairs={{0,4},{4,0},{8,12},{12,8},{16,20},{20,16},{24,28},{28,24},{1,5},{5... | collective-permute-start | bytes 2359304 | tf_op jit(solution)/shard_map/ppermute | solution.py:33
  43.2 2.6 %collective-permute-start.16 = (bf16[4,768,128]{2,1,0:T(8,128)(2,1)S(1)}, bf16[4,768,128]{2,1,0:T(8,128)(2,1)S(1)}, u32[]{:S(2)}, u32[]{:S(2)}) collective-permute-start(bf16[4,768,128]{2,1,0:T(8,128)(2,1)S(1)} %pad_maximum_fusion.1.refs_4_), channel_id=1, source_target_pairs={{0,4},{4,0},{8,12},{12,8},{16,20},{20,16},{24,28},{28,24},{1,5},{5... | collective-permute-start | bytes 2359304 | tf_op jit(solution)/shard_map/ppermute | solution.py:33
  53.2 4.1 %collective-permute-start.18 = (f32[2,8,128]{2,1,0:T(8,128)S(1)}, f32[2,8,128]{2,1,0:T(8,128)S(1)}, u32[]{:S(2)}, u32[]{:S(2)}) collective-permute-start(f32[2,8,128]{2,1,0:T(8,128)S(1)} %get-tuple-element.29), channel_id=1, source_target_pairs={{0,28},{4,8},{8,4},{12,16},{16,12},{20,24},{24,20},{28,0},{1,29},{... | collective-permute-start | bytes 24584 | tf_op jit(solution)/shard_map/ppermute | solution.py:364
  54.8 1.2 %collective-permute-start.17 = (f32[2,8,128]{2,1,0:T(8,128)S(1)}, f32[2,8,128]{2,1,0:T(8,128)S(1)}, u32[]{:S(2)}, u32[]{:S(2)}) collective-permute-start(f32[2,8,128]{2,1,0:T(8,128)S(1)} %get-tuple-element.29), channel_id=1, source_target_pairs={{0,4},{4,0},{8,12},{12,8},{16,20},{20,16},{24,28},{28,24},{1,5},{5... | collective-permute-start | bytes 24584 | tf_op jit(solution)/shard_map/ppermute | solution.py:33
